TPU v7x, 128 devices: a whole 4x4x4 slice. The times are simulated.
128 devices in a mesh: gx: 16 (over x, y), gy: 8 (over z, core).
Axes of the slice: x: 4, y: 4, z: 4, core: 2. Of those that a mesh axis runs over, the one named last changes fastest.
Arguments:
- features: bfloat16 [32, 4194304], P(None, ('gx', 'gy')), may hold values from -6 to 6
- weights: bfloat16 [4194304, 128], P(('gx', 'gy')), as said below
- owners: int32 [32768], P(('gx', 'gy')), may hold values from 0 to 127, as said below
- tile_ids: int32 [32768], P(('gx', 'gy')), may hold values from 0 to 127, as said below
- counts: int32 [128], P(('gx', 'gy')), may hold values from 128 to 256, as said below
- conv_first: bfloat16 [27, 32, 32], replicated, may hold values from -0.21875 to 0.21875
- bias_first: float32 [32], replicated, may hold values from -3 to 3
- conv_second: bfloat16 [27, 32, 32], replicated, may hold values from -0.21875 to 0.21875
- bias_second: float32 [32], replicated, may hold values from -3 to 3
- head: bfloat16 [3, 32], replicated, may hold values from -1 to 1
Outputs:
- grid_out: bfloat16 [32, 16, 128, 1024], P(None, None, 'gx', 'gy')
- velocity: float32 [3, 4194304], P(None, ('gx', 'gy'))
Inputs may be any that keep to these rules, and one draw needn't show every extreme that they name: `owners`: the first 128 slots of each device name the device itself. Later slots that are live name a device whose brick is one step away along gx, along gy or both (no wrap, never the device itself); later slots that are not live name the device itself. Among its later live slots one device names any one owner at most 16 times; some device names every one of its neighbours exactly 16 times, and some device is named exactly 16 times by each of its neighbours other than device 0. `tile_ids`: on each device the first 128 slots name every tile of its brick once; later slots name any tile. `counts`: number of live blocks of each device, which stand first among its slots. Each row holds a particle's quadratic B-spline weights on its block's tile, cell index (z 4 + x) 8 + y; its 27 nonzero weights lie inside the tile and sum to one.
All inputs are finite; a program needn't handle non-finite values.
Results may differ from a plain program's by a relative error of at most 0.0051.
Values may be sent and summed in bfloat16 or wider, within the bound.
No kernel may reach another device: no remote copies, remote signals or barrier semaphores. Data moves between devices by JAX's collectives and lax.ppermute only.
A program may use at most 384 MiB of HBM per device.

v0:
```python
import jax
import jax.numpy as jnp
import numpy as np
from jax import lax
from jax.experimental import pallas as pl
from jax.experimental.pallas import tpu as pltpu
from jax.sharding import PartitionSpec as P

C = 32
SLAB = 16
BY = 128
SLOTS = 16
PAY = SLOTS * 32 + 16
ROWS = 144
STEP = 16
STEPS = 8
MIB = 1 << 20
F32 = jnp.float32
BF16 = jnp.bfloat16
VMEM = pltpu.VMEM
SMEM = pltpu.SMEM


def lanes_of(shape):
    return lax.broadcasted_iota(jnp.int32, shape, len(shape) - 1)


def params(limit, grid=False):
    if grid:
        return pltpu.CompilerParams(
            dimension_semantics=("arbitrary",), vmem_limit_bytes=limit * MIB
        )
    return pltpu.CompilerParams(vmem_limit_bytes=limit * MIB)


def cost(flops, nbytes):
    return pl.CostEstimate(flops=flops, bytes_accessed=nbytes, transcendentals=0)


def splat_four(f_ref, w_ref, first):
    parts = []
    for j in range(4):
        at = (first + j) * 128
        parts.append(
            jnp.dot(f_ref[:, at : at + 128], w_ref[at : at + 128, :], preferred_element_type=F32)
        )
    a = jnp.concatenate(parts, 0).astype(BF16).astype(F32)
    a = a.T.reshape(4, 2, 2, 8, 128)
    lane = lanes_of((4, 2, 8, 128))
    v0, v1 = a[:, 0], a[:, 1]
    n0 = jnp.where(lane < 64, v0, pltpu.roll(v1, 64, 3))
    n1 = jnp.where(lane < 64, pltpu.roll(v0, 64, 3), v1)
    lane = lanes_of((4, 8, 128))
    tiles = []
    for n in (n0, n1):
        v0, v1 = n[:, 0], n[:, 1]
        tiles.append(jnp.where(lane % 64 < 32, v0, pltpu.roll(v1, 32, 2)))
        tiles.append(jnp.where(lane % 64 < 32, pltpu.roll(v0, 96, 2), v1))
    return tiles


def far_splat_kernel(owners, ids, counts, f_ref, w_ref, lo, mid, hi, slots, tiles, idrows, filled):
    step = pl.program_id(0)
    ix = lax.axis_index("gx")
    iy = lax.axis_index("gy")

    @pl.when(step == 0)
    def _():
        tiles[...] = jnp.zeros_like(tiles)
        idrows[...] = jnp.zeros_like(idrows)
        for k in range(9):
            filled[k] = 0

    lane = lanes_of((1, 128))
    count = counts[0]
    for group in range(STEP // 4):
        got = splat_four(f_ref, w_ref, group * 4)
        for j in range(4):
            block = step * STEP + group * 4 + j
            owner = owners[128 + block]
            live = 128 + block < count
            target = ((owner >> 3) - ix + 1) * 3 + (owner & 7) - iy + 1
            target = jnp.where(live, target, 4)
            rank = filled[target]
            filled[target] = jnp.where(live, rank + 1, 0)
            slot = target * SLOTS + rank
            slots[block] = slot
            tiles[slot] = got[j].reshape(32, 128).astype(BF16)
            row = idrows[pl.ds(target, 1), :]
            idrows[pl.ds(target, 1), :] = jnp.where(
                lane == rank, ids[128 + block].astype(F32), row
            )

    @pl.when(step == STEPS - 1)
    def _():
        for dx, out in enumerate((lo, mid, hi)):
            for dy in range(3):
                k = dx * 3 + dy
                out[dy, 0 : SLOTS * 32, :] = tiles[k * SLOTS : (k + 1) * SLOTS].reshape(
                    SLOTS * 32, 128
                )
                out[dy, SLOTS * 32 : PAY, :] = jnp.broadcast_to(
                    idrows[k : k + 1, :], (16, 128)
                ).astype(BF16)


def far_splat(features, weights, owners, ids, counts):
    pay = jax.ShapeDtypeStruct((3, PAY, 128), BF16)
    whole = pl.BlockSpec((3, PAY, 128), lambda i: (0, 0, 0))
    smem = pl.BlockSpec(memory_space=SMEM)
    return pl.pallas_call(
        far_splat_kernel,
        grid=(STEPS,),
        in_specs=[
            smem,
            smem,
            smem,
            pl.BlockSpec((C, STEP * 128), lambda i: (0, STEPS + i)),
            pl.BlockSpec((STEP * 128, 128), lambda i: (STEPS + i, 0)),
        ],
        out_specs=[whole, whole, whole, smem],
        out_shape=[pay, pay, pay, jax.ShapeDtypeStruct((128,), jnp.int32)],
        scratch_shapes=[
            VMEM((9 * SLOTS, 32, 128), BF16),
            VMEM((16, 128), F32),
            SMEM((9,), jnp.int32),
        ],
        compiler_params=params(16, True),
        cost_estimate=cost(2 * 128 * 32 * 128 * 128, 6 * MIB),
        name="far_splat",
    )(owners, ids, counts, features, weights)


def tile_place(tile):
    return (tile >> 5) * 4, (tile >> 4) & 1, pl.multiple_of((tile & 15) * 8, 8)


def own_splat_kernel(ids, f_ref, w_ref, out, grid):
    step = pl.program_id(0)
    for group in range(STEP // 4):
        got = splat_four(f_ref, w_ref, group * 4)
        for j in range(4):
            z, tx, y = tile_place(ids[step * STEP + group * 4 + j])
            grid[tx, pl.ds(z, 4), pl.ds(y, 8), :] = got[j]

    @pl.when(step == STEPS - 1)
    def _():
        out[...] = grid[...].astype(BF16)


def own_splat(features, weights, ids):
    return pl.pallas_call(
        own_splat_kernel,
        grid=(STEPS,),
        in_specs=[
            pl.BlockSpec(memory_space=SMEM),
            pl.BlockSpec((C, STEP * 128), lambda i: (0, i)),
            pl.BlockSpec((STEP * 128, 128), lambda i: (i, 0)),
        ],
        out_specs=pl.BlockSpec((2, SLAB, BY, 128), lambda i: (0, 0, 0, 0)),
        out_shape=jax.ShapeDtypeStruct((2, SLAB, BY, 128), BF16),
        scratch_shapes=[VMEM((2, SLAB, BY, 128), F32)],
        compiler_params=params(16, True),
        cost_estimate=cost(2 * 128 * 32 * 128 * 128, 6 * MIB),
        name="own_splat",
    )(ids, features, weights)


def sum_kernel(own, from_ylo, from_yhi, from_xlo, from_xhi, g, ylo, yhi, ids, grid, idv, sem):
    groups = [(from_ylo, 0), (from_ylo, 1), (from_ylo, 2)]
    groups += [(from_yhi, 0), (from_yhi, 1), (from_yhi, 2)]
    groups += [(from_xlo, 1), (from_xhi, 1)]
    rows = [ref[k, SLOTS * 32 : PAY, :].astype(F32)[0:1] for ref, k in groups]
    idv[...] = jnp.concatenate(rows, 0).astype(jnp.int32)
    copy = pltpu.make_async_copy(idv, ids, sem)
    copy.start()
    grid[...] = own[...].astype(F32)
    copy.wait()
    for n, (ref, k) in enumerate(groups):

        def add(j, carry, n=n, ref=ref, k=k):
            z, tx, y = tile_place(ids[n, j])
            tile = ref[k, pl.ds(pl.multiple_of(j * 32, 32), 32), :].astype(F32).reshape(4, 8, 128)
            grid[tx, pl.ds(z, 4), pl.ds(y, 8), :] += tile
            return carry

        lax.fori_loop(0, SLOTS, add, 0, unroll=4)
    g[...] = grid[...].astype(BF16)
    for tx in range(2):
        for r in range(2):
            ylo[tx * 2 + r] = grid[tx, :, r, :].astype(BF16)
            yhi[tx * 2 + r] = grid[tx, :, BY - 2 + r, :].astype(BF16)


def sum_tiles(own, from_ylo, from_yhi, from_xlo, from_xhi):
    vm = pl.BlockSpec(memory_space=VMEM)
    edge = jax.ShapeDtypeStruct((4, SLAB, 128), BF16)
    return pl.pallas_call(
        sum_kernel,
        in_specs=[vm] * 5,
        out_specs=[vm, vm, vm, pl.BlockSpec(memory_space=SMEM)],
        out_shape=[
            jax.ShapeDtypeStruct((2, SLAB, BY, 128), BF16),
            edge,
            edge,
            jax.ShapeDtypeStruct((8, 128), jnp.int32),
        ],
        scratch_shapes=[
            VMEM((2, SLAB, BY, 128), F32),
            VMEM((8, 128), jnp.int32),
            pltpu.SemaphoreType.DMA,
        ],
        compiler_params=params(16),
        cost_estimate=cost(1000, 4 * MIB),
        name="sum_tiles",
    )(own, from_ylo, from_yhi, from_xlo, from_xhi)


def widen_kernel(g, rlo, rhi, x, slo, shi, edge):
    edge[...] = jnp.zeros_like(edge)
    for tx in range(2):
        for r in range(2):
            edge[tx, 0, :, 6 + r, :] = rlo[tx * 2 + r].astype(F32)
            edge[tx, 1, :, r, :] = rhi[tx * 2 + r].astype(F32)
    lane = lanes_of((ROWS, 128))

    def plane(tx, z):
        return jnp.concatenate([edge[tx, 0, z], g[tx, z].astype(F32), edge[tx, 1, z]], 0)

    def pair(z, carry):
        a, b = plane(0, z), plane(0, z + 8)
        x[0, z] = a.astype(BF16)
        x[0, z + 8] = b.astype(BF16)
        slo[z] = jnp.where(lane < 64, a, pltpu.roll(b, 64, 1)).astype(BF16)
        a, b = plane(1, z), plane(1, z + 8)
        x[1, z] = a.astype(BF16)
        x[1, z + 8] = b.astype(BF16)
        shi[z] = jnp.where(lane < 64, pltpu.roll(a, 64, 1), b).astype(BF16)
        return carry

    lax.fori_loop(0, 8, pair, 0)


def widen_y(g, rlo, rhi):
    vm = pl.BlockSpec(memory_space=VMEM)
    side = jax.ShapeDtypeStruct((SLAB // 2, ROWS, 128), BF16)
    return pl.pallas_call(
        widen_kernel,
        in_specs=[vm] * 3,
        out_specs=[vm] * 3,
        out_shape=[jax.ShapeDtypeStruct((2, SLAB, ROWS, 128), BF16), side, side],
        scratch_shapes=[VMEM((2, 2, SLAB, 8, 128), F32)],
        compiler_params=params(8),
        cost_estimate=cost(1000, 3 * MIB),
        name="widen_y",
    )(g, rlo, rhi)


def rows_inside(shape, iy):
    row = lax.broadcasted_iota(jnp.int32, shape, 1)
    return ((row != 7) | (iy > 0)) & ((row != 136) | (iy < 7))


def shifted(v):
    return (pltpu.roll(v, 1, 1), v, pltpu.roll(v, ROWS - 1, 1))


def inner_kernel(x, g, t1, b1, t2, b2, part, xs, hs):
    iy = lax.axis_index("gy")
    for dy in range(3):
        xs[dy, 0] = jnp.zeros((ROWS, 256), BF16)
        xs[dy, SLAB + 1] = jnp.zeros((ROWS, 256), BF16)
        hs[dy, 0] = jnp.zeros((BY, 256), BF16)
        hs[dy, SLAB + 1] = jnp.zeros((BY, 256), BF16)

    def shift(z, carry):
        for tx in range(2):
            v = x[tx, pl.ds(z, 1)].astype(F32)
            for dy, s in enumerate(shifted(v)):
                xs[dy, pl.ds(z + 1, 1), :, tx * 128 : tx * 128 + 128] = s.astype(BF16)
        return carry

    lax.fori_loop(0, SLAB, shift, 0)

    def first(n, carry):
        taps = [
            xs[dy, pl.ds(n * 4 + dz, 4)].reshape(4 * ROWS, 256)
            for dz in range(3)
            for dy in range(3)
        ]
        acc = jnp.dot(jnp.concatenate(taps, 1), t1[...], preferred_element_type=F32) + b1[...]
        h = jax.nn.gelu(acc).reshape(4, ROWS, 256)
        h = jnp.where(rows_inside(h.shape, iy), h, 0.0)
        for dy, s in enumerate(shifted(h)):
            hs[dy, pl.ds(n * 4 + 1, 4)] = s[:, 8 : 8 + BY].astype(BF16)
        return carry

    lax.fori_loop(0, 4, first, 0)

    def second(n, carry):
        taps = [
            hs[dy, pl.ds(n * 4 + dz, 4)].reshape(4 * BY, 256) for dz in range(3) for dy in range(3)
        ]
        taps += [g[tx, pl.ds(n * 4, 4)].reshape(4 * BY, 128) for tx in range(2)]
        acc = jnp.dot(jnp.concatenate(taps, 1), t2[...], preferred_element_type=F32) + b2[...]
        part[pl.ds(n * 4, 4)] = acc.reshape(4, BY, 256)
        return carry

    lax.fori_loop(0, 4, second, 0)


def inner_convs(x, g, t1, b1, t2, b2):
    vm = pl.BlockSpec(memory_space=VMEM)
    return pl.pallas_call(
        inner_kernel,
        in_specs=[vm] * 6,
        out_specs=vm,
        out_shape=jax.ShapeDtypeStruct((SLAB, BY, 256), F32),
        scratch_shapes=[
            VMEM((3, SLAB + 2, ROWS, 256), BF16),
            VMEM((3, SLAB + 2, BY, 256), BF16),
        ],
        compiler_params=params(32),
        cost_estimate=cost(2 * 20 * 256 * 256 * 2304, 6 * MIB),
        name="inner_convs",
    )(x, g, t1, b1, t2, b2)


def tile_row(tile):
    return ((tile >> 5) * 4 + ((tile >> 2) & 3)) * 8 + ((tile >> 4) & 1) * 4 + (tile & 3)


def edge_kernel(
    x, rlo, rhi, part, t1, b1, t2, headx, ids, out, table, ans_ylo, ans_yhi, ans_x, es, hs, vel
):
    ix = lax.axis_index("gx")
    iy = lax.axis_index("gy")
    for dy in range(3):
        es[dy, 0] = jnp.zeros((ROWS, 256), BF16)
        es[dy, SLAB + 1] = jnp.zeros((ROWS, 256), BF16)
        hs[dy, 0] = jnp.zeros((BY, 128), BF16)
        hs[dy, SLAB + 1] = jnp.zeros((BY, 128), BF16)
    lane = lanes_of((1, ROWS, 128))

    def put(z, low, high):
        for k, v in enumerate((low, high)):
            for dy, s in enumerate(shifted(v)):
                es[dy, pl.ds(z + 1, 1), :, k * 128 : k * 128 + 128] = s.astype(BF16)

    def shift(z, carry):
        a = rlo[pl.ds(z, 1)].astype(F32)
        b = rhi[pl.ds(z, 1)].astype(F32)
        for half in range(2):
            zz = z + 8 * half
            own0 = x[0, pl.ds(zz, 1)].astype(F32)
            own1 = x[1, pl.ds(zz, 1)].astype(F32)
            left = pltpu.roll(a, 64, 2) if half == 0 else a
            right = b if half == 0 else pltpu.roll(b, 64, 2)
            put(zz, jnp.where(lane < 64, own0, left), jnp.where(lane < 64, right, own1))
        return carry

    lax.fori_loop(0, 8, shift, 0)

    def first(n, carry):
        taps = [
            es[dy, pl.ds(n * 4 + dz, 4)].reshape(4 * ROWS, 256)
            for dz in range(3)
            for dy in range(3)
        ]
        acc = jnp.dot(jnp.concatenate(taps, 1), t1[...], preferred_element_type=F32) + b1[...]
        h = jax.nn.gelu(acc).reshape(4, ROWS, 128)
        ln = lanes_of(h.shape)
        keep = ((ln >= 32) | (ix > 0)) & ((ln < 96) | (ix < 15))
        h = jnp.where(rows_inside(h.shape, iy) & keep, h, 0.0)
        for dy, s in enumerate(shifted(h)):
            hs[dy, pl.ds(n * 4 + 1, 4)] = s[:, 8 : 8 + BY].astype(BF16)
        return carry

    lax.fori_loop(0, 4, first, 0)

    def second(n, carry):
        taps = [
            hs[dy, pl.ds(n * 4 + dz, 4)].reshape(4 * BY, 128) for dz in range(3) for dy in range(3)
        ]
        acc = jnp.dot(jnp.concatenate(taps, 1), t2[...], preferred_element_type=F32)
        for k in range(4):
            z = n * 4 + k
            total = (acc[k * BY : (k + 1) * BY] + part[z]).T.astype(BF16)
            out[:, pl.ds(z, 1)] = total.reshape(32, 1, 8, 128)
            v = jnp.dot(headx[...], total, preferred_element_type=F32)
            for a in range(3):
                vel[a, pl.ds(z, 1)] = v[8 * a : 8 * a + 8].reshape(1, 8, 128)
        return carry

    lax.fori_loop(0, 4, second, 0)

    table[...] = jnp.zeros_like(table)
    sub = lax.broadcasted_iota(jnp.int32, (4, 8, 128), 1)
    ln = lanes_of((4, 8, 128))
    for a in range(3):
        v = vel[a].reshape(4, 2, 2, 8, 128)
        v0, v1 = v[:, 0], v[:, 1]
        l2 = lanes_of(v0.shape)
        m0 = jnp.where(l2 < 64, v0, pltpu.roll(v1, 64, 3))
        m1 = jnp.where(l2 < 64, pltpu.roll(v0, 64, 3), v1)
        for k, m in enumerate((m0, m1)):
            v0, v1 = m[:, 0], m[:, 1]
            n0 = jnp.where(ln % 64 < 32, v0, pltpu.roll(v1, 32, 2))
            n1 = jnp.where(ln % 64 < 32, pltpu.roll(v0, 96, 2), v1)
            for kk, w in enumerate((n0, n1)):
                for bit, step in ((2, 16), (1, 8)):
                    up = pltpu.roll(pltpu.roll(w, 8 - bit, 1), step, 2)
                    down = pltpu.roll(pltpu.roll(w, bit, 1), 128 - step, 2)
                    s1 = (sub & bit) != 0
                    l1 = (ln & step) != 0
                    w = jnp.where(s1 == l1, w, jnp.where(l1, up, down))
                for tz in range(4):
                    row = (tz * 4 + k * 2 + kk) * 8
                    table[row : row + 8, a, :] = w[tz]

    srow = lax.broadcasted_iota(jnp.int32, (8, 128), 0)
    places = [(ans_ylo, 0), (ans_ylo, 1), (ans_ylo, 2), (ans_yhi, 0), (ans_yhi, 1), (ans_yhi, 2)]
    places += [(ans_x, 0), (ans_x, 1)]
    for n, (ref, k) in enumerate(places):

        def answer(j, carry, n=n, ref=ref, k=k):
            halves = []
            for h in range(2):
                r0 = table[tile_row(ids[n, j * 4 + 2 * h])]
                r1 = table[tile_row(ids[n, j * 4 + 2 * h + 1])]
                halves.append(jnp.where(srow < 4, r0, pltpu.roll(r1, 4, 0)))
            ref[k, pl.ds(pl.multiple_of(j * 16, 16), 16), :] = jnp.concatenate(halves, 0).astype(
                BF16
            )
            return carry

        lax.fori_loop(0, SLOTS // 4, answer, 0, unroll=2)


def edge_convs(x, rlo, rhi, part, t1, b1, t2, headx, ids):
    vm = pl.BlockSpec(memory_space=VMEM)
    ans = jax.ShapeDtypeStruct((3, 64, 128), BF16)
    return pl.pallas_call(
        edge_kernel,
        in_specs=[vm] * 8 + [pl.BlockSpec(memory_space=SMEM)],
        out_specs=[vm] * 5,
        out_shape=[
            jax.ShapeDtypeStruct((C, SLAB, 8, BY), BF16),
            jax.ShapeDtypeStruct((128, 8, 128), F32),
            ans,
            ans,
            jax.ShapeDtypeStruct((2, 64, 128), BF16),
        ],
        scratch_shapes=[
            VMEM((3, SLAB + 2, ROWS, 256), BF16),
            VMEM((3, SLAB + 2, BY, 128), BF16),
            VMEM((3, SLAB, 8, 128), F32),
        ],
        compiler_params=params(32),
        cost_estimate=cost(2 * 9 * 256 * 256 * 2304, 6 * MIB),
        name="edge_convs",
    )(x, rlo, rhi, part, t1, b1, t2, headx, ids)


def read_four(rows, w_ref, first):
    lhs = jnp.concatenate(rows, 0).astype(BF16)
    w = w_ref[first * 128 : (first + 4) * 128, :]
    r = lax.dot_general(lhs, w, (((1,), (1,)), ((), ())), preferred_element_type=F32)
    return [r[8 * j : 8 * j + 3, 128 * j : 128 * j + 128] for j in range(4)]


def own_read_kernel(ids, table, w_ref, out):
    step = pl.program_id(0)
    for group in range(STEP // 4):
        rows = [table[tile_row(ids[step * STEP + group * 4 + j])] for j in range(4)]
        for j, v in enumerate(read_four(rows, w_ref, group * 4)):
            at = (group * 4 + j) * 128
            out[:, at : at + 128] = v


def own_read(ids, table, weights, particles):
    return pl.pallas_call(
        own_read_kernel,
        grid=(STEPS,),
        in_specs=[
            pl.BlockSpec(memory_space=SMEM),
            pl.BlockSpec((128, 8, 128), lambda i: (0, 0, 0)),
            pl.BlockSpec((STEP * 128, 128), lambda i: (i, 0)),
        ],
        out_specs=pl.BlockSpec((3, STEP * 128), lambda i: (0, i)),
        out_shape=jax.ShapeDtypeStruct((3, particles), F32),
        compiler_params=params(16, True),
        cost_estimate=cost(2 * 128 * 32 * 128 * 128, 5 * MIB),
        name="own_read",
    )(ids, table, weights)


def far_read_kernel(slots, counts, blo, bhi, ylo, yhi, w_ref, vel, out, table):
    step = pl.program_id(0)

    @pl.when(step == 0)
    def _():
        places = [(blo, 0), (blo, 1), (blo, 2), (ylo, 1), None, (yhi, 1)]
        places += [(bhi, 0), (bhi, 1), (bhi, 2)]
        for k, place in enumerate(places):
            if place is None:
                table[k * SLOTS : (k + 1) * SLOTS] = jnp.zeros((SLOTS, 8, 128), F32)
                continue
            v = place[0][place[1]].astype(F32).reshape(8, 8, 128)
            turned = pltpu.roll(v, 4, 1)
            for j in range(8):
                table[k * SLOTS + 2 * j] = v[j]
                table[k * SLOTS + 2 * j + 1] = turned[j]

    count = counts[0]
    for group in range(STEP // 4):
        first = step * STEP + group * 4
        rows = [table[slots[first + j]] for j in range(4)]
        for j, v in enumerate(read_four(rows, w_ref, group * 4)):
            at = (group * 4 + j) * 128
            out[:, at : at + 128] = jnp.where(128 + first + j < count, v, 0.0)


def far_read(slots, counts, blo, bhi, ylo, yhi, weights, vel):
    smem = pl.BlockSpec(memory_space=SMEM)
    ans = pl.BlockSpec((3, 64, 128), lambda i: (0, 0, 0))
    return pl.pallas_call(
        far_read_kernel,
        grid=(STEPS,),
        in_specs=[
            smem,
            smem,
            ans,
            ans,
            ans,
            ans,
            pl.BlockSpec((STEP * 128, 128), lambda i: (STEPS + i, 0)),
            pl.BlockSpec(memory_space=pl.ANY),
        ],
        out_specs=pl.BlockSpec((3, STEP * 128), lambda i: (0, STEPS + i)),
        out_shape=jax.ShapeDtypeStruct(vel.shape, F32),
        scratch_shapes=[VMEM((9 * SLOTS, 8, 128), F32)],
        input_output_aliases={7: 0},
        compiler_params=params(16, True),
        cost_estimate=cost(2 * 128 * 32 * 128 * 128, 5 * MIB),
        name="far_read",
    )(slots, counts, blo, bhi, ylo, yhi, weights, vel)


def band(pin, pout):
    out = np.zeros((len(pin), len(pout), 3), np.float32)
    for i, p in enumerate(pin):
        for j, q in enumerate(pout):
            if p is not None and q is not None and abs(p - q) <= 1:
                out[i, j, p - q + 1] = 1
    return jnp.asarray(out, BF16)


def banded(conv, pin, pout, out_last):
    taps = conv.reshape(3, 3, 3, C, C)
    spec = "zdyoc,pqd->zypcoq" if out_last else "zdyoc,pqd->zypcqo"
    t = jnp.einsum(spec, taps, band(pin, pout), preferred_element_type=F32).astype(BF16)
    return t.reshape(9 * len(pin) * C, len(pout) * C)


def on_device(
    features,
    weights,
    owners,
    tile_ids,
    counts,
    conv_first,
    bias_first,
    conv_second,
    bias_second,
    head,
):
    particles = features.shape[1]

    def step(x, axis, by):
        size = lax.axis_size(axis)
        return lax.ppermute(
            x, axis, [(i, i + by) for i in range(size) if 0 <= i + by < size]
        )

    none = None
    t1a = banded(conv_first, [0, 1, 2, 3, 4, 5, 6, 7], [none, 1, 2, 3, 4, 5, 6, none], False)
    t1b = banded(conv_first, [0, 1, -2, -1, 8, 9, 6, 7], [-1, 0, 7, 8], False)
    t2a = banded(conv_second, [none, 1, 2, 3, 4, 5, 6, none], list(range(8)), True)
    t2b = banded(conv_second, [-1, 0, 7, 8], list(range(8)), True)
    same = np.zeros((8, C, C, 8), np.float32)
    for q in range(8):
        same[q, np.arange(C), np.arange(C), q] = 1
    t2a = jnp.concatenate([t2a, jnp.asarray(same.reshape(256, 256), BF16)], 0)
    b1a = jnp.tile(bias_first, 8)[None, :]
    b1b = jnp.tile(bias_first, 4)[None, :]
    b2 = jnp.repeat(bias_second, 8)[None, :]
    headx = jnp.einsum("ao,xw->axow", head, jnp.eye(8, dtype=BF16)).reshape(24, 256)
    headx = jnp.concatenate([headx, jnp.zeros((8, 256), BF16)], 0)

    lo, mid, hi, slots = far_splat(features, weights, owners, tile_ids, counts)
    from_xlo = step(hi, "gx", 1)
    from_xhi = step(lo, "gx", -1)
    own = own_splat(features, weights, tile_ids)
    to_hi = jnp.stack([from_xlo[2], mid[2], from_xhi[2]])
    to_lo = jnp.stack([from_xlo[0], mid[0], from_xhi[0]])
    from_ylo = step(to_hi, "gy", 1)
    from_yhi = step(to_lo, "gy", -1)
    g, ylo, yhi, ids = sum_tiles(own, from_ylo, from_yhi, from_xlo, from_xhi)

    rlo = step(yhi, "gy", 1)
    rhi = step(ylo, "gy", -1)
    x, slo, shi = widen_y(g, rlo, rhi)
    xlo = step(shi, "gx", 1)
    xhi = step(slo, "gx", -1)
    part = inner_convs(x, g, t1a, b1a, t2a, b2)
    grid_out, table, ans_ylo, ans_yhi, ans_x = edge_convs(
        x, xlo, xhi, part, t1b, b1b, t2b, headx, ids
    )

    back_yhi = step(ans_ylo, "gy", -1)
    back_ylo = step(ans_yhi, "gy", 1)
    vel = own_read(tile_ids, table, weights, particles)
    to_lo = jnp.stack([back_ylo[0], ans_x[0], back_yhi[0]])
    to_hi = jnp.stack([back_ylo[2], ans_x[1], back_yhi[2]])
    back_xhi = step(to_lo, "gx", -1)
    back_xlo = step(to_hi, "gx", 1)
    velocity = far_read(slots, counts, back_xlo, back_xhi, back_ylo, back_yhi, weights, vel)
    return grid_out, velocity


def solution(mesh):
    in_specs = (
        P(None, ("gx", "gy")),
        P(("gx", "gy"), None),
        P(("gx", "gy")),
        P(("gx", "gy")),
        P(("gx", "gy")),
        P(),
        P(),
        P(),
        P(),
        P(),
    )
    out_specs = (P(None, None, "gx", "gy"), P(None, ("gx", "gy")))
    return jax.shard_map(
        on_device, mesh=mesh, in_specs=in_specs, out_specs=out_specs, check_vma=False
    )
```

profile of v0, /device:TPU:102, one launch (start us, length us, event | category | flops | bytes accessed | tf_op | source)
XLA Modules:
  0.0 171.7 jit_solution(684127367464004468)
XLA Ops:
  1.3 3.4 %copy-done = bf16[32768,128]{1,0:T(8,128)(2,1)S(1)} copy-done((bf16[32768,128]{1,0:T(8,128)(2,1)S(1)}, bf16[32768,128]{1,0:T(8,128)(2,1)}, u32[]{:S(2)}) %copy-start) | copy-done | bytes 8388632
  7.6 6.3 %far_splat.1 = (bf16[3,528,128]{2,1,0:T(8,128)(2,1)S(1)}, bf16[3,528,128]{2,1,0:T(8,128)(2,1)S(1)}, bf16[3,528,128]{2,1,0:T(8,128)(2,1)S(1)}, s32[128]{0:T(128)S(1)}) custom-call(s32[256]{0:T(256)S(1)} %copy-done.11, s32[256]{0:T(256)S(1)} %copy-done.8, s32[1]{0:T(128)S(6)} %copy.57.counts, bf16[32,32768]{1,0:T(8,128)(2,1)S(1)} %copy-done.2, ...), custom_call_target="tpu_custom_call" | custom-call | flops 134217728 | bytes 6291456 | tf_op jit(solution)/shard_map/far_splat/pallas_call | solution.py:111
  13.9 5.2 %collective-permute-start.1 = (bf16[3,528,128]{2,1,0:T(8,128)(2,1)S(1)}, bf16[3,528,128]{2,1,0:T(8,128)(2,1)S(1)}, u32[]{:S(2)}, u32[]{:S(2)}) collective-permute-start(bf16[3,528,128]{2,1,0:T(8,128)(2,1)S(1)} %get-tuple-element.20), channel_id=1, source_target_pairs={{8,0},{16,8},{24,16},{32,24},{40,32},{48,40},{56,48},{64,56},{72,6... | collective-permute-start | bytes 1216520 | tf_op jit(solution)/shard_map/ppermute | solution.py:582
  19.1 1.9 %collective-permute-start = (bf16[3,528,128]{2,1,0:T(8,128)(2,1)S(1)}, bf16[3,528,128]{2,1,0:T(8,128)(2,1)S(1)}, u32[]{:S(2)}, u32[]{:S(2)}) collective-permute-start(bf16[3,528,128]{2,1,0:T(8,128)(2,1)S(1)} %get-tuple-element.18), channel_id=1, source_target_pairs={{0,8},{8,16},{16,24},{24,32},{32,40},{40,48},{48,56},{56,64},{64,7... | collective-permute-start | bytes 1216520 | tf_op jit(solution)/shard_map/ppermute | solution.py:582
  21.0 3.6 %convert_bitcast_fusion.1 = bf16[3,3,8,32,8,32]{3,4,5,1,0,2:T(8,128)(2,1)} fusion(bf16[8,8,3,1,1,1]{1,2,5,4,3,0:T(4,128)(2,1)S(1)} %copy-done.23, bf16[3,3,3,32,32]{4,3,2,1,0:T(8,128)(2,1)S(1)} %bitcast.52), kind=kOutput, calls=%fused_computation.1 | convolution fusion | flops 4128768 | bytes 1235328 | tf_op jit(solution)/shard_map/zdyoc,pqd->zypcqo/dot_general | solution.py:562
  24.6 2.1 %convert_bitcast_fusion.3 = bf16[3,3,8,32,4,32]{3,2,5,1,0,4:T(8,128)(2,1)} fusion(bf16[8,4,3,1,1,1]{0,2,5,4,3,1:T(4,128)(2,1)S(1)} %copy-done.26, bf16[3,3,3,32,32]{4,3,2,1,0:T(8,128)(2,1)S(1)} %bitcast.53), kind=kOutput, calls=%fused_computation.3 | convolution fusion | flops 2064384 | bytes 645312 | tf_op jit(solution)/shard_map/zdyoc,pqd->zypcqo/dot_general | solution.py:562
  28.5 2.1 %convert_bitcast_fusion.2 = bf16[3,3,4,32,32,8]{3,5,4,1,0,2:T(8,128)(2,1)} fusion(bf16[4,8,3,1,1,1]{1,2,5,4,3,0:T(4,128)(2,1)S(1)} %copy-done.25, bf16[3,3,3,32,32]{4,3,2,1,0:T(8,128)(2,1)S(1)} %bitcast.55), kind=kOutput, calls=%fused_computation.2 | convolution fusion | flops 2064384 | bytes 645312 | tf_op jit(solution)/shard_map/zdyoc,pqd->zypcoq/dot_general | solution.py:562
  30.6 3.3 %collective-permute-done.from_xlo = bf16[3,528,128]{2,1,0:T(8,128)(2,1)S(1)} collective-permute-done((bf16[3,528,128]{2,1,0:T(8,128)(2,1)S(1)}, bf16[3,528,128]{2,1,0:T(8,128)(2,1)S(1)}, u32[]{:S(2)}, u32[]{:S(2)}) %collective-permute-start) | collective-permute-done | bytes 405536 | tf_op jit(solution)/shard_map/ppermute | solution.py:582
  37.5 3.8 %collective-permute-start.3 = (bf16[3,528,128]{2,1,0:T(8,128)(2,1)}, bf16[3,528,128]{2,1,0:T(8,128)(2,1)}, u32[]{:S(2)}, u32[]{:S(2)}) collective-permute-start(bf16[3,528,128]{2,1,0:T(8,128)(2,1)} %pad_maximum_fusion.2), channel_id=1, source_target_pairs={{1,0},{2,1},{3,2},{4,3},{5,4},{6,5},{7,6},{9,8},{10,9},{11,10},{12... | collective-permute-start | bytes 1216520 | tf_op jit(solution)/shard_map/ppermute | solution.py:582
  41.3 7.6 %copy.29 = bf16[3,3,8,32,32,8]{3,2,1,0,5,4:T(8,128)(2,1)} copy(bf16[3,3,8,32,32,8]{3,5,4,1,0,2:T(8,128)(2,1)S(1)} %convert_bitcast_fusion) | data formatting | bytes 2359296 | tf_op jit(solution)/shard_map/convert_element_type | solution.py:562
  48.9 6.4 %reshape.31 = bf16[2304,256]{0,1:T(8,128)(2,1)} reshape(bf16[3,3,8,32,32,8]{3,2,1,0,5,4:T(8,128)(2,1)} %copy.29) | data formatting | bytes 2359296 | tf_op jit(solution)/shard_map/reshape | solution.py:563
  55.4 2.5 %copy.30 = bf16[2304,256]{1,0:T(8,128)(2,1)} copy(bf16[2304,256]{0,1:T(8,128)(2,1)} %reshape.31) | data formatting | bytes 2359296 | tf_op jit(solution)/shard_map/reshape | solution.py:563
  57.9 3.4 %copy-done.1 = bf16[32768,128]{1,0:T(8,128)(2,1)S(1)} copy-done((bf16[32768,128]{1,0:T(8,128)(2,1)S(1)}, bf16[32768,128]{1,0:T(8,128)(2,1)}, u32[]{:S(2)}) %copy-start.1) | copy-done | bytes 8388632
  61.3 5.2 %own_splat.1.own = bf16[2,16,128,128]{3,2,1,0:T(8,128)(2,1)S(1)} custom-call(s32[256]{0:T(256)S(1)} %copy-done.9, bf16[32,32768]{1,0:T(8,128)(2,1)S(1)} %copy-done.3, bf16[32768,128]{1,0:T(8,128)(2,1)S(1)} %copy-done.1), custom_call_target="tpu_custom_call" | custom-call | flops 134217728 | bytes 6291456 | tf_op jit(solution)/shard_map/own_splat/pallas_call | solution.py:152
  66.7 3.3 %sum_tiles.1 = (bf16[2,16,128,128]{3,2,1,0:T(8,128)(2,1)S(1)}, bf16[4,16,128]{2,1,0:T(8,128)(2,1)}, bf16[4,16,128]{2,1,0:T(8,128)(2,1)}, s32[8,128]{1,0:T(8,128)S(1)}) custom-call(bf16[2,16,128,128]{3,2,1,0:T(8,128)(2,1)S(1)} %own_splat.1.own, bf16[3,528,128]{2,1,0:T(8,128)(2,1)S(1)} %collective-permute-done.2.from_ylo, ...), custom_call_target="tpu_custom_call" | custom-call | flops 1000 | bytes 4194304 | tf_op jit(solution)/shard_map/sum_tiles/pallas_call | solution.py:198
  73.5 3.9 %collective-permute-start.5 = (bf16[4,16,128]{2,1,0:T(8,128)(2,1)}, bf16[4,16,128]{2,1,0:T(8,128)(2,1)}, u32[]{:S(2)}, u32[]{:S(2)}) collective-permute-start(bf16[4,16,128]{2,1,0:T(8,128)(2,1)} %get-tuple-element.23), channel_id=1, source_target_pairs={{1,0},{2,1},{3,2},{4,3},{5,4},{6,5},{7,6},{9,8},{10,9},{11,10},{12... | collective-permute-start | bytes 49160 | tf_op jit(solution)/shard_map/ppermute | solution.py:582
  78.1 7.5 %copy.27 = bf16[3,3,8,32,8,32]{5,4,3,2,1,0:T(8,128)(2,1)} copy(bf16[3,3,8,32,8,32]{3,4,5,1,0,2:T(8,128)(2,1)} %convert_bitcast_fusion.1) | data formatting | bytes 2359296 | tf_op jit(solution)/shard_map/convert_element_type | solution.py:562
  85.6 5.8 %reshape.29.t1 = bf16[2304,256]{1,0:T(8,128)(2,1)S(1)} reshape(bf16[3,3,8,32,8,32]{5,4,3,2,1,0:T(8,128)(2,1)} %copy.27) | data formatting | bytes 2359296 | tf_op jit(solution)/shard_map/reshape | solution.py:563
  92.8 6.0 %copy.32 = bf16[3,3,8,32,4,32]{5,4,3,2,1,0:T(4,128)(2,1)} copy(bf16[3,3,8,32,4,32]{3,2,5,1,0,4:T(8,128)(2,1)} %convert_bitcast_fusion.3) | data formatting | bytes 1179648 | tf_op jit(solution)/shard_map/convert_element_type | solution.py:562
  98.9 4.1 %reshape.32.t1 = bf16[2304,128]{1,0:T(8,128)(2,1)} reshape(bf16[3,3,8,32,4,32]{5,4,3,2,1,0:T(4,128)(2,1)} %copy.32) | data formatting | bytes 1179648 | tf_op jit(solution)/shard_map/reshape | solution.py:563
  103.6 4.9 %copy.34 = bf16[3,3,4,32,32,8]{3,2,1,0,5,4:T(4,128)(2,1)} copy(bf16[3,3,4,32,32,8]{3,5,4,1,0,2:T(8,128)(2,1)} %convert_bitcast_fusion.2) | data formatting | bytes 1179648 | tf_op jit(solution)/shard_map/convert_element_type | solution.py:562
  108.5 4.2 %reshape.33 = bf16[1152,256]{0,1:T(8,128)(2,1)} reshape(bf16[3,3,4,32,32,8]{3,2,1,0,5,4:T(4,128)(2,1)} %copy.34) | data formatting | bytes 1179648 | tf_op jit(solution)/shard_map/reshape | solution.py:563
  112.7 2.1 %copy.35.t2 = bf16[1152,256]{1,0:T(8,128)(2,1)} copy(bf16[1152,256]{0,1:T(8,128)(2,1)} %reshape.33) | data formatting | bytes 1179648 | tf_op jit(solution)/shard_map/reshape | solution.py:563
  118.8 1.9 %collective-permute-start.6 = (bf16[8,144,128]{2,1,0:T(8,128)(2,1)S(1)}, bf16[8,144,128]{2,1,0:T(8,128)(2,1)S(1)}, u32[]{:S(2)}, u32[]{:S(2)}) collective-permute-start(bf16[8,144,128]{2,1,0:T(8,128)(2,1)S(1)} %get-tuple-element.25), channel_id=1, source_target_pairs={{0,8},{8,16},{16,24},{24,32},{32,40},{40,48},{48,56},{56,64},{64,7... | collective-permute-start | bytes 884744 | tf_op jit(solution)/shard_map/ppermute | solution.py:582
  120.8 6.0 %collective-permute-start.7 = (bf16[8,144,128]{2,1,0:T(8,128)(2,1)S(1)}, bf16[8,144,128]{2,1,0:T(8,128)(2,1)S(1)}, u32[]{:S(2)}, u32[]{:S(2)}) collective-permute-start(bf16[8,144,128]{2,1,0:T(8,128)(2,1)S(1)} %get-tuple-element.26), channel_id=1, source_target_pairs={{8,0},{16,8},{24,16},{32,24},{40,32},{48,40},{56,48},{64,56},{72,6... | collective-permute-start | bytes 884744 | tf_op jit(solution)/shard_map/ppermute | solution.py:582
  128.5 8.2 %inner_convs.1.part = f32[16,128,256]{2,1,0:T(8,128)S(1)} custom-call(bf16[2,16,144,128]{3,2,1,0:T(8,128)(2,1)S(1)} %get-tuple-element.24.x, bf16[2,16,128,128]{3,2,1,0:T(8,128)(2,1)S(1)} %copy-done.5, bf16[2304,256]{1,0:T(8,128)(2,1)S(1)} %reshape.29.t1, f32[1,256]{1,0:T(1,128)S(1)} %copy-done.12, bf16[2560,256]{1,0:T(8,128)(2,1)S(1)} %pad_maximum_fusion.t2, ...), custom_call_target="tpu_custom_call" | custom-call | flops 6039797760 | bytes 6291456 | tf_op jit(solution)/shard_map/inner_convs/pallas_call | solution.py:314
  136.8 10.5 %edge_convs.1 = (bf16[32,16,8,128]{3,2,1,0:T(8,128)(2,1)}, f32[128,8,128]{2,1,0:T(8,128)S(1)}, bf16[3,64,128]{2,1,0:T(8,128)(2,1)S(1)}, bf16[3,64,128]{2,1,0:T(8,128)(2,1)S(1)}, bf16[2,64,128]{2,1,0:T(8,128)(2,1)S(1)}) custom-call(bf16[2,16,144,128]{3,2,1,0:T(8,128)(2,1)S(1)} %get-tuple-element.24.x, bf16[8,144,128]{2,1,0:T(8,128)(2,1)S(1)} %collective-permute-done.6.rlo, ...), custom_call_target="tpu_custom_call" | custom-call | flops 2717908992 | bytes 6291456 | tf_op jit(solution)/shard_map/edge_convs/pallas_call | solution.py:443
  149.2 2.4 %collective-permute-start.8 = (bf16[3,64,128]{2,1,0:T(8,128)(2,1)S(1)}, bf16[3,64,128]{2,1,0:T(8,128)(2,1)S(1)}, u32[]{:S(2)}, u32[]{:S(2)}) collective-permute-start(bf16[3,64,128]{2,1,0:T(8,128)(2,1)S(1)} %get-tuple-element.30), channel_id=1, source_target_pairs={{0,1},{1,2},{2,3},{3,4},{4,5},{5,6},{6,7},{8,9},{9,10},{10,11},{11... | collective-permute-start | bytes 147464 | tf_op jit(solution)/shard_map/ppermute | solution.py:582
  151.6 3.0 %collective-permute-done.8.ylo = bf16[3,64,128]{2,1,0:T(8,128)(2,1)S(1)} collective-permute-done((bf16[3,64,128]{2,1,0:T(8,128)(2,1)S(1)}, bf16[3,64,128]{2,1,0:T(8,128)(2,1)S(1)}, u32[]{:S(2)}, u32[]{:S(2)}) %collective-permute-start.8) | collective-permute-done | bytes 49184 | tf_op jit(solution)/shard_map/ppermute | solution.py:582
  156.6 6.0 %collective-permute-start.11 = (bf16[3,64,128]{2,1,0:T(8,128)(2,1)S(1)}, bf16[3,64,128]{2,1,0:T(8,128)(2,1)S(1)}, u32[]{:S(2)}, u32[]{:S(2)}) collective-permute-start(bf16[3,64,128]{2,1,0:T(8,128)(2,1)S(1)} %pad_maximum_fusion.4), channel_id=1, source_target_pairs={{8,0},{16,8},{24,16},{32,24},{40,32},{48,40},{56,48},{64,56},{72,6... | collective-permute-start | bytes 147464 | tf_op jit(solution)/shard_map/ppermute | solution.py:582
  162.7 4.5 %own_read.1.vel = f32[3,32768]{1,0:T(4,128)} custom-call(s32[256]{0:T(256)S(1)} %copy-done.10, f32[128,8,128]{2,1,0:T(8,128)S(1)} %get-tuple-element.33.table, bf16[32768,128]{1,0:T(8,128)(2,1)S(1)} %bitcast.51), custom_call_target="tpu_custom_call" | custom-call | flops 134217728 | bytes 5242880 | tf_op jit(solution)/shard_map/own_read/pallas_call | solution.py:482
  167.2 4.5 %far_read.1 = f32[3,32768]{1,0:T(4,128)} custom-call(s32[128]{0:T(128)S(1)} %copy-done.15, s32[1]{0:T(128)S(6)} %copy.57.counts, bf16[3,64,128]{2,1,0:T(8,128)(2,1)S(1)} %collective-permute-done.10.blo, bf16[3,64,128]{2,1,0:T(8,128)(2,1)S(1)} %collective-permute-done.11.bhi, ...), custom_call_target="tpu_custom_call", output_to_operand_aliasing={{}: (7, {})} | custom-call | flops 134217728 | bytes 5242880 | tf_op jit(solution)/shard_map/far_read/pallas_call | solution.py:527
  (100 shorter events, 24.3 us)
Async XLA Ops:
  1.3 3.4 %copy-start = (bf16[32768,128]{1,0:T(8,128)(2,1)S(1)}, bf16[32768,128]{1,0:T(8,128)(2,1)}, u32[]{:S(2)}) copy-start(bf16[32768,128]{1,0:T(8,128)(2,1)} %w_ref.7) | copy-start | bytes 25165828
  7.6 13.4 %copy-start.20 = (bf16[27,32,32]{2,1,0:T(8,128)(2,1)S(1)}, bf16[27,32,32]{2,1,0:T(8,128)(2,1)}, u32[]{:S(2)}) copy-start(bf16[27,32,32]{2,1,0:T(8,128)(2,1)} %param.20) | copy-start | bytes 165892
  7.6 13.4 %copy-start.23 = (bf16[8,8,3,1,1,1]{1,2,5,4,3,0:T(4,128)(2,1)S(1)}, bf16[8,8,3,1,1,1]{1,2,5,4,3,0:T(4,128)(2,1)}, u32[]{:S(2)}) copy-start(bf16[8,8,3,1,1,1]{1,2,5,4,3,0:T(4,128)(2,1)} %constant.20) | copy-start | bytes 1156
  13.9 10.7 %copy-start.14 = (s32[128]{0:T(128)}, s32[128]{0:T(128)S(1)}, u32[]{:S(2)}) copy-start(s32[128]{0:T(128)S(1)} %get-tuple-element.29.slots) | copy-start | bytes 1540
  13.9 16.7 %collective-permute-start.1 = (bf16[3,528,128]{2,1,0:T(8,128)(2,1)S(1)}, bf16[3,528,128]{2,1,0:T(8,128)(2,1)S(1)}, u32[]{:S(2)}, u32[]{:S(2)}) collective-permute-start(bf16[3,528,128]{2,1,0:T(8,128)(2,1)S(1)} %get-tuple-element.20), channel_id=1, source_target_pairs={{8,0},{16,8},{24,16},{32,24},{40,32},{48,40},{56,48},{64,56},{72,6... | collective-permute-start | bytes 1216520 | tf_op jit(solution)/shard_map/ppermute | solution.py:582
  19.1 14.9 %collective-permute-start = (bf16[3,528,128]{2,1,0:T(8,128)(2,1)S(1)}, bf16[3,528,128]{2,1,0:T(8,128)(2,1)S(1)}, u32[]{:S(2)}, u32[]{:S(2)}) collective-permute-start(bf16[3,528,128]{2,1,0:T(8,128)(2,1)S(1)} %get-tuple-element.18), channel_id=1, source_target_pairs={{0,8},{8,16},{16,24},{24,32},{32,40},{40,48},{48,56},{56,64},{64,7... | collective-permute-start | bytes 1216520 | tf_op jit(solution)/shard_map/ppermute | solution.py:582
  21.0 3.6 %copy-start.26 = (bf16[8,4,3,1,1,1]{0,2,5,4,3,1:T(4,128)(2,1)S(1)}, bf16[8,4,3,1,1,1]{0,2,5,4,3,1:T(4,128)(2,1)}, u32[]{:S(2)}) copy-start(bf16[8,4,3,1,1,1]{0,2,5,4,3,1:T(4,128)(2,1)} %constant.22) | copy-start | bytes 580
  34.8 31.9 %collective-permute-start.2 = (bf16[3,528,128]{2,1,0:T(8,128)(2,1)}, bf16[3,528,128]{2,1,0:T(8,128)(2,1)S(1)}, u32[]{:S(2)}, u32[]{:S(2)}) collective-permute-start(bf16[3,528,128]{2,1,0:T(8,128)(2,1)} %pad_maximum_fusion.1), channel_id=1, source_target_pairs={{0,1},{1,2},{2,3},{3,4},{4,5},{5,6},{6,7},{8,9},{9,10},{10,11},{11... | collective-permute-start | bytes 1216520 | tf_op jit(solution)/shard_map/ppermute | solution.py:582
  37.5 29.2 %collective-permute-start.3 = (bf16[3,528,128]{2,1,0:T(8,128)(2,1)}, bf16[3,528,128]{2,1,0:T(8,128)(2,1)}, u32[]{:S(2)}, u32[]{:S(2)}) collective-permute-start(bf16[3,528,128]{2,1,0:T(8,128)(2,1)} %pad_maximum_fusion.2), channel_id=1, source_target_pairs={{1,0},{2,1},{3,2},{4,3},{5,4},{6,5},{7,6},{9,8},{10,9},{11,10},{12... | collective-permute-start | bytes 1216520 | tf_op jit(solution)/shard_map/ppermute | solution.py:582
  57.9 3.4 %copy-start.1 = (bf16[32768,128]{1,0:T(8,128)(2,1)S(1)}, bf16[32768,128]{1,0:T(8,128)(2,1)}, u32[]{:S(2)}) copy-start(bf16[32768,128]{1,0:T(8,128)(2,1)} %w_ref.7) | copy-start | bytes 25165828
  61.3 5.2 %copy-start.19 = (bf16[2304,256]{1,0:T(8,128)(2,1)S(1)}, bf16[2304,256]{1,0:T(8,128)(2,1)}, u32[]{:S(2)}) copy-start(bf16[2304,256]{1,0:T(8,128)(2,1)} %copy.30) | copy-start | bytes 3538948
  61.3 5.2 %copy-start.22 = (bf16[256,256]{1,0:T(8,128)(2,1)S(1)}, bf16[256,256]{1,0:T(8,128)(2,1)}, u32[]{:S(2)}) copy-start(bf16[256,256]{1,0:T(8,128)(2,1)} %constant.16.clone) | copy-start | bytes 393220
  66.5 10.8 %copy-start.28 = (bf16[3,32]{1,0:T(4,128)(2,1)S(1)}, bf16[3,32]{1,0:T(4,128)(2,1)}, u32[]{:S(2)}) copy-start(bf16[3,32]{1,0:T(4,128)(2,1)} %param.24) | copy-start | bytes 580
  71.6 45.8 %collective-permute-start.4 = (bf16[4,16,128]{2,1,0:T(8,128)(2,1)}, bf16[4,16,128]{2,1,0:T(8,128)(2,1)S(1)}, u32[]{:S(2)}, u32[]{:S(2)}) collective-permute-start(bf16[4,16,128]{2,1,0:T(8,128)(2,1)} %get-tuple-element.22), channel_id=1, source_target_pairs={{0,1},{1,2},{2,3},{3,4},{4,5},{5,6},{6,7},{8,9},{9,10},{10,11},{11... | collective-permute-start | bytes 49160 | tf_op jit(solution)/shard_map/ppermute | solution.py:582
  73.5 43.8 %collective-permute-start.5 = (bf16[4,16,128]{2,1,0:T(8,128)(2,1)}, bf16[4,16,128]{2,1,0:T(8,128)(2,1)}, u32[]{:S(2)}, u32[]{:S(2)}) collective-permute-start(bf16[4,16,128]{2,1,0:T(8,128)(2,1)} %get-tuple-element.23), channel_id=1, source_target_pairs={{1,0},{2,1},{3,2},{4,3},{5,4},{6,5},{7,6},{9,8},{10,9},{11,10},{12... | collective-permute-start | bytes 49160 | tf_op jit(solution)/shard_map/ppermute | solution.py:582
  85.6 5.8 %copy-start.27 = (f32[32]{0:T(128)S(1)}, f32[32]{0:T(128)}, u32[]{:S(2)}) copy-start(f32[32]{0:T(128)} %param.21) | copy-start | bytes 388
  85.6 6.5 %copy-start.29 = (f32[32]{0:T(128)S(1)}, f32[32]{0:T(128)}, u32[]{:S(2)}) copy-start(f32[32]{0:T(128)} %param.23) | copy-start | bytes 388
  108.5 8.8 %copy-start.5 = (bf16[2,16,128,128]{3,2,1,0:T(8,128)(2,1)S(1)}, bf16[2,16,128,128]{3,2,1,0:T(8,128)(2,1)}, u32[]{:S(2)}) copy-start(bf16[2,16,128,128]{3,2,1,0:T(8,128)(2,1)} %copy-done.4) | copy-start | bytes 3145732
  118.8 17.9 %collective-permute-start.6 = (bf16[8,144,128]{2,1,0:T(8,128)(2,1)S(1)}, bf16[8,144,128]{2,1,0:T(8,128)(2,1)S(1)}, u32[]{:S(2)}, u32[]{:S(2)}) collective-permute-start(bf16[8,144,128]{2,1,0:T(8,128)(2,1)S(1)} %get-tuple-element.25), channel_id=1, source_target_pairs={{0,8},{8,16},{16,24},{24,32},{32,40},{40,48},{48,56},{56,64},{64,7... | collective-permute-start | bytes 884744 | tf_op jit(solution)/shard_map/ppermute | solution.py:582
  120.8 16.0 %collective-permute-start.7 = (bf16[8,144,128]{2,1,0:T(8,128)(2,1)S(1)}, bf16[8,144,128]{2,1,0:T(8,128)(2,1)S(1)}, u32[]{:S(2)}, u32[]{:S(2)}) collective-permute-start(bf16[8,144,128]{2,1,0:T(8,128)(2,1)S(1)} %get-tuple-element.26), channel_id=1, source_target_pairs={{8,0},{16,8},{24,16},{32,24},{40,32},{48,40},{56,48},{64,56},{72,6... | collective-permute-start | bytes 884744 | tf_op jit(solution)/shard_map/ppermute | solution.py:582
  126.8 35.8 %slice-start = ((s8[8388608]{0:T(1024)(128)(4,1)}), s8[4194304]{0:T(1024)(128)(4,1)S(1)}, s32[]{:S(2)}) async-start(s8[8388608]{0:T(1024)(128)(4,1)} %bitcast.50), calls=%async_computation | async-start | bytes 8388608
  128.5 8.2 %copy-start.6 = (bf16[1152,256]{1,0:T(8,128)(2,1)S(1)}, bf16[1152,256]{1,0:T(8,128)(2,1)}, u32[]{:S(2)}) copy-start(bf16[1152,256]{1,0:T(8,128)(2,1)} %copy.35.t2) | copy-start | bytes 1769476
  128.5 8.2 %copy-start.7 = (bf16[2304,128]{1,0:T(8,128)(2,1)S(1)}, bf16[2304,128]{1,0:T(8,128)(2,1)}, u32[]{:S(2)}) copy-start(bf16[2304,128]{1,0:T(8,128)(2,1)} %reshape.32.t1) | copy-start | bytes 1769476
  128.5 8.2 %copy-start.16 = (f32[1,128]{1,0:T(1,128)S(1)}, f32[1,128]{1,0:T(1,128)}, u32[]{:S(2)}) copy-start(f32[1,128]{1,0:T(1,128)} %broadcast_in_dim_tile.7.b1) | copy-start | bytes 1540
  128.5 8.2 %copy-start.18 = (s32[8,128]{1,0:T(8,128)S(1)}, s32[8,128]{1,0:T(8,128)}, u32[]{:S(2)}) copy-start(s32[8,128]{1,0:T(8,128)} %copy-done.17) | copy-start | bytes 12292
  128.5 34.1 %slice-start.1 = ((s8[8388608]{0:T(1024)(128)(4,1)}), s8[4194304]{0:T(1024)(128)(4,1)S(1)}, s32[]{:S(2)}) async-start(s8[8388608]{0:T(1024)(128)(4,1)} %bitcast.50), calls=%async_computation.1 | async-start | bytes 8388608
  136.8 25.9 %copy-start.10 = (s32[256]{0:T(256)S(1)}, s32[256]{0:T(256)}, u32[]{:S(2)}) copy-start(s32[256]{0:T(256)} %ids.5) | copy-start | bytes 3076
  147.3 4.3 %collective-permute-start.9 = (bf16[3,64,128]{2,1,0:T(8,128)(2,1)S(1)}, bf16[3,64,128]{2,1,0:T(8,128)(2,1)S(1)}, u32[]{:S(2)}, u32[]{:S(2)}) collective-permute-start(bf16[3,64,128]{2,1,0:T(8,128)(2,1)S(1)} %get-tuple-element.32), channel_id=1, source_target_pairs={{1,0},{2,1},{3,2},{4,3},{5,4},{6,5},{7,6},{9,8},{10,9},{11,10},{12... | collective-permute-start | bytes 147464 | tf_op jit(solution)/shard_map/ppermute | solution.py:582
  149.2 5.4 %collective-permute-start.8 = (bf16[3,64,128]{2,1,0:T(8,128)(2,1)S(1)}, bf16[3,64,128]{2,1,0:T(8,128)(2,1)S(1)}, u32[]{:S(2)}, u32[]{:S(2)}) collective-permute-start(bf16[3,64,128]{2,1,0:T(8,128)(2,1)S(1)} %get-tuple-element.30), channel_id=1, source_target_pairs={{0,1},{1,2},{2,3},{3,4},{4,5},{5,6},{6,7},{8,9},{9,10},{10,11},{11... | collective-permute-start | bytes 147464 | tf_op jit(solution)/shard_map/ppermute | solution.py:582
  154.6 12.5 %collective-permute-start.10 = (bf16[3,64,128]{2,1,0:T(8,128)(2,1)S(1)}, bf16[3,64,128]{2,1,0:T(8,128)(2,1)S(1)}, u32[]{:S(2)}, u32[]{:S(2)}) collective-permute-start(bf16[3,64,128]{2,1,0:T(8,128)(2,1)S(1)} %pad_maximum_fusion.3), channel_id=1, source_target_pairs={{0,8},{8,16},{16,24},{24,32},{32,40},{40,48},{48,56},{56,64},{64,7... | collective-permute-start | bytes 147464 | tf_op jit(solution)/shard_map/ppermute | solution.py:582
  156.6 10.6 %collective-permute-start.11 = (bf16[3,64,128]{2,1,0:T(8,128)(2,1)S(1)}, bf16[3,64,128]{2,1,0:T(8,128)(2,1)S(1)}, u32[]{:S(2)}, u32[]{:S(2)}) collective-permute-start(bf16[3,64,128]{2,1,0:T(8,128)(2,1)S(1)} %pad_maximum_fusion.4), channel_id=1, source_target_pairs={{8,0},{16,8},{24,16},{32,24},{40,32},{48,40},{56,48},{64,56},{72,6... | collective-permute-start | bytes 147464 | tf_op jit(solution)/shard_map/ppermute | solution.py:582
  162.7 4.5 %copy-start.15 = (s32[128]{0:T(128)S(1)}, s32[128]{0:T(128)}, u32[]{:S(2)}) copy-start(s32[128]{0:T(128)} %copy-done.14) | copy-start | bytes 1540
  (12 other events, 17.3 us)
where the time goes:
time: 173 us; the launch traced here: 172 us
  local copies, waits for them, and re-layouts  68.8 us (40%)
  Pallas kernels  44 us (25%)
  starting transfers between devices  38.8 us (22%)
  matrix products  9.5 us (5%)
  waiting for transfers between devices  6.3 us (4%)
  other arithmetic  2.47 us (1%)
  between operations  1.78 us (1%)
    ppermute x12, starting transfers between devices, step(): lax.ppermute(x, axis, [(i, i + by) for i in range(size) if 0 <= i + by <...  38.8 us
    convert_element_type x4, local copies, waits for them, and re-layouts, banded(): jnp.einsum(spec, taps, band(pin, pout), preferred_element_type=F32)  26 us
    reshape x6, local copies, waits for them, and re-layouts, banded(): return t.reshape(9 * len(pin) * C, len(pout) * C)  25.1 us
    unnamed x64, local copies, waits for them, and re-layouts  13 us
    pallas_call x1, Pallas kernels, edge_convs(): pl.pallas_call(edge_kernel, in_specs=[vm] * 8 + [pl.BlockSpec(memory_spac...  10.5 us
    dot_general x4, matrix products, banded(): jnp.einsum(spec, taps, band(pin, pout), preferred_element_type=F32)  9.5 us
    pallas_call x1, Pallas kernels, inner_convs(): pl.pallas_call(inner_kernel, in_specs=[vm] * 6, out_specs=vm, out_shape=j...  8.17 us
    ppermute x12, waiting for transfers between devices, step(): lax.ppermute(x, axis, [(i, i + by) for i in range(size) if 0 <= i + by <...  6.3 us
  transfers between devices with their start and end apart: 12, of which 2 were waited for; matrix products, arithmetic and copies ran while one was open for 39% of the time, Pallas kernels for 10%

commit v1 on v0

--- a/solution.py
+++ b/solution.py
@@ -37,15 +37,19 @@
     return pl.CostEstimate(flops=flops, bytes_accessed=nbytes, transcendentals=0)
 
 
-def splat_four(f_ref, w_ref, first):
+def splat_four(f, w_ref, first):
     parts = []
-    for j in range(4):
+    for j in (0, 2):
         at = (first + j) * 128
-        parts.append(
-            jnp.dot(f_ref[:, at : at + 128], w_ref[at : at + 128, :], preferred_element_type=F32)
+        fa = f[:, at : at + 128]
+        fb = f[:, at + 128 : at + 256]
+        none = jnp.zeros_like(fa)
+        lhs = jnp.concatenate(
+            [jnp.concatenate([fa, none], 1), jnp.concatenate([none, fb], 1)], 0
         )
-    a = jnp.concatenate(parts, 0).astype(BF16).astype(F32)
-    a = a.T.reshape(4, 2, 2, 8, 128)
+        parts.append(jnp.dot(lhs, w_ref[at : at + 256, :], preferred_element_type=F32))
+    a = jnp.concatenate(parts, 0).astype(BF16).T.astype(F32)
+    a = a.reshape(4, 2, 2, 8, 128)
     lane = lanes_of((4, 2, 8, 128))
     v0, v1 = a[:, 0], a[:, 1]
     n0 = jnp.where(lane < 64, v0, pltpu.roll(v1, 64, 3))
@@ -59,24 +63,54 @@
     return tiles
 
 
-def far_splat_kernel(owners, ids, counts, f_ref, w_ref, lo, mid, hi, slots, tiles, idrows, filled):
-    step = pl.program_id(0)
+def chunk_copies(f_hbm, w_hbm, fv, wv, sems, first):
+    rows = STEP * 128
+    pairs = []
+    for c in range(STEPS):
+        at = first * 128 + c * rows
+        pairs.append(
+            (
+                pltpu.make_async_copy(
+                    w_hbm.at[pl.ds(at, rows)], wv.at[pl.ds(c * rows, rows)], sems.at[c]
+                ),
+                pltpu.make_async_copy(f_hbm.at[:, pl.ds(at, rows)], fv.at[c], sems.at[STEPS + c]),
+            )
+        )
+    return pairs
+
+
+def far_splat_kernel(
+    owners_h, ids_h, counts_h, f_hbm, w_hbm, lo, mid, hi, slots,
+    fv, wv, tiles, idrows, filled, owners, ids, counts, sems, isems,
+):
     ix = lax.axis_index("gx")
     iy = lax.axis_index("gy")
-
-    @pl.when(step == 0)
-    def _():
-        tiles[...] = jnp.zeros_like(tiles)
-        idrows[...] = jnp.zeros_like(idrows)
-        for k in range(9):
-            filled[k] = 0
-
+    copies = chunk_copies(f_hbm, w_hbm, fv, wv, sems, 128)
+    small = [
+        pltpu.make_async_copy(src, dst, isems.at[k])
+        for k, (src, dst) in enumerate(((owners_h, owners), (ids_h, ids), (counts_h, counts)))
+    ]
+    for copy in small:
+        copy.start()
+    for pair in copies:
+        for copy in pair:
+            copy.start()
+    tiles[...] = jnp.zeros_like(tiles)
+    idrows[...] = jnp.zeros_like(idrows)
+    for k in range(9):
+        filled[k] = 0
+    for copy in small:
+        copy.wait()
     lane = lanes_of((1, 128))
     count = counts[0]
-    for group in range(STEP // 4):
-        got = splat_four(f_ref, w_ref, group * 4)
-        for j in range(4):
-            block = step * STEP + group * 4 + j
+    for c, pair in enumerate(copies):
+        for copy in pair:
+            copy.wait()
+        got = []
+        for group in range(STEP // 4):
+            got += splat_four(fv.at[c], wv.at[pl.ds(c * STEP * 128, STEP * 128)], group * 4)
+        for j in range(STEP):
+            block = c * STEP + j
             owner = owners[128 + block]
             live = 128 + block < count
             target = ((owner >> 3) - ix + 1) * 3 + (owner & 7) - iy + 1
@@ -90,42 +124,39 @@
             idrows[pl.ds(target, 1), :] = jnp.where(
                 lane == rank, ids[128 + block].astype(F32), row
             )
-
-    @pl.when(step == STEPS - 1)
-    def _():
-        for dx, out in enumerate((lo, mid, hi)):
-            for dy in range(3):
-                k = dx * 3 + dy
-                out[dy, 0 : SLOTS * 32, :] = tiles[k * SLOTS : (k + 1) * SLOTS].reshape(
-                    SLOTS * 32, 128
-                )
-                out[dy, SLOTS * 32 : PAY, :] = jnp.broadcast_to(
-                    idrows[k : k + 1, :], (16, 128)
-                ).astype(BF16)
+    for dx, out in enumerate((lo, mid, hi)):
+        for dy in range(3):
+            k = dx * 3 + dy
+            out[dy, 0 : SLOTS * 32, :] = tiles[k * SLOTS : (k + 1) * SLOTS].reshape(
+                SLOTS * 32, 128
+            )
+            out[dy, SLOTS * 32 : PAY, :] = jnp.broadcast_to(
+                idrows[k : k + 1, :], (16, 128)
+            ).astype(BF16)
 
 
 def far_splat(features, weights, owners, ids, counts):
     pay = jax.ShapeDtypeStruct((3, PAY, 128), BF16)
-    whole = pl.BlockSpec((3, PAY, 128), lambda i: (0, 0, 0))
-    smem = pl.BlockSpec(memory_space=SMEM)
+    vm = pl.BlockSpec(memory_space=VMEM)
+    anywhere = pl.BlockSpec(memory_space=pl.ANY)
     return pl.pallas_call(
         far_splat_kernel,
-        grid=(STEPS,),
-        in_specs=[
-            smem,
-            smem,
-            smem,
-            pl.BlockSpec((C, STEP * 128), lambda i: (0, STEPS + i)),
-            pl.BlockSpec((STEP * 128, 128), lambda i: (STEPS + i, 0)),
-        ],
-        out_specs=[whole, whole, whole, smem],
+        in_specs=[anywhere] * 5,
+        out_specs=[vm, vm, vm, pl.BlockSpec(memory_space=SMEM)],
         out_shape=[pay, pay, pay, jax.ShapeDtypeStruct((128,), jnp.int32)],
         scratch_shapes=[
+            VMEM((STEPS, C, STEP * 128), BF16),
+            VMEM((STEPS * STEP * 128, 128), BF16),
             VMEM((9 * SLOTS, 32, 128), BF16),
             VMEM((16, 128), F32),
             SMEM((9,), jnp.int32),
-        ],
-        compiler_params=params(16, True),
+            SMEM((256,), jnp.int32),
+            SMEM((256,), jnp.int32),
+            SMEM((1,), jnp.int32),
+            pltpu.SemaphoreType.DMA((2 * STEPS,)),
+            pltpu.SemaphoreType.DMA((3,)),
+        ],
+        compiler_params=params(56),
         cost_estimate=cost(2 * 128 * 32 * 128 * 128, 6 * MIB),
         name="far_splat",
     )(owners, ids, counts, features, weights)
@@ -135,32 +166,37 @@
     return (tile >> 5) * 4, (tile >> 4) & 1, pl.multiple_of((tile & 15) * 8, 8)
 
 
-def own_splat_kernel(ids, f_ref, w_ref, out, grid):
-    step = pl.program_id(0)
-    for group in range(STEP // 4):
-        got = splat_four(f_ref, w_ref, group * 4)
-        for j in range(4):
-            z, tx, y = tile_place(ids[step * STEP + group * 4 + j])
+def own_splat_kernel(ids, f_hbm, w_hbm, out, fv, wv, grid, sems):
+    copies = chunk_copies(f_hbm, w_hbm, fv, wv, sems, 0)
+    for pair in copies:
+        for copy in pair:
+            copy.start()
+    for c, pair in enumerate(copies):
+        for copy in pair:
+            copy.wait()
+        got = []
+        for group in range(STEP // 4):
+            got += splat_four(fv.at[c], wv.at[pl.ds(c * STEP * 128, STEP * 128)], group * 4)
+        for j in range(STEP):
+            z, tx, y = tile_place(ids[c * STEP + j])
             grid[tx, pl.ds(z, 4), pl.ds(y, 8), :] = got[j]
-
-    @pl.when(step == STEPS - 1)
-    def _():
-        out[...] = grid[...].astype(BF16)
+    out[...] = grid[...].astype(BF16)
 
 
 def own_splat(features, weights, ids):
+    anywhere = pl.BlockSpec(memory_space=pl.ANY)
     return pl.pallas_call(
         own_splat_kernel,
-        grid=(STEPS,),
-        in_specs=[
-            pl.BlockSpec(memory_space=SMEM),
-            pl.BlockSpec((C, STEP * 128), lambda i: (0, i)),
-            pl.BlockSpec((STEP * 128, 128), lambda i: (i, 0)),
-        ],
-        out_specs=pl.BlockSpec((2, SLAB, BY, 128), lambda i: (0, 0, 0, 0)),
+        in_specs=[pl.BlockSpec(memory_space=SMEM), anywhere, anywhere],
+        out_specs=pl.BlockSpec(memory_space=VMEM),
         out_shape=jax.ShapeDtypeStruct((2, SLAB, BY, 128), BF16),
-        scratch_shapes=[VMEM((2, SLAB, BY, 128), F32)],
-        compiler_params=params(16, True),
+        scratch_shapes=[
+            VMEM((STEPS, C, STEP * 128), BF16),
+            VMEM((STEPS * STEP * 128, 128), BF16),
+            VMEM((2, SLAB, BY, 128), F32),
+            pltpu.SemaphoreType.DMA((2 * STEPS,)),
+        ],
+        compiler_params=params(56),
         cost_estimate=cost(2 * 128 * 32 * 128 * 128, 6 * MIB),
         name="own_splat",
     )(ids, features, weights)
@@ -418,7 +454,6 @@
                     row = (tz * 4 + k * 2 + kk) * 8
                     table[row : row + 8, a, :] = w[tz]
 
-    srow = lax.broadcasted_iota(jnp.int32, (8, 128), 0)
     places = [(ans_ylo, 0), (ans_ylo, 1), (ans_ylo, 2), (ans_yhi, 0), (ans_yhi, 1), (ans_yhi, 2)]
     places += [(ans_x, 0), (ans_x, 1)]
     for n, (ref, k) in enumerate(places):
@@ -428,7 +463,7 @@
             for h in range(2):
                 r0 = table[tile_row(ids[n, j * 4 + 2 * h])]
                 r1 = table[tile_row(ids[n, j * 4 + 2 * h + 1])]
-                halves.append(jnp.where(srow < 4, r0, pltpu.roll(r1, 4, 0)))
+                halves.append(two_blocks(r0, r1))
             ref[k, pl.ds(pl.multiple_of(j * 16, 16), 16), :] = jnp.concatenate(halves, 0).astype(
                 BF16
             )
@@ -462,105 +497,201 @@
     )(x, rlo, rhi, part, t1, b1, t2, headx, ids)
 
 
-def read_four(rows, w_ref, first):
-    lhs = jnp.concatenate(rows, 0).astype(BF16)
-    w = w_ref[first * 128 : (first + 4) * 128, :]
-    r = lax.dot_general(lhs, w, (((1,), (1,)), ((), ())), preferred_element_type=F32)
-    return [r[8 * j : 8 * j + 3, 128 * j : 128 * j + 128] for j in range(4)]
-
-
-def own_read_kernel(ids, table, w_ref, out):
-    step = pl.program_id(0)
-    for group in range(STEP // 4):
-        rows = [table[tile_row(ids[step * STEP + group * 4 + j])] for j in range(4)]
-        for j, v in enumerate(read_four(rows, w_ref, group * 4)):
-            at = (group * 4 + j) * 128
-            out[:, at : at + 128] = v
+BATCH = 32
+
+
+def read_batch(rows, w_ref, first, out, at, count):
+    cells = rows.astype(BF16).T
+    owner = lanes_of((128, 128)) >> 2
+    right = jnp.concatenate(
+        [jnp.where(owner == b, cells, jnp.zeros_like(cells)) for b in range(BATCH)], 0
+    )
+    left = jnp.concatenate(
+        [w_ref[(first + b) * 128 : (first + b + 1) * 128, :] for b in range(BATCH)], 1
+    )
+    r = jnp.dot(left, right, preferred_element_type=F32).T
+    for b in range(BATCH):
+        v = r[4 * b : 4 * b + 3]
+        if count is not None:
+            v = jnp.where(128 + first + b < count, v, 0.0)
+        out[:, at + b * 128 : at + (b + 1) * 128] = v
+
+
+def two_blocks(r0, r1):
+    row = lax.broadcasted_iota(jnp.int32, (8, 128), 0)
+    return jnp.where(row < 4, r0, pltpu.roll(r1, 4, 0))
+
+
+def weight_copies(w_hbm, wv, sems, first):
+    n = 128 // BATCH
+    rows = BATCH * 128
+    return [
+        pltpu.make_async_copy(
+            w_hbm.at[pl.ds(first * 128 + k * rows, rows)], wv.at[pl.ds(k * rows, rows)], sems.at[k]
+        )
+        for k in range(n)
+    ]
+
+
+def own_read_kernel(ids, table, w_hbm, out, far_w, wv, sems, fsems):
+    copies = weight_copies(w_hbm, wv, sems, 0)
+    later = weight_copies(w_hbm, far_w, fsems, 128)
+    for copy in copies + later:
+        copy.start()
+    for k, copy in enumerate(copies):
+        rows = [
+            two_blocks(
+                table[tile_row(ids[k * BATCH + 2 * j])], table[tile_row(ids[k * BATCH + 2 * j + 1])]
+            )
+            for j in range(BATCH // 2)
+        ]
+        copy.wait()
+        read_batch(jnp.concatenate(rows, 0), wv, k * BATCH, out, k * BATCH * 128, None)
+    for copy in later:
+        copy.wait()
 
 
 def own_read(ids, table, weights, particles):
+    vm = pl.BlockSpec(memory_space=VMEM)
     return pl.pallas_call(
         own_read_kernel,
-        grid=(STEPS,),
-        in_specs=[
-            pl.BlockSpec(memory_space=SMEM),
-            pl.BlockSpec((128, 8, 128), lambda i: (0, 0, 0)),
-            pl.BlockSpec((STEP * 128, 128), lambda i: (i, 0)),
-        ],
-        out_specs=pl.BlockSpec((3, STEP * 128), lambda i: (0, i)),
-        out_shape=jax.ShapeDtypeStruct((3, particles), F32),
-        compiler_params=params(16, True),
-        cost_estimate=cost(2 * 128 * 32 * 128 * 128, 5 * MIB),
+        in_specs=[pl.BlockSpec(memory_space=SMEM), vm, pl.BlockSpec(memory_space=pl.ANY)],
+        out_specs=[vm, vm],
+        out_shape=[
+            jax.ShapeDtypeStruct((3, particles // 2), F32),
+            jax.ShapeDtypeStruct((particles // 2, 128), BF16),
+        ],
+        scratch_shapes=[
+            VMEM((particles // 2, 128), BF16),
+            pltpu.SemaphoreType.DMA((128 // BATCH,)),
+            pltpu.SemaphoreType.DMA((128 // BATCH,)),
+        ],
+        compiler_params=params(48),
+        cost_estimate=cost(2 * 128 * 32 * 128 * 128, 9 * MIB),
         name="own_read",
     )(ids, table, weights)
 
 
-def far_read_kernel(slots, counts, blo, bhi, ylo, yhi, w_ref, vel, out, table):
-    step = pl.program_id(0)
-
-    @pl.when(step == 0)
-    def _():
-        places = [(blo, 0), (blo, 1), (blo, 2), (ylo, 1), None, (yhi, 1)]
-        places += [(bhi, 0), (bhi, 1), (bhi, 2)]
-        for k, place in enumerate(places):
-            if place is None:
-                table[k * SLOTS : (k + 1) * SLOTS] = jnp.zeros((SLOTS, 8, 128), F32)
-                continue
-            v = place[0][place[1]].astype(F32).reshape(8, 8, 128)
-            turned = pltpu.roll(v, 4, 1)
-            for j in range(8):
-                table[k * SLOTS + 2 * j] = v[j]
-                table[k * SLOTS + 2 * j + 1] = turned[j]
-
-    count = counts[0]
-    for group in range(STEP // 4):
-        first = step * STEP + group * 4
-        rows = [table[slots[first + j]] for j in range(4)]
-        for j, v in enumerate(read_four(rows, w_ref, group * 4)):
-            at = (group * 4 + j) * 128
-            out[:, at : at + 128] = jnp.where(128 + first + j < count, v, 0.0)
-
-
-def far_read(slots, counts, blo, bhi, ylo, yhi, weights, vel):
+def far_read_kernel(slots, counts, blo, bhi, ylo, yhi, w, near, out, table):
+    places = [(blo, 0), (blo, 1), (blo, 2), (ylo, 1), None, (yhi, 1)]
+    places += [(bhi, 0), (bhi, 1), (bhi, 2)]
+    for k, place in enumerate(places):
+        if place is None:
+            table[k * SLOTS : (k + 1) * SLOTS] = jnp.zeros((SLOTS, 8, 128), F32)
+            continue
+        v = place[0][place[1]].astype(F32).reshape(8, 8, 128)
+        turned = pltpu.roll(v, 4, 1)
+        for j in range(8):
+            table[k * SLOTS + 2 * j] = v[j]
+            table[k * SLOTS + 2 * j + 1] = turned[j]
+    half = near.shape[1]
+    out[:, 0:half] = near[...]
+    for k in range(128 // BATCH):
+        rows = [
+            two_blocks(table[slots[k * BATCH + 2 * j]], table[slots[k * BATCH + 2 * j + 1]])
+            for j in range(BATCH // 2)
+        ]
+        read_batch(
+            jnp.concatenate(rows, 0), w, k * BATCH, out, half + k * BATCH * 128, counts[0]
+        )
+
+
+def far_read(slots, counts, blo, bhi, ylo, yhi, w, near):
+    vm = pl.BlockSpec(memory_space=VMEM)
     smem = pl.BlockSpec(memory_space=SMEM)
-    ans = pl.BlockSpec((3, 64, 128), lambda i: (0, 0, 0))
     return pl.pallas_call(
         far_read_kernel,
-        grid=(STEPS,),
-        in_specs=[
-            smem,
-            smem,
-            ans,
-            ans,
-            ans,
-            ans,
-            pl.BlockSpec((STEP * 128, 128), lambda i: (STEPS + i, 0)),
-            pl.BlockSpec(memory_space=pl.ANY),
-        ],
-        out_specs=pl.BlockSpec((3, STEP * 128), lambda i: (0, STEPS + i)),
-        out_shape=jax.ShapeDtypeStruct(vel.shape, F32),
+        in_specs=[smem, smem] + [vm] * 6,
+        out_specs=vm,
+        out_shape=jax.ShapeDtypeStruct((3, 2 * near.shape[1]), F32),
         scratch_shapes=[VMEM((9 * SLOTS, 8, 128), F32)],
-        input_output_aliases={7: 0},
-        compiler_params=params(16, True),
+        compiler_params=params(24),
         cost_estimate=cost(2 * 128 * 32 * 128 * 128, 5 * MIB),
         name="far_read",
-    )(slots, counts, blo, bhi, ylo, yhi, weights, vel)
-
-
-def band(pin, pout):
-    out = np.zeros((len(pin), len(pout), 3), np.float32)
+    )(slots, counts, blo, bhi, ylo, yhi, w, near)
+
+
+def band(pin, pout, out_last):
+    out = np.zeros((4, C, len(pin), len(pout), C), np.float32)
     for i, p in enumerate(pin):
         for j, q in enumerate(pout):
             if p is not None and q is not None and abs(p - q) <= 1:
-                out[i, j, p - q + 1] = 1
-    return jnp.asarray(out, BF16)
-
-
-def banded(conv, pin, pout, out_last):
-    taps = conv.reshape(3, 3, 3, C, C)
-    spec = "zdyoc,pqd->zypcoq" if out_last else "zdyoc,pqd->zypcqo"
-    t = jnp.einsum(spec, taps, band(pin, pout), preferred_element_type=F32).astype(BF16)
-    return t.reshape(9 * len(pin) * C, len(pout) * C)
+                out[p - q + 1, np.arange(C), i, j, np.arange(C)] = 1
+    if out_last:
+        out = out.swapaxes(3, 4)
+    return jnp.asarray(out.reshape(4 * C, -1), BF16)
+
+
+def prepare_kernel(
+    c1, c2, bias1, bias2, head, e1a, e1b, e2a, e2b, t1a, t1b, t2a, t2b, hx, b1a, b1b, b2
+):
+    one = (
+        lax.broadcasted_iota(jnp.int32, (C, C), 0) == lax.broadcasted_iota(jnp.int32, (C, C), 1)
+    ).astype(BF16)
+    nothing = jnp.zeros((C, C), BF16)
+    for conv, made in ((c1, ((e1a, t1a, 256), (e1b, t1b, 128))), (c2, ((e2a, t2a, 256), (e2b, t2b, 256)))):
+        pieces = []
+        for k in range(9):
+            pieces += [conv[k // 3 * 9 + d * 3 + k % 3] for d in range(3)] + [nothing]
+        turned = lax.dot_general(
+            one, jnp.concatenate(pieces, 0), (((1,), (1,)), ((), ())), preferred_element_type=F32
+        ).astype(BF16)
+        lhs = jnp.concatenate([turned[:, 128 * k : 128 * k + 128] for k in range(9)], 0)
+        for e, t, width in made:
+            planes = e.shape[1] // width
+            for p in range(planes):
+                r = jnp.dot(lhs, e[:, p * width : (p + 1) * width], preferred_element_type=F32)
+                r = r.astype(BF16)
+                for k in range(9):
+                    at = (k * planes + p) * C
+                    t[at : at + C, :] = r[C * k : C * k + C]
+    row = lax.broadcasted_iota(jnp.int32, (256, 256), 0)
+    col = lanes_of((256, 256))
+    t2a[2304:2560, :] = ((row & 31) == (col >> 3)).astype(F32).astype(BF16) * (
+        (row >> 5) == (col & 7)
+    ).astype(F32).astype(BF16)
+    spread = (
+        lax.broadcasted_iota(jnp.int32, (C, 256), 0) == (lanes_of((C, 256)) >> 3)
+    ).astype(F32)
+    wide = jnp.dot(head[...], spread.astype(BF16), preferred_element_type=F32)
+    keep = (lanes_of((8, 256)) & 7) == lax.broadcasted_iota(jnp.int32, (8, 256), 0)
+    parts = [jnp.where(keep, jnp.broadcast_to(wide[a : a + 1], (8, 256)), 0.0) for a in range(3)]
+    hx[...] = jnp.concatenate(parts + [jnp.zeros((8, 256), F32)], 0).astype(BF16)
+    b1 = jnp.concatenate([bias1[...]] * 8, 1)
+    b1a[...] = b1
+    b1b[...] = b1[:, 0:128]
+    b2[...] = jnp.dot(
+        bias2[...], spread, preferred_element_type=F32, precision=lax.Precision.HIGHEST
+    )
+
+
+def prepare(conv_first, conv_second, bias_first, bias_second, head):
+    none = None
+    inner = [none, 1, 2, 3, 4, 5, 6, none]
+    every = list(range(8))
+    e1a = band(every, inner, False)
+    e1b = band([0, 1, -2, -1, 8, 9, 6, 7], [-1, 0, 7, 8], False)
+    e2a = band(inner, every, True)
+    e2b = band([-1, 0, 7, 8], every, True)
+    vm = pl.BlockSpec(memory_space=VMEM)
+    return pl.pallas_call(
+        prepare_kernel,
+        in_specs=[vm] * 9,
+        out_specs=[vm] * 8,
+        out_shape=[
+            jax.ShapeDtypeStruct((2304, 256), BF16),
+            jax.ShapeDtypeStruct((2304, 128), BF16),
+            jax.ShapeDtypeStruct((2560, 256), BF16),
+            jax.ShapeDtypeStruct((1152, 256), BF16),
+            jax.ShapeDtypeStruct((32, 256), BF16),
+            jax.ShapeDtypeStruct((1, 256), F32),
+            jax.ShapeDtypeStruct((1, 128), F32),
+            jax.ShapeDtypeStruct((1, 256), F32),
+        ],
+        compiler_params=params(16),
+        cost_estimate=cost(2 * 300 * 128 * 6144, 5 * MIB),
+        name="prepare",
+    )(conv_first, conv_second, bias_first[None], bias_second[None], head, e1a, e1b, e2a, e2b)
 
 
 def on_device(
@@ -583,24 +714,12 @@
             x, axis, [(i, i + by) for i in range(size) if 0 <= i + by < size]
         )
 
-    none = None
-    t1a = banded(conv_first, [0, 1, 2, 3, 4, 5, 6, 7], [none, 1, 2, 3, 4, 5, 6, none], False)
-    t1b = banded(conv_first, [0, 1, -2, -1, 8, 9, 6, 7], [-1, 0, 7, 8], False)
-    t2a = banded(conv_second, [none, 1, 2, 3, 4, 5, 6, none], list(range(8)), True)
-    t2b = banded(conv_second, [-1, 0, 7, 8], list(range(8)), True)
-    same = np.zeros((8, C, C, 8), np.float32)
-    for q in range(8):
-        same[q, np.arange(C), np.arange(C), q] = 1
-    t2a = jnp.concatenate([t2a, jnp.asarray(same.reshape(256, 256), BF16)], 0)
-    b1a = jnp.tile(bias_first, 8)[None, :]
-    b1b = jnp.tile(bias_first, 4)[None, :]
-    b2 = jnp.repeat(bias_second, 8)[None, :]
-    headx = jnp.einsum("ao,xw->axow", head, jnp.eye(8, dtype=BF16)).reshape(24, 256)
-    headx = jnp.concatenate([headx, jnp.zeros((8, 256), BF16)], 0)
-
     lo, mid, hi, slots = far_splat(features, weights, owners, tile_ids, counts)
     from_xlo = step(hi, "gx", 1)
     from_xhi = step(lo, "gx", -1)
+    t1a, t1b, t2a, t2b, headx, b1a, b1b, b2 = prepare(
+        conv_first, conv_second, bias_first, bias_second, head
+    )
     own = own_splat(features, weights, tile_ids)
     to_hi = jnp.stack([from_xlo[2], mid[2], from_xhi[2]])
     to_lo = jnp.stack([from_xlo[0], mid[0], from_xhi[0]])
@@ -620,12 +739,12 @@
 
     back_yhi = step(ans_ylo, "gy", -1)
     back_ylo = step(ans_yhi, "gy", 1)
-    vel = own_read(tile_ids, table, weights, particles)
+    near, far_w = own_read(tile_ids, table, weights, particles)
     to_lo = jnp.stack([back_ylo[0], ans_x[0], back_yhi[0]])
     to_hi = jnp.stack([back_ylo[2], ans_x[1], back_yhi[2]])
     back_xhi = step(to_lo, "gx", -1)
     back_xlo = step(to_hi, "gx", 1)
-    velocity = far_read(slots, counts, back_xlo, back_xhi, back_ylo, back_yhi, weights, vel)
+    velocity = far_read(slots, counts, back_xlo, back_xhi, back_ylo, back_yhi, far_w, near)
     return grid_out, velocity
 
 

time: 173 us -> 99.3 us (0.57)
  the two profiles are of different devices: /device:TPU:102 before, /device:TPU:39 now
where the time goes in v1:
time: 99.3 us; the launch traced here: 98.8 us
  Pallas kernels  42.6 us (43%)
  starting transfers between devices  39.5 us (40%)
  waiting for transfers between devices  12.6 us (13%)
  local copies, waits for them, and re-layouts  2.34 us (2%)
  between operations  1.71 us (2%)
    ppermute x12, starting transfers between devices, step(): lax.ppermute(x, axis, [(i, i + by) for i in range(size) if 0 <= i + by <...  39.5 us
    ppermute x12, waiting for transfers between devices, step(): lax.ppermute(x, axis, [(i, i + by) for i in range(size) if 0 <= i + by <...  12.6 us
    pallas_call x1, Pallas kernels, edge_convs(): pl.pallas_call(edge_kernel, in_specs=[vm] * 8 + [pl.BlockSpec(memory_spac...  10.5 us
    pallas_call x1, Pallas kernels, inner_convs(): pl.pallas_call(inner_kernel, in_specs=[vm] * 6, out_specs=vm, out_shape=j...  8.17 us
    pallas_call x1, Pallas kernels, own_splat(): pl.pallas_call(own_splat_kernel, in_specs=[pl.BlockSpec(memory_space=SMEM...  6.58 us
    pallas_call x1, Pallas kernels, far_splat(): pl.pallas_call(far_splat_kernel, in_specs=[anywhere] * 5, out_specs=[vm,...  5.85 us
    pallas_call x1, Pallas kernels, own_read(): pl.pallas_call(own_read_kernel, in_specs=[pl.BlockSpec(memory_space=SMEM)...  4.28 us
    pallas_call x1, Pallas kernels, far_read(): pl.pallas_call(far_read_kernel, in_specs=[smem, smem] + [vm] * 6, out_spe...  2.75 us
  transfers between devices with their start and end apart: 12, of which 5 were waited for; matrix products, arithmetic and copies ran while one was open for 1% of the time, Pallas kernels for 21%

profile of v1, /device:TPU:39, one launch (start us, length us, event | category | flops | bytes accessed | tf_op | source)
XLA Modules:
  0.0 98.8 jit_solution(13620574295964076473)
XLA Ops:
  1.3 5.8 %far_splat.1 = (bf16[3,528,128]{2,1,0:T(8,128)(2,1)}, bf16[3,528,128]{2,1,0:T(8,128)(2,1)}, bf16[3,528,128]{2,1,0:T(8,128)(2,1)}, s32[128]{0:T(128)}) custom-call(s32[256]{0:T(256)} %owners_h.1, s32[256]{0:T(256)} %ids.3, s32[1]{0:T(128)S(6)} %copy.16.counts_h.counts, bf16[32,32768]{1,0:T(8,128)(2,1)} %f_hbm.3, bf16[32768,128]{1,0:T(8,128)(2,1)} %w_hbm.5), custom_call_target="tpu_custom_call" | custom-call | flops 134217728 | bytes 6291456 | tf_op jit(solution)/shard_map/far_splat/pallas_call | solution.py:142
  7.1 3.2 %collective-permute-start = (bf16[3,528,128]{2,1,0:T(8,128)(2,1)}, bf16[3,528,128]{2,1,0:T(8,128)(2,1)S(1)}, u32[]{:S(2)}, u32[]{:S(2)}) collective-permute-start(bf16[3,528,128]{2,1,0:T(8,128)(2,1)} %get-tuple-element.28), channel_id=1, source_target_pairs={{0,8},{8,16},{16,24},{24,32},{32,40},{40,48},{48,56},{56,64},{64,7... | collective-permute-start | bytes 1216520 | tf_op jit(solution)/shard_map/ppermute | solution.py:713
  10.4 4.2 %collective-permute-start.1 = (bf16[3,528,128]{2,1,0:T(8,128)(2,1)}, bf16[3,528,128]{2,1,0:T(8,128)(2,1)S(1)}, u32[]{:S(2)}, u32[]{:S(2)}) collective-permute-start(bf16[3,528,128]{2,1,0:T(8,128)(2,1)} %get-tuple-element.30), channel_id=1, source_target_pairs={{8,0},{16,8},{24,16},{32,24},{40,32},{48,40},{56,48},{64,56},{72,6... | collective-permute-start | bytes 1216520 | tf_op jit(solution)/shard_map/ppermute | solution.py:713
  14.5 1.0 %fusion.1 = (bf16[1,528,128]{2,1,0:T(8,128)(2,1)S(1)}, bf16[1,528,128]{2,1,0:T(8,128)(2,1)S(1)}) fusion(bf16[3,528,128]{2,1,0:T(8,128)(2,1)} %get-tuple-element.29), kind=kLoop, calls=%fused_computation.5 | loop fusion | bytes 540672 | tf_op jit(solution)/shard_map/slice | solution.py:725
  15.5 6.1 %collective-permute-done.from_xlo = bf16[3,528,128]{2,1,0:T(8,128)(2,1)S(1)} collective-permute-done((bf16[3,528,128]{2,1,0:T(8,128)(2,1)}, bf16[3,528,128]{2,1,0:T(8,128)(2,1)S(1)}, u32[]{:S(2)}, u32[]{:S(2)}) %collective-permute-start) | collective-permute-done | bytes 405536 | tf_op jit(solution)/shard_map/ppermute | solution.py:713
  21.6 0.9 collective-permute-done.1.from_xhi
  22.7 5.3 %collective-permute-start.2 = (bf16[3,528,128]{2,1,0:T(8,128)(2,1)S(1)}, bf16[3,528,128]{2,1,0:T(8,128)(2,1)S(1)}, u32[]{:S(2)}, u32[]{:S(2)}) collective-permute-start(bf16[3,528,128]{2,1,0:T(8,128)(2,1)S(1)} %pad_maximum_fusion), channel_id=1, source_target_pairs={{0,1},{1,2},{2,3},{3,4},{4,5},{5,6},{6,7},{8,9},{9,10},{10,11},{11... | collective-permute-start | bytes 1216520 | tf_op jit(solution)/shard_map/ppermute | solution.py:713
  28.0 1.9 %collective-permute-start.3 = (bf16[3,528,128]{2,1,0:T(8,128)(2,1)S(1)}, bf16[3,528,128]{2,1,0:T(8,128)(2,1)S(1)}, u32[]{:S(2)}, u32[]{:S(2)}) collective-permute-start(bf16[3,528,128]{2,1,0:T(8,128)(2,1)S(1)} %pad_maximum_fusion.1), channel_id=1, source_target_pairs={{1,0},{2,1},{3,2},{4,3},{5,4},{6,5},{7,6},{9,8},{10,9},{11,10},{12... | collective-permute-start | bytes 1216520 | tf_op jit(solution)/shard_map/ppermute | solution.py:713
  29.9 0.0 copy-start.1
  29.9 0.0 copy-start.2
  29.9 0.0 copy-start.3
  30.0 0.0 copy-start.4
  30.0 6.6 %own_splat.1.own = bf16[2,16,128,128]{3,2,1,0:T(8,128)(2,1)} custom-call(s32[256]{0:T(256)} %ids.3, bf16[32,32768]{1,0:T(8,128)(2,1)} %f_hbm.3, bf16[32768,128]{1,0:T(8,128)(2,1)} %w_hbm.5), custom_call_target="tpu_custom_call" | custom-call | flops 134217728 | bytes 6291456 | tf_op jit(solution)/shard_map/own_splat/pallas_call | solution.py:188
  36.6 0.6 collective-permute-done.3.from_yhi
  37.2 1.2 %copy-done = bf16[2,16,128,128]{3,2,1,0:T(8,128)(2,1)S(1)} copy-done((bf16[2,16,128,128]{3,2,1,0:T(8,128)(2,1)S(1)}, bf16[2,16,128,128]{3,2,1,0:T(8,128)(2,1)}, u32[]{:S(2)}) %copy-start) | copy-done | bytes 1048600
  38.4 2.2 %sum_tiles.1 = (bf16[2,16,128,128]{3,2,1,0:T(8,128)(2,1)S(1)}, bf16[4,16,128]{2,1,0:T(8,128)(2,1)S(1)}, bf16[4,16,128]{2,1,0:T(8,128)(2,1)S(1)}, s32[8,128]{1,0:T(8,128)S(1)}) custom-call(bf16[2,16,128,128]{3,2,1,0:T(8,128)(2,1)S(1)} %copy-done, bf16[3,528,128]{2,1,0:T(8,128)(2,1)S(1)} %collective-permute-done.2.from_ylo, ...), custom_call_target="tpu_custom_call" | custom-call | flops 1000 | bytes 4194304 | tf_op jit(solution)/shard_map/sum_tiles/pallas_call | solution.py:234
  40.7 3.0 %collective-permute-start.4 = (bf16[4,16,128]{2,1,0:T(8,128)(2,1)S(1)}, bf16[4,16,128]{2,1,0:T(8,128)(2,1)S(1)}, u32[]{:S(2)}, u32[]{:S(2)}) collective-permute-start(bf16[4,16,128]{2,1,0:T(8,128)(2,1)S(1)} %get-tuple-element.32), channel_id=1, source_target_pairs={{0,1},{1,2},{2,3},{3,4},{4,5},{5,6},{6,7},{8,9},{9,10},{10,11},{11... | collective-permute-start | bytes 49160 | tf_op jit(solution)/shard_map/ppermute | solution.py:713
  43.7 1.9 %collective-permute-start.5 = (bf16[4,16,128]{2,1,0:T(8,128)(2,1)S(1)}, bf16[4,16,128]{2,1,0:T(8,128)(2,1)S(1)}, u32[]{:S(2)}, u32[]{:S(2)}) collective-permute-start(bf16[4,16,128]{2,1,0:T(8,128)(2,1)S(1)} %get-tuple-element.33), channel_id=1, source_target_pairs={{1,0},{2,1},{3,2},{4,3},{5,4},{6,5},{7,6},{9,8},{10,9},{11,10},{12... | collective-permute-start | bytes 49160 | tf_op jit(solution)/shard_map/ppermute | solution.py:713
  45.7 1.5 %prepare.1 = (bf16[2304,256]{1,0:T(8,128)(2,1)S(1)}, bf16[2304,128]{1,0:T(8,128)(2,1)S(1)}, bf16[2560,256]{1,0:T(8,128)(2,1)S(1)}, bf16[1152,256]{1,0:T(8,128)(2...) custom-call(bf16[27,32,32]{2,1,0:T(8,128)(2,1)S(1)} %copy-done.5, ...), custom_call_target="tpu_custom_call" | custom-call | flops 471859200 | bytes 5242880 | tf_op jit(solution)/shard_map/prepare/pallas_call | solution.py:677
  47.3 1.5 %collective-permute-done.5.rhi = bf16[4,16,128]{2,1,0:T(8,128)(2,1)S(1)} collective-permute-done((bf16[4,16,128]{2,1,0:T(8,128)(2,1)S(1)}, bf16[4,16,128]{2,1,0:T(8,128)(2,1)S(1)}, u32[]{:S(2)}, u32[]{:S(2)}) %collective-permute-start.5) | collective-permute-done | bytes 16416 | tf_op jit(solution)/shard_map/ppermute | solution.py:713
  48.8 0.8 widen_y.1
  49.6 3.0 %collective-permute-start.6 = (bf16[8,144,128]{2,1,0:T(8,128)(2,1)S(1)}, bf16[8,144,128]{2,1,0:T(8,128)(2,1)S(1)}, u32[]{:S(2)}, u32[]{:S(2)}) collective-permute-start(bf16[8,144,128]{2,1,0:T(8,128)(2,1)S(1)} %get-tuple-element.35), channel_id=1, source_target_pairs={{0,8},{8,16},{16,24},{24,32},{32,40},{40,48},{48,56},{56,64},{64,7... | collective-permute-start | bytes 884744 | tf_op jit(solution)/shard_map/ppermute | solution.py:713
  52.6 5.2 %collective-permute-start.7 = (bf16[8,144,128]{2,1,0:T(8,128)(2,1)S(1)}, bf16[8,144,128]{2,1,0:T(8,128)(2,1)S(1)}, u32[]{:S(2)}, u32[]{:S(2)}) collective-permute-start(bf16[8,144,128]{2,1,0:T(8,128)(2,1)S(1)} %get-tuple-element.36), channel_id=1, source_target_pairs={{8,0},{16,8},{24,16},{32,24},{40,32},{48,40},{56,48},{64,56},{72,6... | collective-permute-start | bytes 884744 | tf_op jit(solution)/shard_map/ppermute | solution.py:713
  57.8 8.2 %inner_convs.1.part = f32[16,128,256]{2,1,0:T(8,128)S(1)} custom-call(bf16[2,16,144,128]{3,2,1,0:T(8,128)(2,1)S(1)} %get-tuple-element.34.x, bf16[2,16,128,128]{3,2,1,0:T(8,128)(2,1)S(1)} %get-tuple-element.31.g, bf16[2304,256]{1,0:T(8,128)(2,1)S(1)} %get-tuple-element.37.t1, f32[1,256]{1,0:T(1,128)S(1)} %get-tuple-element.38.b1, ...), custom_call_target="tpu_custom_call" | custom-call | flops 6039797760 | bytes 6291456 | tf_op jit(solution)/shard_map/inner_convs/pallas_call | solution.py:350
  66.0 10.5 %edge_convs.1 = (bf16[32,16,8,128]{3,2,1,0:T(8,128)(2,1)}, f32[128,8,128]{2,1,0:T(8,128)S(1)}, bf16[3,64,128]{2,1,0:T(8,128)(2,1)S(1)}, bf16[3,64,128]{2,1,0:T(8,128)(2,1)S(1)}, bf16[2,64,128]{2,1,0:T(8,128)(2,1)S(1)}) custom-call(bf16[2,16,144,128]{3,2,1,0:T(8,128)(2,1)S(1)} %get-tuple-element.34.x, bf16[8,144,128]{2,1,0:T(8,128)(2,1)S(1)} %collective-permute-done.6.rlo, ...), custom_call_target="tpu_custom_call" | custom-call | flops 2717908992 | bytes 6291456 | tf_op jit(solution)/shard_map/edge_convs/pallas_call | solution.py:478
  76.5 2.4 %collective-permute-start.8 = (bf16[3,64,128]{2,1,0:T(8,128)(2,1)S(1)}, bf16[3,64,128]{2,1,0:T(8,128)(2,1)S(1)}, u32[]{:S(2)}, u32[]{:S(2)}) collective-permute-start(bf16[3,64,128]{2,1,0:T(8,128)(2,1)S(1)} %get-tuple-element.48), channel_id=1, source_target_pairs={{0,1},{1,2},{2,3},{3,4},{4,5},{5,6},{6,7},{8,9},{9,10},{10,11},{11... | collective-permute-start | bytes 147464 | tf_op jit(solution)/shard_map/ppermute | solution.py:713
  78.9 1.9 %collective-permute-start.9 = (bf16[3,64,128]{2,1,0:T(8,128)(2,1)S(1)}, bf16[3,64,128]{2,1,0:T(8,128)(2,1)S(1)}, u32[]{:S(2)}, u32[]{:S(2)}) collective-permute-start(bf16[3,64,128]{2,1,0:T(8,128)(2,1)S(1)} %get-tuple-element.50), channel_id=1, source_target_pairs={{1,0},{2,1},{3,2},{4,3},{5,4},{6,5},{7,6},{9,8},{10,9},{11,10},{12... | collective-permute-start | bytes 147464 | tf_op jit(solution)/shard_map/ppermute | solution.py:713
  80.8 3.5 %collective-permute-done.9.yhi = bf16[3,64,128]{2,1,0:T(8,128)(2,1)S(1)} collective-permute-done((bf16[3,64,128]{2,1,0:T(8,128)(2,1)S(1)}, bf16[3,64,128]{2,1,0:T(8,128)(2,1)S(1)}, u32[]{:S(2)}, u32[]{:S(2)}) %collective-permute-start.9) | collective-permute-done | bytes 49184 | tf_op jit(solution)/shard_map/ppermute | solution.py:713
  84.3 1.9 %collective-permute-start.10 = (bf16[3,64,128]{2,1,0:T(8,128)(2,1)S(1)}, bf16[3,64,128]{2,1,0:T(8,128)(2,1)S(1)}, u32[]{:S(2)}, u32[]{:S(2)}) collective-permute-start(bf16[3,64,128]{2,1,0:T(8,128)(2,1)S(1)} %pad_maximum_fusion.2), channel_id=1, source_target_pairs={{0,8},{8,16},{16,24},{24,32},{32,40},{40,48},{48,56},{56,64},{64,7... | collective-permute-start | bytes 147464 | tf_op jit(solution)/shard_map/ppermute | solution.py:713
  86.3 5.5 %collective-permute-start.11 = (bf16[3,64,128]{2,1,0:T(8,128)(2,1)S(1)}, bf16[3,64,128]{2,1,0:T(8,128)(2,1)S(1)}, u32[]{:S(2)}, u32[]{:S(2)}) collective-permute-start(bf16[3,64,128]{2,1,0:T(8,128)(2,1)S(1)} %pad_maximum_fusion.3), channel_id=1, source_target_pairs={{8,0},{16,8},{24,16},{32,24},{40,32},{48,40},{56,48},{64,56},{72,6... | collective-permute-start | bytes 147464 | tf_op jit(solution)/shard_map/ppermute | solution.py:713
  91.8 4.3 %own_read.1 = (f32[3,16384]{1,0:T(4,128)S(1)}, bf16[16384,128]{1,0:T(8,128)(2,1)S(1)}) custom-call(s32[256]{0:T(256)S(1)} %copy-done.7, f32[128,8,128]{2,1,0:T(8,128)S(1)} %get-tuple-element.51.table, bf16[32768,128]{1,0:T(8,128)(2,1)} %w_hbm.5), custom_call_target="tpu_custom_call" | custom-call | flops 134217728 | bytes 9437184 | tf_op jit(solution)/shard_map/own_read/pallas_call | solution.py:556
  96.1 2.8 %far_read.1 = f32[3,32768]{1,0:T(4,128)} custom-call(s32[128]{0:T(128)S(1)} %copy-done.11, s32[1]{0:T(128)S(6)} %copy.16.counts_h.counts, bf16[3,64,128]{2,1,0:T(8,128)(2,1)S(1)} %collective-permute-done.10.blo, bf16[3,64,128]{2,1,0:T(8,128)(2,1)S(1)} %collective-permute-done.11.bhi, bf16[3,64,128]{2,1,0:T(8,128)(2,1)S(1)} %collective-permute-done.8.ylo, ...), custom_call_target="tpu_custom_call" | custom-call | flops 134217728 | bytes 5242880 | tf_op jit(solution)/shard_map/far_read/pallas_call | solution.py:602
  (35 shorter events, 0.2 us)
Async XLA Ops:
  7.1 14.5 %collective-permute-start = (bf16[3,528,128]{2,1,0:T(8,128)(2,1)}, bf16[3,528,128]{2,1,0:T(8,128)(2,1)S(1)}, u32[]{:S(2)}, u32[]{:S(2)}) collective-permute-start(bf16[3,528,128]{2,1,0:T(8,128)(2,1)} %get-tuple-element.28), channel_id=1, source_target_pairs={{0,8},{8,16},{16,24},{24,32},{32,40},{40,48},{48,56},{56,64},{64,7... | collective-permute-start | bytes 1216520 | tf_op jit(solution)/shard_map/ppermute | solution.py:713
  10.4 12.2 %collective-permute-start.1 = (bf16[3,528,128]{2,1,0:T(8,128)(2,1)}, bf16[3,528,128]{2,1,0:T(8,128)(2,1)S(1)}, u32[]{:S(2)}, u32[]{:S(2)}) collective-permute-start(bf16[3,528,128]{2,1,0:T(8,128)(2,1)} %get-tuple-element.30), channel_id=1, source_target_pairs={{8,0},{16,8},{24,16},{32,24},{40,32},{48,40},{56,48},{64,56},{72,6... | collective-permute-start | bytes 1216520 | tf_op jit(solution)/shard_map/ppermute | solution.py:713
  22.7 14.0 %collective-permute-start.2 = (bf16[3,528,128]{2,1,0:T(8,128)(2,1)S(1)}, bf16[3,528,128]{2,1,0:T(8,128)(2,1)S(1)}, u32[]{:S(2)}, u32[]{:S(2)}) collective-permute-start(bf16[3,528,128]{2,1,0:T(8,128)(2,1)S(1)} %pad_maximum_fusion), channel_id=1, source_target_pairs={{0,1},{1,2},{2,3},{3,4},{4,5},{5,6},{6,7},{8,9},{9,10},{10,11},{11... | collective-permute-start | bytes 1216520 | tf_op jit(solution)/shard_map/ppermute | solution.py:713
  28.0 9.2 %collective-permute-start.3 = (bf16[3,528,128]{2,1,0:T(8,128)(2,1)S(1)}, bf16[3,528,128]{2,1,0:T(8,128)(2,1)S(1)}, u32[]{:S(2)}, u32[]{:S(2)}) collective-permute-start(bf16[3,528,128]{2,1,0:T(8,128)(2,1)S(1)} %pad_maximum_fusion.1), channel_id=1, source_target_pairs={{1,0},{2,1},{3,2},{4,3},{5,4},{6,5},{7,6},{9,8},{10,9},{11,10},{12... | collective-permute-start | bytes 1216520 | tf_op jit(solution)/shard_map/ppermute | solution.py:713
  29.9 15.7 %copy-start.1 = (bf16[128,2048]{1,0:T(8,128)(2,1)S(1)}, bf16[128,2048]{1,0:T(8,128)(2,1)}, u32[]{:S(2)}) copy-start(bf16[128,2048]{1,0:T(8,128)(2,1)} %constant.10.clone.e2a) | copy-start | bytes 1572868
  29.9 15.7 %copy-start.2 = (bf16[128,2048]{1,0:T(8,128)(2,1)S(1)}, bf16[128,2048]{1,0:T(8,128)(2,1)}, u32[]{:S(2)}) copy-start(bf16[128,2048]{1,0:T(8,128)(2,1)} %constant.8.clone.e1a) | copy-start | bytes 1572868
  29.9 15.7 %copy-start.3 = (bf16[128,1024]{1,0:T(8,128)(2,1)S(1)}, bf16[128,1024]{1,0:T(8,128)(2,1)}, u32[]{:S(2)}) copy-start(bf16[128,1024]{1,0:T(8,128)(2,1)} %constant.11.clone.e2b) | copy-start | bytes 786436
  30.0 15.7 %copy-start.4 = (bf16[128,1024]{1,0:T(8,128)(2,1)S(1)}, bf16[128,1024]{1,0:T(8,128)(2,1)}, u32[]{:S(2)}) copy-start(bf16[128,1024]{1,0:T(8,128)(2,1)} %constant.9.clone.e1b) | copy-start | bytes 786436
  30.0 15.7 %copy-start.5 = (bf16[27,32,32]{2,1,0:T(8,128)(2,1)S(1)}, bf16[27,32,32]{2,1,0:T(8,128)(2,1)}, u32[]{:S(2)}) copy-start(bf16[27,32,32]{2,1,0:T(8,128)(2,1)} %c1.1) | copy-start | bytes 165892
  30.0 15.7 %copy-start.6 = (bf16[27,32,32]{2,1,0:T(8,128)(2,1)S(1)}, bf16[27,32,32]{2,1,0:T(8,128)(2,1)}, u32[]{:S(2)}) copy-start(bf16[27,32,32]{2,1,0:T(8,128)(2,1)} %c2.1) | copy-start | bytes 165892
  30.0 15.7 %copy-start.8 = (bf16[3,32]{1,0:T(4,128)(2,1)S(1)}, bf16[3,32]{1,0:T(4,128)(2,1)}, u32[]{:S(2)}) copy-start(bf16[3,32]{1,0:T(4,128)(2,1)} %head.1) | copy-start | bytes 580
  30.0 15.7 %copy-start.9 = (f32[32]{0:T(128)S(1)}, f32[32]{0:T(128)}, u32[]{:S(2)}) copy-start(f32[32]{0:T(128)} %param.20) | copy-start | bytes 388
  30.0 15.7 %copy-start.10 = (f32[32]{0:T(128)S(1)}, f32[32]{0:T(128)}, u32[]{:S(2)}) copy-start(f32[32]{0:T(128)} %param.22) | copy-start | bytes 388
  37.2 1.2 %copy-start = (bf16[2,16,128,128]{3,2,1,0:T(8,128)(2,1)S(1)}, bf16[2,16,128,128]{3,2,1,0:T(8,128)(2,1)}, u32[]{:S(2)}) copy-start(bf16[2,16,128,128]{3,2,1,0:T(8,128)(2,1)} %own_splat.1.own) | copy-start | bytes 3145732
  40.7 6.6 %collective-permute-start.4 = (bf16[4,16,128]{2,1,0:T(8,128)(2,1)S(1)}, bf16[4,16,128]{2,1,0:T(8,128)(2,1)S(1)}, u32[]{:S(2)}, u32[]{:S(2)}) collective-permute-start(bf16[4,16,128]{2,1,0:T(8,128)(2,1)S(1)} %get-tuple-element.32), channel_id=1, source_target_pairs={{0,1},{1,2},{2,3},{3,4},{4,5},{5,6},{6,7},{8,9},{9,10},{10,11},{11... | collective-permute-start | bytes 49160 | tf_op jit(solution)/shard_map/ppermute | solution.py:713
  43.7 5.1 %collective-permute-start.5 = (bf16[4,16,128]{2,1,0:T(8,128)(2,1)S(1)}, bf16[4,16,128]{2,1,0:T(8,128)(2,1)S(1)}, u32[]{:S(2)}, u32[]{:S(2)}) collective-permute-start(bf16[4,16,128]{2,1,0:T(8,128)(2,1)S(1)} %get-tuple-element.33), channel_id=1, source_target_pairs={{1,0},{2,1},{3,2},{4,3},{5,4},{6,5},{7,6},{9,8},{10,9},{11,10},{12... | collective-permute-start | bytes 49160 | tf_op jit(solution)/shard_map/ppermute | solution.py:713
  49.6 16.4 %collective-permute-start.6 = (bf16[8,144,128]{2,1,0:T(8,128)(2,1)S(1)}, bf16[8,144,128]{2,1,0:T(8,128)(2,1)S(1)}, u32[]{:S(2)}, u32[]{:S(2)}) collective-permute-start(bf16[8,144,128]{2,1,0:T(8,128)(2,1)S(1)} %get-tuple-element.35), channel_id=1, source_target_pairs={{0,8},{8,16},{16,24},{24,32},{32,40},{40,48},{48,56},{56,64},{64,7... | collective-permute-start | bytes 884744 | tf_op jit(solution)/shard_map/ppermute | solution.py:713
  52.6 13.4 %collective-permute-start.7 = (bf16[8,144,128]{2,1,0:T(8,128)(2,1)S(1)}, bf16[8,144,128]{2,1,0:T(8,128)(2,1)S(1)}, u32[]{:S(2)}, u32[]{:S(2)}) collective-permute-start(bf16[8,144,128]{2,1,0:T(8,128)(2,1)S(1)} %get-tuple-element.36), channel_id=1, source_target_pairs={{8,0},{16,8},{24,16},{32,24},{40,32},{48,40},{56,48},{64,56},{72,6... | collective-permute-start | bytes 884744 | tf_op jit(solution)/shard_map/ppermute | solution.py:713
  66.0 25.8 %copy-start.7 = (s32[256]{0:T(256)S(1)}, s32[256]{0:T(256)}, u32[]{:S(2)}) copy-start(s32[256]{0:T(256)} %ids.3) | copy-start | bytes 3076
  76.5 4.4 %collective-permute-start.8 = (bf16[3,64,128]{2,1,0:T(8,128)(2,1)S(1)}, bf16[3,64,128]{2,1,0:T(8,128)(2,1)S(1)}, u32[]{:S(2)}, u32[]{:S(2)}) collective-permute-start(bf16[3,64,128]{2,1,0:T(8,128)(2,1)S(1)} %get-tuple-element.48), channel_id=1, source_target_pairs={{0,1},{1,2},{2,3},{3,4},{4,5},{5,6},{6,7},{8,9},{9,10},{10,11},{11... | collective-permute-start | bytes 147464 | tf_op jit(solution)/shard_map/ppermute | solution.py:713
  78.9 5.4 %collective-permute-start.9 = (bf16[3,64,128]{2,1,0:T(8,128)(2,1)S(1)}, bf16[3,64,128]{2,1,0:T(8,128)(2,1)S(1)}, u32[]{:S(2)}, u32[]{:S(2)}) collective-permute-start(bf16[3,64,128]{2,1,0:T(8,128)(2,1)S(1)} %get-tuple-element.50), channel_id=1, source_target_pairs={{1,0},{2,1},{3,2},{4,3},{5,4},{6,5},{7,6},{9,8},{10,9},{11,10},{12... | collective-permute-start | bytes 147464 | tf_op jit(solution)/shard_map/ppermute | solution.py:713
  84.3 11.7 %collective-permute-start.10 = (bf16[3,64,128]{2,1,0:T(8,128)(2,1)S(1)}, bf16[3,64,128]{2,1,0:T(8,128)(2,1)S(1)}, u32[]{:S(2)}, u32[]{:S(2)}) collective-permute-start(bf16[3,64,128]{2,1,0:T(8,128)(2,1)S(1)} %pad_maximum_fusion.2), channel_id=1, source_target_pairs={{0,8},{8,16},{16,24},{24,32},{32,40},{40,48},{48,56},{56,64},{64,7... | collective-permute-start | bytes 147464 | tf_op jit(solution)/shard_map/ppermute | solution.py:713
  86.3 9.8 %collective-permute-start.11 = (bf16[3,64,128]{2,1,0:T(8,128)(2,1)S(1)}, bf16[3,64,128]{2,1,0:T(8,128)(2,1)S(1)}, u32[]{:S(2)}, u32[]{:S(2)}) collective-permute-start(bf16[3,64,128]{2,1,0:T(8,128)(2,1)S(1)} %pad_maximum_fusion.3), channel_id=1, source_target_pairs={{8,0},{16,8},{24,16},{32,24},{40,32},{48,40},{56,48},{64,56},{72,6... | collective-permute-start | bytes 147464 | tf_op jit(solution)/shard_map/ppermute | solution.py:713
  91.8 4.3 %copy-start.11 = (s32[128]{0:T(128)S(1)}, s32[128]{0:T(128)}, u32[]{:S(2)}) copy-start(s32[128]{0:T(128)} %get-tuple-element.47.slots) | copy-start | bytes 1540

commit v2 on v1

--- a/solution.py
+++ b/solution.py
@@ -301,65 +301,74 @@
     return (pltpu.roll(v, 1, 1), v, pltpu.roll(v, ROWS - 1, 1))
 
 
-def inner_kernel(x, g, t1, b1, t2, b2, part, xs, hs):
+PAIRS = SLAB // 2
+
+
+def window(ref, n, k):
+    m = n * 4 + k // 2
+    out = []
+    for dy in range(3):
+        v = ref[dy, m : m + 4, k % 2]
+        out.append(v.reshape(4 * v.shape[1], v.shape[2]))
+    return out
+
+
+def inner_kernel(x, g, t1, t1o, b1, t2, b2, part, pre, xs, hs):
     iy = lax.axis_index("gy")
     for dy in range(3):
-        xs[dy, 0] = jnp.zeros((ROWS, 256), BF16)
-        xs[dy, SLAB + 1] = jnp.zeros((ROWS, 256), BF16)
-        hs[dy, 0] = jnp.zeros((BY, 256), BF16)
-        hs[dy, SLAB + 1] = jnp.zeros((BY, 256), BF16)
-
-    def shift(z, carry):
-        for tx in range(2):
-            v = x[tx, pl.ds(z, 1)].astype(F32)
-            for dy, s in enumerate(shifted(v)):
-                xs[dy, pl.ds(z + 1, 1), :, tx * 128 : tx * 128 + 128] = s.astype(BF16)
+        xs[dy, 0, 0] = jnp.zeros((ROWS, 256), BF16)
+        xs[dy, PAIRS, 1] = jnp.zeros((ROWS, 256), BF16)
+        hs[dy, 0, 0] = jnp.zeros((BY, 256), BF16)
+        hs[dy, PAIRS, 1] = jnp.zeros((BY, 256), BF16)
+
+    def shift(n, carry):
+        for k in range(2):
+            for tx in range(2):
+                v = x[tx, pl.ds(2 * n + k, 1)].astype(F32)
+                for dy, s in enumerate(shifted(v)):
+                    xs[dy, pl.ds(n + k, 1), 1 - k, :, tx * 128 : tx * 128 + 128] = s.astype(BF16)
         return carry
 
-    lax.fori_loop(0, SLAB, shift, 0)
-
-    def first(n, carry):
-        taps = [
-            xs[dy, pl.ds(n * 4 + dz, 4)].reshape(4 * ROWS, 256)
-            for dz in range(3)
-            for dy in range(3)
-        ]
-        acc = jnp.dot(jnp.concatenate(taps, 1), t1[...], preferred_element_type=F32) + b1[...]
-        h = jax.nn.gelu(acc).reshape(4, ROWS, 256)
-        h = jnp.where(rows_inside(h.shape, iy), h, 0.0)
-        for dy, s in enumerate(shifted(h)):
-            hs[dy, pl.ds(n * 4 + 1, 4)] = s[:, 8 : 8 + BY].astype(BF16)
-        return carry
-
-    lax.fori_loop(0, 4, first, 0)
-
-    def second(n, carry):
-        taps = [
-            hs[dy, pl.ds(n * 4 + dz, 4)].reshape(4 * BY, 256) for dz in range(3) for dy in range(3)
-        ]
-        taps += [g[tx, pl.ds(n * 4, 4)].reshape(4 * BY, 128) for tx in range(2)]
-        acc = jnp.dot(jnp.concatenate(taps, 1), t2[...], preferred_element_type=F32) + b2[...]
-        part[pl.ds(n * 4, 4)] = acc.reshape(4, BY, 256)
-        return carry
-
-    lax.fori_loop(0, 4, second, 0)
-
-
-def inner_convs(x, g, t1, b1, t2, b2):
+    lax.fori_loop(0, PAIRS, shift, 0)
+    for n in range(2):
+        for zo in range(2):
+            taps = window(xs, n, zo) + window(xs, n, zo + 1) + window(xs, n, zo + 2)
+            acc = jnp.dot(jnp.concatenate(taps, 1), t1[...], preferred_element_type=F32) + b1[...]
+            h = jax.nn.gelu(acc).reshape(4, ROWS, 256)
+            h = jnp.where(rows_inside(h.shape, iy), h, 0.0)
+            for dy, s in enumerate(shifted(h)):
+                m = n * 4 + zo
+                hs[dy, m : m + 4, 1 - zo] = s[:, 8 : 8 + BY].astype(BF16)
+    for n in range(2):
+        taps = sum([window(xs, n, zi) for zi in range(4)], [])
+        acc = jnp.dot(jnp.concatenate(taps, 1), t1o[...], preferred_element_type=F32) + b1[...]
+        pre[n] = acc
+    for n in range(2):
+        for zo in range(2):
+            taps = window(hs, n, zo) + window(hs, n, zo + 1) + window(hs, n, zo + 2)
+            taps += [g[tx, n * 4 : n * 4 + 4, zo].reshape(4 * BY, 128) for tx in range(2)]
+            acc = jnp.dot(jnp.concatenate(taps, 1), t2[...], preferred_element_type=F32) + b2[...]
+            part[n * 4 : n * 4 + 4, zo] = acc.reshape(4, BY, 256)
+
+
+def inner_convs(x, g, t1, t1o, b1, t2, b2):
     vm = pl.BlockSpec(memory_space=VMEM)
     return pl.pallas_call(
         inner_kernel,
-        in_specs=[vm] * 6,
-        out_specs=vm,
-        out_shape=jax.ShapeDtypeStruct((SLAB, BY, 256), F32),
+        in_specs=[vm] * 7,
+        out_specs=[vm, vm],
+        out_shape=[
+            jax.ShapeDtypeStruct((PAIRS, 2, BY, 256), F32),
+            jax.ShapeDtypeStruct((2, 4 * ROWS, 256), F32),
+        ],
         scratch_shapes=[
-            VMEM((3, SLAB + 2, ROWS, 256), BF16),
-            VMEM((3, SLAB + 2, BY, 256), BF16),
+            VMEM((3, PAIRS + 1, 2, ROWS, 256), BF16),
+            VMEM((3, PAIRS + 1, 2, BY, 256), BF16),
         ],
         compiler_params=params(32),
         cost_estimate=cost(2 * 20 * 256 * 256 * 2304, 6 * MIB),
         name="inner_convs",
-    )(x, g, t1, b1, t2, b2)
+    )(x, g.reshape(2, PAIRS, 2, BY, 128), t1, t1o, b1, t2, b2)
 
 
 def tile_row(tile):
@@ -367,68 +376,49 @@
 
 
 def edge_kernel(
-    x, rlo, rhi, part, t1, b1, t2, headx, ids, out, table, ans_ylo, ans_yhi, ans_x, es, hs, vel
+    rlo, rhi, part, pre, t1, t2, headx, ids, total, table, ans_ylo, ans_yhi, ans_x, es, hs, vel
 ):
     ix = lax.axis_index("gx")
     iy = lax.axis_index("gy")
     for dy in range(3):
-        es[dy, 0] = jnp.zeros((ROWS, 256), BF16)
-        es[dy, SLAB + 1] = jnp.zeros((ROWS, 256), BF16)
-        hs[dy, 0] = jnp.zeros((BY, 128), BF16)
-        hs[dy, SLAB + 1] = jnp.zeros((BY, 128), BF16)
+        es[dy, 0, 0] = jnp.zeros((ROWS, 128), BF16)
+        es[dy, PAIRS, 1] = jnp.zeros((ROWS, 128), BF16)
+        hs[dy, 0, 0] = jnp.zeros((BY, 128), BF16)
+        hs[dy, PAIRS, 1] = jnp.zeros((BY, 128), BF16)
     lane = lanes_of((1, ROWS, 128))
-
-    def put(z, low, high):
-        for k, v in enumerate((low, high)):
+    for z in range(8):
+        a = rlo[z : z + 1].astype(F32)
+        b = rhi[z : z + 1].astype(F32)
+        near = jnp.where(lane < 64, a, pltpu.roll(b, 64, 2))
+        far = jnp.where(lane < 64, pltpu.roll(a, 64, 2), b)
+        for zz, v in ((z, near), (z + 8, far)):
+            m = (zz + 1) // 2
             for dy, s in enumerate(shifted(v)):
-                es[dy, pl.ds(z + 1, 1), :, k * 128 : k * 128 + 128] = s.astype(BF16)
-
-    def shift(z, carry):
-        a = rlo[pl.ds(z, 1)].astype(F32)
-        b = rhi[pl.ds(z, 1)].astype(F32)
-        for half in range(2):
-            zz = z + 8 * half
-            own0 = x[0, pl.ds(zz, 1)].astype(F32)
-            own1 = x[1, pl.ds(zz, 1)].astype(F32)
-            left = pltpu.roll(a, 64, 2) if half == 0 else a
-            right = b if half == 0 else pltpu.roll(b, 64, 2)
-            put(zz, jnp.where(lane < 64, own0, left), jnp.where(lane < 64, right, own1))
-        return carry
-
-    lax.fori_loop(0, 8, shift, 0)
-
-    def first(n, carry):
-        taps = [
-            es[dy, pl.ds(n * 4 + dz, 4)].reshape(4 * ROWS, 256)
-            for dz in range(3)
-            for dy in range(3)
-        ]
-        acc = jnp.dot(jnp.concatenate(taps, 1), t1[...], preferred_element_type=F32) + b1[...]
-        h = jax.nn.gelu(acc).reshape(4, ROWS, 128)
-        ln = lanes_of(h.shape)
+                es[dy, m : m + 1, (zz + 1) % 2] = s.astype(BF16)
+    for n in range(2):
+        taps = sum([window(es, n, zi) for zi in range(4)], [])
+        acc = jnp.dot(jnp.concatenate(taps, 1), t1[...], preferred_element_type=F32) + pre[n]
+        h = jax.nn.gelu(acc).reshape(4, ROWS, 256)
+        ln = lanes_of(h.shape) & 127
         keep = ((ln >= 32) | (ix > 0)) & ((ln < 96) | (ix < 15))
         h = jnp.where(rows_inside(h.shape, iy) & keep, h, 0.0)
         for dy, s in enumerate(shifted(h)):
-            hs[dy, pl.ds(n * 4 + 1, 4)] = s[:, 8 : 8 + BY].astype(BF16)
-        return carry
-
-    lax.fori_loop(0, 4, first, 0)
-
-    def second(n, carry):
-        taps = [
-            hs[dy, pl.ds(n * 4 + dz, 4)].reshape(4 * BY, 128) for dz in range(3) for dy in range(3)
-        ]
-        acc = jnp.dot(jnp.concatenate(taps, 1), t2[...], preferred_element_type=F32)
-        for k in range(4):
-            z = n * 4 + k
-            total = (acc[k * BY : (k + 1) * BY] + part[z]).T.astype(BF16)
-            out[:, pl.ds(z, 1)] = total.reshape(32, 1, 8, 128)
-            v = jnp.dot(headx[...], total, preferred_element_type=F32)
-            for a in range(3):
-                vel[a, pl.ds(z, 1)] = v[8 * a : 8 * a + 8].reshape(1, 8, 128)
-        return carry
-
-    lax.fori_loop(0, 4, second, 0)
+            s = s[:, 8 : 8 + BY].astype(BF16)
+            hs[dy, n * 4 : n * 4 + 4, 1] = s[:, :, 0:128]
+            hs[dy, n * 4 + 1 : n * 4 + 5, 0] = s[:, :, 128:256]
+    for n in range(2):
+        for zo in range(2):
+            taps = window(hs, n, zo) + window(hs, n, zo + 1) + window(hs, n, zo + 2)
+            acc = jnp.dot(jnp.concatenate(taps, 1), t2[...], preferred_element_type=F32)
+            acc = acc.reshape(4, BY, 256) + part[n * 4 : n * 4 + 4, zo]
+            acc = acc.astype(BF16)
+            total[n * 4 : n * 4 + 4, zo] = acc
+            v = jnp.concatenate([acc[p] for p in range(4)], 1)
+            v = jnp.dot(v, headx[...], preferred_element_type=F32).T
+            for p in range(4):
+                for a in range(3):
+                    at = p * 32 + a * 8
+                    vel[a, 2 * (n * 4 + p) + zo] = v[at : at + 8]
 
     table[...] = jnp.zeros_like(table)
     sub = lax.broadcasted_iota(jnp.int32, (4, 8, 128), 1)
@@ -469,32 +459,50 @@
             )
             return carry
 
-        lax.fori_loop(0, SLOTS // 4, answer, 0, unroll=2)
-
-
-def edge_convs(x, rlo, rhi, part, t1, b1, t2, headx, ids):
+        lax.fori_loop(0, SLOTS // 4, answer, 0, unroll=4)
+
+
+def edge_convs(rlo, rhi, part, pre, t1, t2, headx, ids):
     vm = pl.BlockSpec(memory_space=VMEM)
     ans = jax.ShapeDtypeStruct((3, 64, 128), BF16)
     return pl.pallas_call(
         edge_kernel,
-        in_specs=[vm] * 8 + [pl.BlockSpec(memory_space=SMEM)],
+        in_specs=[vm] * 7 + [pl.BlockSpec(memory_space=SMEM)],
         out_specs=[vm] * 5,
         out_shape=[
-            jax.ShapeDtypeStruct((C, SLAB, 8, BY), BF16),
+            jax.ShapeDtypeStruct((SLAB // 2, 2, BY, 256), BF16),
             jax.ShapeDtypeStruct((128, 8, 128), F32),
             ans,
             ans,
             jax.ShapeDtypeStruct((2, 64, 128), BF16),
         ],
         scratch_shapes=[
-            VMEM((3, SLAB + 2, ROWS, 256), BF16),
-            VMEM((3, SLAB + 2, BY, 128), BF16),
+            VMEM((3, PAIRS + 1, 2, ROWS, 128), BF16),
+            VMEM((3, PAIRS + 1, 2, BY, 128), BF16),
             VMEM((3, SLAB, 8, 128), F32),
         ],
         compiler_params=params(32),
         cost_estimate=cost(2 * 9 * 256 * 256 * 2304, 6 * MIB),
         name="edge_convs",
-    )(x, rlo, rhi, part, t1, b1, t2, headx, ids)
+    )(rlo, rhi, part, pre, t1, t2, headx, ids)
+
+
+def turn_kernel(total, out):
+    for k in range(4):
+        out[:, k] = total[k // 2, k % 2].T.reshape(32, 8, 128)
+
+
+def turn(total):
+    return pl.pallas_call(
+        turn_kernel,
+        grid=(4,),
+        in_specs=[pl.BlockSpec((2, 2, BY, 256), lambda i: (i, 0, 0, 0))],
+        out_specs=pl.BlockSpec((C, 4, 8, BY), lambda i: (0, i, 0, 0)),
+        out_shape=jax.ShapeDtypeStruct((C, SLAB, 8, BY), BF16),
+        compiler_params=params(8, True),
+        cost_estimate=cost(1000, 8 * MIB),
+        name="turn",
+    )(total)
 
 
 BATCH = 32
@@ -623,13 +631,21 @@
 
 
 def prepare_kernel(
-    c1, c2, bias1, bias2, head, e1a, e1b, e2a, e2b, t1a, t1b, t2a, t2b, hx, b1a, b1b, b2
+    c1, c2, bias1, bias2, head, e1a, e1o, e1r, e2a, e2b, t1a, t1o, t1r, t2a, t2b, hx, b1, b2
 ):
     one = (
         lax.broadcasted_iota(jnp.int32, (C, C), 0) == lax.broadcasted_iota(jnp.int32, (C, C), 1)
     ).astype(BF16)
     nothing = jnp.zeros((C, C), BF16)
-    for conv, made in ((c1, ((e1a, t1a, 256), (e1b, t1b, 128))), (c2, ((e2a, t2a, 256), (e2b, t2b, 256)))):
+    for t in (t1o, t1r):
+        third = t.shape[0] // 4
+        t[0:third, 128:256] = jnp.zeros((third, 128), BF16)
+        t[3 * third : 4 * third, 0:128] = jnp.zeros((third, 128), BF16)
+    plans = (
+        (c1, ((e1a, t1a, 256), (e1o, t1o, 128), (e1r, t1r, 128))),
+        (c2, ((e2a, t2a, 256), (e2b, t2b, 256))),
+    )
+    for conv, made in plans:
         pieces = []
         for k in range(9):
             pieces += [conv[k // 3 * 9 + d * 3 + k % 3] for d in range(3)] + [nothing]
@@ -643,8 +659,14 @@
                 r = jnp.dot(lhs, e[:, p * width : (p + 1) * width], preferred_element_type=F32)
                 r = r.astype(BF16)
                 for k in range(9):
+                    block = r[C * k : C * k + C]
                     at = (k * planes + p) * C
-                    t[at : at + C, :] = r[C * k : C * k + C]
+                    if width == 256:
+                        t[at : at + C, :] = block
+                        continue
+                    for zo in range(2):
+                        down = at + zo * 3 * planes * C
+                        t[down : down + C, zo * 128 : zo * 128 + 128] = block
     row = lax.broadcasted_iota(jnp.int32, (256, 256), 0)
     col = lanes_of((256, 256))
     t2a[2304:2560, :] = ((row & 31) == (col >> 3)).astype(F32).astype(BF16) * (
@@ -656,10 +678,12 @@
     wide = jnp.dot(head[...], spread.astype(BF16), preferred_element_type=F32)
     keep = (lanes_of((8, 256)) & 7) == lax.broadcasted_iota(jnp.int32, (8, 256), 0)
     parts = [jnp.where(keep, jnp.broadcast_to(wide[a : a + 1], (8, 256)), 0.0) for a in range(3)]
-    hx[...] = jnp.concatenate(parts + [jnp.zeros((8, 256), F32)], 0).astype(BF16)
-    b1 = jnp.concatenate([bias1[...]] * 8, 1)
-    b1a[...] = b1
-    b1b[...] = b1[:, 0:128]
+    one_z = jnp.concatenate(parts + [jnp.zeros((8, 256), F32)], 0)
+    turned = jnp.concatenate([one_z] * 4, 0).T
+    group = lanes_of((256, 128)) >> 5
+    for p in range(4):
+        hx[p * 256 : p * 256 + 256, :] = jnp.where(group == p, turned, 0.0).astype(BF16)
+    b1[...] = jnp.concatenate([bias1[...]] * 8, 1)
     b2[...] = jnp.dot(
         bias2[...], spread, preferred_element_type=F32, precision=lax.Precision.HIGHEST
     )
@@ -670,28 +694,29 @@
     inner = [none, 1, 2, 3, 4, 5, 6, none]
     every = list(range(8))
     e1a = band(every, inner, False)
-    e1b = band([0, 1, -2, -1, 8, 9, 6, 7], [-1, 0, 7, 8], False)
+    e1o = band(every, [-1, 0, 7, 8], False)
+    e1r = band([-2, -1, 8, 9], [-1, 0, 7, 8], False)
     e2a = band(inner, every, True)
     e2b = band([-1, 0, 7, 8], every, True)
     vm = pl.BlockSpec(memory_space=VMEM)
     return pl.pallas_call(
         prepare_kernel,
-        in_specs=[vm] * 9,
+        in_specs=[vm] * 10,
         out_specs=[vm] * 8,
         out_shape=[
             jax.ShapeDtypeStruct((2304, 256), BF16),
-            jax.ShapeDtypeStruct((2304, 128), BF16),
+            jax.ShapeDtypeStruct((3072, 256), BF16),
+            jax.ShapeDtypeStruct((1536, 256), BF16),
             jax.ShapeDtypeStruct((2560, 256), BF16),
             jax.ShapeDtypeStruct((1152, 256), BF16),
-            jax.ShapeDtypeStruct((32, 256), BF16),
+            jax.ShapeDtypeStruct((1024, 128), BF16),
             jax.ShapeDtypeStruct((1, 256), F32),
-            jax.ShapeDtypeStruct((1, 128), F32),
             jax.ShapeDtypeStruct((1, 256), F32),
         ],
         compiler_params=params(16),
         cost_estimate=cost(2 * 300 * 128 * 6144, 5 * MIB),
         name="prepare",
-    )(conv_first, conv_second, bias_first[None], bias_second[None], head, e1a, e1b, e2a, e2b)
+    )(conv_first, conv_second, bias_first[None], bias_second[None], head, e1a, e1o, e1r, e2a, e2b)
 
 
 def on_device(
@@ -717,10 +742,11 @@
     lo, mid, hi, slots = far_splat(features, weights, owners, tile_ids, counts)
     from_xlo = step(hi, "gx", 1)
     from_xhi = step(lo, "gx", -1)
-    t1a, t1b, t2a, t2b, headx, b1a, b1b, b2 = prepare(
+    t1a, t1o, t1r, t2a, t2b, headx, b1, b2 = prepare(
         conv_first, conv_second, bias_first, bias_second, head
     )
     own = own_splat(features, weights, tile_ids)
+    own, from_xlo, from_xhi, mid = lax.optimization_barrier((own, from_xlo, from_xhi, mid))
     to_hi = jnp.stack([from_xlo[2], mid[2], from_xhi[2]])
     to_lo = jnp.stack([from_xlo[0], mid[0], from_xhi[0]])
     from_ylo = step(to_hi, "gy", 1)
@@ -732,13 +758,15 @@
     x, slo, shi = widen_y(g, rlo, rhi)
     xlo = step(shi, "gx", 1)
     xhi = step(slo, "gx", -1)
-    part = inner_convs(x, g, t1a, b1a, t2a, b2)
-    grid_out, table, ans_ylo, ans_yhi, ans_x = edge_convs(
-        x, xlo, xhi, part, t1b, b1b, t2b, headx, ids
+    part, pre = inner_convs(x, g, t1a, t1o, b1, t2a, b2)
+    total, table, ans_ylo, ans_yhi, ans_x = edge_convs(
+        xlo, xhi, part, pre, t1r, t2b, headx, ids
     )
 
     back_yhi = step(ans_ylo, "gy", -1)
     back_ylo = step(ans_yhi, "gy", 1)
+    grid_out = turn(total)
+    grid_out, back_ylo, back_yhi = lax.optimization_barrier((grid_out, back_ylo, back_yhi))
     near, far_w = own_read(tile_ids, table, weights, particles)
     to_lo = jnp.stack([back_ylo[0], ans_x[0], back_yhi[0]])
     to_hi = jnp.stack([back_ylo[2], ans_x[1], back_yhi[2]])

time: 99.3 us -> 94 us (0.947)
  the two profiles are of different devices: /device:TPU:39 before, /device:TPU:3 now
where the time goes in v2:
time: 94 us; the launch traced here: 93.6 us
  Pallas kernels  40.2 us (43%)
  starting transfers between devices  39.7 us (42%)
  waiting for transfers between devices  11.7 us (12%)
  between operations  1.72 us (2%)
    ppermute x12, starting transfers between devices, step(): lax.ppermute(x, axis, [(i, i + by) for i in range(size) if 0 <= i + by <...  39.7 us
    ppermute x12, waiting for transfers between devices, step(): lax.ppermute(x, axis, [(i, i + by) for i in range(size) if 0 <= i + by <...  11.7 us
    pallas_call x1, Pallas kernels, inner_convs(): pl.pallas_call(inner_kernel, in_specs=[vm] * 7, out_specs=[vm, vm], out_s...  8.19 us
    pallas_call x1, Pallas kernels, own_splat(): pl.pallas_call(own_splat_kernel, in_specs=[pl.BlockSpec(memory_space=SMEM...  6.4 us
    pallas_call x1, Pallas kernels, edge_convs(): pl.pallas_call(edge_kernel, in_specs=[vm] * 7 + [pl.BlockSpec(memory_spac...  6.2 us
    pallas_call x1, Pallas kernels, far_splat(): pl.pallas_call(far_splat_kernel, in_specs=[anywhere] * 5, out_specs=[vm,...  5.85 us
    pallas_call x1, Pallas kernels, own_read(): pl.pallas_call(own_read_kernel, in_specs=[pl.BlockSpec(memory_space=SMEM)...  4.28 us
    pallas_call x1, Pallas kernels, far_read(): pl.pallas_call(far_read_kernel, in_specs=[smem, smem] + [vm] * 6, out_spe...  2.76 us
  transfers between devices with their start and end apart: 12, of which 6 were waited for; matrix products, arithmetic and copies ran while one was open for 0% of the time, Pallas kernels for 24%

profile of v2, /device:TPU:3, one launch (start us, length us, event | category | flops | bytes accessed | tf_op | source)
XLA Modules:
  0.0 93.6 jit_solution(15190293579382523217)
XLA Ops:
  1.3 5.9 %far_splat.1 = (bf16[3,528,128]{2,1,0:T(8,128)(2,1)}, bf16[3,528,128]{2,1,0:T(8,128)(2,1)}, bf16[3,528,128]{2,1,0:T(8,128)(2,1)}, s32[128]{0:T(128)}) custom-call(s32[256]{0:T(256)} %owners_h.1, s32[256]{0:T(256)} %ids.3, s32[1]{0:T(128)S(6)} %copy.17.counts_h.counts, bf16[32,32768]{1,0:T(8,128)(2,1)} %f_hbm.3, bf16[32768,128]{1,0:T(8,128)(2,1)} %w_hbm.5), custom_call_target="tpu_custom_call" | custom-call | flops 134217728 | bytes 6291456 | tf_op jit(solution)/shard_map/far_splat/pallas_call | solution.py:142
  7.1 3.2 %collective-permute-start = (bf16[3,528,128]{2,1,0:T(8,128)(2,1)}, bf16[3,528,128]{2,1,0:T(8,128)(2,1)S(1)}, u32[]{:S(2)}, u32[]{:S(2)}) collective-permute-start(bf16[3,528,128]{2,1,0:T(8,128)(2,1)} %get-tuple-element.37), channel_id=1, source_target_pairs={{0,8},{8,16},{16,24},{24,32},{32,40},{40,48},{48,56},{56,64},{64,7... | collective-permute-start | bytes 1216520 | tf_op jit(solution)/shard_map/ppermute | solution.py:738
  10.3 4.3 %collective-permute-start.1 = (bf16[3,528,128]{2,1,0:T(8,128)(2,1)}, bf16[3,528,128]{2,1,0:T(8,128)(2,1)S(1)}, u32[]{:S(2)}, u32[]{:S(2)}) collective-permute-start(bf16[3,528,128]{2,1,0:T(8,128)(2,1)} %get-tuple-element.38), channel_id=1, source_target_pairs={{8,0},{16,8},{24,16},{32,24},{40,32},{48,40},{56,48},{64,56},{72,6... | collective-permute-start | bytes 1216520 | tf_op jit(solution)/shard_map/ppermute | solution.py:738
  14.7 6.4 %own_splat.1.own = bf16[2,16,128,128]{3,2,1,0:T(8,128)(2,1)} custom-call(s32[256]{0:T(256)} %ids.3, bf16[32,32768]{1,0:T(8,128)(2,1)} %f_hbm.3, bf16[32768,128]{1,0:T(8,128)(2,1)} %w_hbm.5), custom_call_target="tpu_custom_call" | custom-call | flops 134217728 | bytes 6291456 | tf_op jit(solution)/shard_map/own_splat/pallas_call | solution.py:188
  21.1 0.5 collective-permute-done.from_xlo
  21.6 1.1 %collective-permute-done.1.from_xhi = bf16[3,528,128]{2,1,0:T(8,128)(2,1)S(1)} collective-permute-done((bf16[3,528,128]{2,1,0:T(8,128)(2,1)}, bf16[3,528,128]{2,1,0:T(8,128)(2,1)S(1)}, u32[]{:S(2)}, u32[]{:S(2)}) %collective-permute-start.1) | collective-permute-done | bytes 405536 | tf_op jit(solution)/shard_map/ppermute | solution.py:738
  22.7 0.1 fusion
  22.8 5.4 %collective-permute-start.2 = (bf16[3,528,128]{2,1,0:T(8,128)(2,1)S(1)}, bf16[3,528,128]{2,1,0:T(8,128)(2,1)S(1)}, u32[]{:S(2)}, u32[]{:S(2)}) collective-permute-start(bf16[3,528,128]{2,1,0:T(8,128)(2,1)S(1)} %pad_maximum_fusion), channel_id=1, source_target_pairs={{0,1},{1,2},{2,3},{3,4},{4,5},{5,6},{6,7},{8,9},{9,10},{10,11},{11... | collective-permute-start | bytes 1216520 | tf_op jit(solution)/shard_map/ppermute | solution.py:738
  28.3 0.0 copy-start.1
  28.3 0.0 copy-start.2
  28.3 0.0 copy-start.3
  28.4 2.1 %collective-permute-start.3 = (bf16[3,528,128]{2,1,0:T(8,128)(2,1)S(1)}, bf16[3,528,128]{2,1,0:T(8,128)(2,1)S(1)}, u32[]{:S(2)}, u32[]{:S(2)}) collective-permute-start(bf16[3,528,128]{2,1,0:T(8,128)(2,1)S(1)} %pad_maximum_fusion.1), channel_id=1, source_target_pairs={{1,0},{2,1},{3,2},{4,3},{5,4},{6,5},{7,6},{9,8},{10,9},{11,10},{12... | collective-permute-start | bytes 1216520 | tf_op jit(solution)/shard_map/ppermute | solution.py:738
  30.5 2.6 %collective-permute-done.2.from_ylo = bf16[3,528,128]{2,1,0:T(8,128)(2,1)S(1)} collective-permute-done((bf16[3,528,128]{2,1,0:T(8,128)(2,1)S(1)}, bf16[3,528,128]{2,1,0:T(8,128)(2,1)S(1)}, u32[]{:S(2)}, u32[]{:S(2)}) %collective-permute-start.2) | collective-permute-done | bytes 405536 | tf_op jit(solution)/shard_map/ppermute | solution.py:738
  33.1 4.7 %collective-permute-done.3.from_yhi = bf16[3,528,128]{2,1,0:T(8,128)(2,1)S(1)} collective-permute-done((bf16[3,528,128]{2,1,0:T(8,128)(2,1)S(1)}, bf16[3,528,128]{2,1,0:T(8,128)(2,1)S(1)}, u32[]{:S(2)}, u32[]{:S(2)}) %collective-permute-start.3) | collective-permute-done | bytes 405536 | tf_op jit(solution)/shard_map/ppermute | solution.py:738
  37.8 2.2 %sum_tiles.1 = (bf16[2,16,128,128]{3,2,1,0:T(8,128)(2,1)S(1)}, bf16[4,16,128]{2,1,0:T(8,128)(2,1)S(1)}, bf16[4,16,128]{2,1,0:T(8,128)(2,1)S(1)}, s32[8,128]{1,0:T(8,128)S(1)}) custom-call(bf16[2,16,128,128]{3,2,1,0:T(8,128)(2,1)S(1)} %copy-done, bf16[3,528,128]{2,1,0:T(8,128)(2,1)S(1)} %collective-permute-done.2.from_ylo, ...), custom_call_target="tpu_custom_call" | custom-call | flops 1000 | bytes 4194304 | tf_op jit(solution)/shard_map/sum_tiles/pallas_call | solution.py:234
  40.0 1.9 %collective-permute-start.4 = (bf16[4,16,128]{2,1,0:T(8,128)(2,1)S(1)}, bf16[4,16,128]{2,1,0:T(8,128)(2,1)S(1)}, u32[]{:S(2)}, u32[]{:S(2)}) collective-permute-start(bf16[4,16,128]{2,1,0:T(8,128)(2,1)S(1)} %get-tuple-element.45), channel_id=1, source_target_pairs={{0,1},{1,2},{2,3},{3,4},{4,5},{5,6},{6,7},{8,9},{9,10},{10,11},{11... | collective-permute-start | bytes 49160 | tf_op jit(solution)/shard_map/ppermute | solution.py:738
  42.0 2.4 %collective-permute-start.5 = (bf16[4,16,128]{2,1,0:T(8,128)(2,1)S(1)}, bf16[4,16,128]{2,1,0:T(8,128)(2,1)S(1)}, u32[]{:S(2)}, u32[]{:S(2)}) collective-permute-start(bf16[4,16,128]{2,1,0:T(8,128)(2,1)S(1)} %get-tuple-element.46), channel_id=1, source_target_pairs={{1,0},{2,1},{3,2},{4,3},{5,4},{6,5},{7,6},{9,8},{10,9},{11,10},{12... | collective-permute-start | bytes 49160 | tf_op jit(solution)/shard_map/ppermute | solution.py:738
  44.5 1.7 %prepare.1 = (bf16[2304,256]{1,0:T(8,128)(2,1)S(1)}, bf16[3072,256]{1,0:T(8,128)(2,1)S(1)}, bf16[1536,256]{1,0:T(8,128)(2,1)S(1)}, bf16[2560,256]{1,0:T(8,128)(2...) custom-call(bf16[27,32,32]{2,1,0:T(8,128)(2,1)S(1)} %copy-done.5, ...), custom_call_target="tpu_custom_call" | custom-call | flops 471859200 | bytes 5242880 | tf_op jit(solution)/shard_map/prepare/pallas_call | solution.py:702
  46.2 1.1 %collective-permute-done.5.rhi = bf16[4,16,128]{2,1,0:T(8,128)(2,1)S(1)} collective-permute-done((bf16[4,16,128]{2,1,0:T(8,128)(2,1)S(1)}, bf16[4,16,128]{2,1,0:T(8,128)(2,1)S(1)}, u32[]{:S(2)}, u32[]{:S(2)}) %collective-permute-start.5) | collective-permute-done | bytes 16416 | tf_op jit(solution)/shard_map/ppermute | solution.py:738
  47.3 0.8 widen_y.1
  48.1 3.0 %collective-permute-start.6 = (bf16[8,144,128]{2,1,0:T(8,128)(2,1)S(1)}, bf16[8,144,128]{2,1,0:T(8,128)(2,1)S(1)}, u32[]{:S(2)}, u32[]{:S(2)}) collective-permute-start(bf16[8,144,128]{2,1,0:T(8,128)(2,1)S(1)} %get-tuple-element.47), channel_id=1, source_target_pairs={{0,8},{8,16},{16,24},{24,32},{32,40},{40,48},{48,56},{56,64},{64,7... | collective-permute-start | bytes 884744 | tf_op jit(solution)/shard_map/ppermute | solution.py:738
  51.1 5.2 %collective-permute-start.7 = (bf16[8,144,128]{2,1,0:T(8,128)(2,1)S(1)}, bf16[8,144,128]{2,1,0:T(8,128)(2,1)S(1)}, u32[]{:S(2)}, u32[]{:S(2)}) collective-permute-start(bf16[8,144,128]{2,1,0:T(8,128)(2,1)S(1)} %get-tuple-element.48), channel_id=1, source_target_pairs={{8,0},{16,8},{24,16},{32,24},{40,32},{48,40},{56,48},{64,56},{72,6... | collective-permute-start | bytes 884744 | tf_op jit(solution)/shard_map/ppermute | solution.py:738
  56.3 8.2 %inner_convs.1 = (f32[8,2,128,256]{3,2,1,0:T(8,128)S(1)}, f32[2,576,256]{2,1,0:T(8,128)S(1)}) custom-call(bf16[2,16,144,128]{3,2,1,0:T(8,128)(2,1)S(1)} %get-tuple-element.49.x, bf16[2,8,2,128,128]{4,3,2,1,0:T(8,128)(2,1)S(1)} %bitcast.3, bf16[2304,256]{1,0:T(8,128)(2,1)S(1)} %get-tuple-element.50.t1, bf16[3072,256]{1,0:T(8,128)(2,1)S(1)} %get-tuple-element.51.t1o, ...), custom_call_target="tpu_custom_call" | custom-call | flops 6039797760 | bytes 6291456 | tf_op jit(solution)/shard_map/inner_convs/pallas_call | solution.py:356
  64.6 6.2 %edge_convs.1 = (bf16[8,2,128,256]{3,2,1,0:T(8,128)(2,1)S(1)}, f32[128,8,128]{2,1,0:T(8,128)S(1)}, bf16[3,64,128]{2,1,0:T(8,128)(2,1)S(1)}, bf16[3,64,128]{2,1,0:T(8,128)(2,1)S(1)}, bf16[2,64,128]{2,1,0:T(8,128)(2,1)S(1)}) custom-call(bf16[8,144,128]{2,1,0:T(8,128)(2,1)S(1)} %collective-permute-done.6.rlo, ...), custom_call_target="tpu_custom_call" | custom-call | flops 2717908992 | bytes 6291456 | tf_op jit(solution)/shard_map/edge_convs/pallas_call | solution.py:468
  70.8 2.6 %collective-permute-start.8 = (bf16[3,64,128]{2,1,0:T(8,128)(2,1)S(1)}, bf16[3,64,128]{2,1,0:T(8,128)(2,1)S(1)}, u32[]{:S(2)}, u32[]{:S(2)}) collective-permute-start(bf16[3,64,128]{2,1,0:T(8,128)(2,1)S(1)} %get-tuple-element.62), channel_id=1, source_target_pairs={{0,1},{1,2},{2,3},{3,4},{4,5},{5,6},{6,7},{8,9},{9,10},{10,11},{11... | collective-permute-start | bytes 147464 | tf_op jit(solution)/shard_map/ppermute | solution.py:738
  73.4 1.9 %collective-permute-start.9 = (bf16[3,64,128]{2,1,0:T(8,128)(2,1)S(1)}, bf16[3,64,128]{2,1,0:T(8,128)(2,1)S(1)}, u32[]{:S(2)}, u32[]{:S(2)}) collective-permute-start(bf16[3,64,128]{2,1,0:T(8,128)(2,1)S(1)} %get-tuple-element.63), channel_id=1, source_target_pairs={{1,0},{2,1},{3,2},{4,3},{5,4},{6,5},{7,6},{9,8},{10,9},{11,10},{12... | collective-permute-start | bytes 147464 | tf_op jit(solution)/shard_map/ppermute | solution.py:738
  75.3 1.8 %turn.1 = bf16[32,16,8,128]{3,2,1,0:T(8,128)(2,1)} custom-call(bf16[8,2,128,256]{3,2,1,0:T(8,128)(2,1)S(1)} %get-tuple-element.61.total), custom_call_target="tpu_custom_call" | custom-call | flops 1000 | bytes 8388608 | tf_op jit(solution)/shard_map/turn/pallas_call | solution.py:496
  77.2 1.7 %collective-permute-done.9.yhi = bf16[3,64,128]{2,1,0:T(8,128)(2,1)S(1)} collective-permute-done((bf16[3,64,128]{2,1,0:T(8,128)(2,1)S(1)}, bf16[3,64,128]{2,1,0:T(8,128)(2,1)S(1)}, u32[]{:S(2)}, u32[]{:S(2)}) %collective-permute-start.9) | collective-permute-done | bytes 49184 | tf_op jit(solution)/shard_map/ppermute | solution.py:738
  78.8 2.2 %collective-permute-start.10 = (bf16[3,64,128]{2,1,0:T(8,128)(2,1)S(1)}, bf16[3,64,128]{2,1,0:T(8,128)(2,1)S(1)}, u32[]{:S(2)}, u32[]{:S(2)}) collective-permute-start(bf16[3,64,128]{2,1,0:T(8,128)(2,1)S(1)} %pad_maximum_fusion.2), channel_id=1, source_target_pairs={{0,8},{8,16},{16,24},{24,32},{32,40},{40,48},{48,56},{56,64},{64,7... | collective-permute-start | bytes 147464 | tf_op jit(solution)/shard_map/ppermute | solution.py:738
  81.1 5.4 %collective-permute-start.11 = (bf16[3,64,128]{2,1,0:T(8,128)(2,1)S(1)}, bf16[3,64,128]{2,1,0:T(8,128)(2,1)S(1)}, u32[]{:S(2)}, u32[]{:S(2)}) collective-permute-start(bf16[3,64,128]{2,1,0:T(8,128)(2,1)S(1)} %pad_maximum_fusion.3), channel_id=1, source_target_pairs={{8,0},{16,8},{24,16},{32,24},{40,32},{48,40},{56,48},{64,56},{72,6... | collective-permute-start | bytes 147464 | tf_op jit(solution)/shard_map/ppermute | solution.py:738
  86.5 4.3 %own_read.1 = (f32[3,16384]{1,0:T(4,128)S(1)}, bf16[16384,128]{1,0:T(8,128)(2,1)S(1)}) custom-call(s32[256]{0:T(256)S(1)} %copy-done.8, f32[128,8,128]{2,1,0:T(8,128)S(1)} %get-tuple-element.69.table, bf16[32768,128]{1,0:T(8,128)(2,1)} %w_hbm.5), custom_call_target="tpu_custom_call" | custom-call | flops 134217728 | bytes 9437184 | tf_op jit(solution)/shard_map/own_read/pallas_call | solution.py:564
  90.8 2.8 %far_read.1 = f32[3,32768]{1,0:T(4,128)} custom-call(s32[128]{0:T(128)S(1)} %copy-done.12, s32[1]{0:T(128)S(6)} %copy.17.counts_h.counts, bf16[3,64,128]{2,1,0:T(8,128)(2,1)S(1)} %collective-permute-done.10.blo, bf16[3,64,128]{2,1,0:T(8,128)(2,1)S(1)} %collective-permute-done.11.bhi, bf16[3,64,128]{2,1,0:T(8,128)(2,1)S(1)} %collective-permute-done.8.ylo, ...), custom_call_target="tpu_custom_call" | custom-call | flops 134217728 | bytes 5242880 | tf_op jit(solution)/shard_map/far_read/pallas_call | solution.py:610
  (39 shorter events, 0.2 us)
Async XLA Ops:
  7.1 14.4 %collective-permute-start = (bf16[3,528,128]{2,1,0:T(8,128)(2,1)}, bf16[3,528,128]{2,1,0:T(8,128)(2,1)S(1)}, u32[]{:S(2)}, u32[]{:S(2)}) collective-permute-start(bf16[3,528,128]{2,1,0:T(8,128)(2,1)} %get-tuple-element.37), channel_id=1, source_target_pairs={{0,8},{8,16},{16,24},{24,32},{32,40},{40,48},{48,56},{56,64},{64,7... | collective-permute-start | bytes 1216520 | tf_op jit(solution)/shard_map/ppermute | solution.py:738
  10.3 12.4 %copy-start.13 = (bf16[3,528,128]{2,1,0:T(8,128)(2,1)S(1)}, bf16[3,528,128]{2,1,0:T(8,128)(2,1)}, u32[]{:S(2)}) copy-start(bf16[3,528,128]{2,1,0:T(8,128)(2,1)} %get-tuple-element.42) | copy-start | bytes 1216516
  10.3 12.3 %collective-permute-start.1 = (bf16[3,528,128]{2,1,0:T(8,128)(2,1)}, bf16[3,528,128]{2,1,0:T(8,128)(2,1)S(1)}, u32[]{:S(2)}, u32[]{:S(2)}) collective-permute-start(bf16[3,528,128]{2,1,0:T(8,128)(2,1)} %get-tuple-element.38), channel_id=1, source_target_pairs={{8,0},{16,8},{24,16},{32,24},{40,32},{48,40},{56,48},{64,56},{72,6... | collective-permute-start | bytes 1216520 | tf_op jit(solution)/shard_map/ppermute | solution.py:738
  22.7 15.1 %copy-start = (bf16[2,16,128,128]{3,2,1,0:T(8,128)(2,1)S(1)}, bf16[2,16,128,128]{3,2,1,0:T(8,128)(2,1)}, u32[]{:S(2)}) copy-start(bf16[2,16,128,128]{3,2,1,0:T(8,128)(2,1)} %own_splat.1.own) | copy-start | bytes 3145732
  22.8 10.3 %collective-permute-start.2 = (bf16[3,528,128]{2,1,0:T(8,128)(2,1)S(1)}, bf16[3,528,128]{2,1,0:T(8,128)(2,1)S(1)}, u32[]{:S(2)}, u32[]{:S(2)}) collective-permute-start(bf16[3,528,128]{2,1,0:T(8,128)(2,1)S(1)} %pad_maximum_fusion), channel_id=1, source_target_pairs={{0,1},{1,2},{2,3},{3,4},{4,5},{5,6},{6,7},{8,9},{9,10},{10,11},{11... | collective-permute-start | bytes 1216520 | tf_op jit(solution)/shard_map/ppermute | solution.py:738
  28.3 16.1 %copy-start.1 = (bf16[128,2048]{1,0:T(8,128)(2,1)S(1)}, bf16[128,2048]{1,0:T(8,128)(2,1)}, u32[]{:S(2)}) copy-start(bf16[128,2048]{1,0:T(8,128)(2,1)} %constant.13.clone.e2a) | copy-start | bytes 1572868
  28.3 16.1 %copy-start.2 = (bf16[128,2048]{1,0:T(8,128)(2,1)S(1)}, bf16[128,2048]{1,0:T(8,128)(2,1)}, u32[]{:S(2)}) copy-start(bf16[128,2048]{1,0:T(8,128)(2,1)} %constant.10.clone.e1a) | copy-start | bytes 1572868
  28.3 16.1 %copy-start.3 = (bf16[128,1024]{1,0:T(8,128)(2,1)S(1)}, bf16[128,1024]{1,0:T(8,128)(2,1)}, u32[]{:S(2)}) copy-start(bf16[128,1024]{1,0:T(8,128)(2,1)} %constant.14.clone.e2b) | copy-start | bytes 786436
  28.3 16.1 %copy-start.4 = (bf16[128,1024]{1,0:T(8,128)(2,1)S(1)}, bf16[128,1024]{1,0:T(8,128)(2,1)}, u32[]{:S(2)}) copy-start(bf16[128,1024]{1,0:T(8,128)(2,1)} %constant.11.clone.e1o) | copy-start | bytes 786436
  28.3 16.1 %copy-start.5 = (bf16[27,32,32]{2,1,0:T(8,128)(2,1)S(1)}, bf16[27,32,32]{2,1,0:T(8,128)(2,1)}, u32[]{:S(2)}) copy-start(bf16[27,32,32]{2,1,0:T(8,128)(2,1)} %c1.1) | copy-start | bytes 165892
  28.3 16.1 %copy-start.6 = (bf16[27,32,32]{2,1,0:T(8,128)(2,1)S(1)}, bf16[27,32,32]{2,1,0:T(8,128)(2,1)}, u32[]{:S(2)}) copy-start(bf16[27,32,32]{2,1,0:T(8,128)(2,1)} %c2.1) | copy-start | bytes 165892
  28.3 16.1 %copy-start.7 = (bf16[128,512]{1,0:T(8,128)(2,1)S(1)}, bf16[128,512]{1,0:T(8,128)(2,1)}, u32[]{:S(2)}) copy-start(bf16[128,512]{1,0:T(8,128)(2,1)} %constant.12.clone.e1r) | copy-start | bytes 393220
  28.3 16.1 %copy-start.9 = (bf16[3,32]{1,0:T(4,128)(2,1)S(1)}, bf16[3,32]{1,0:T(4,128)(2,1)}, u32[]{:S(2)}) copy-start(bf16[3,32]{1,0:T(4,128)(2,1)} %head.1) | copy-start | bytes 580
  28.4 16.1 %copy-start.10 = (f32[32]{0:T(128)S(1)}, f32[32]{0:T(128)}, u32[]{:S(2)}) copy-start(f32[32]{0:T(128)} %param.21) | copy-start | bytes 388
  28.4 16.1 %copy-start.11 = (f32[32]{0:T(128)S(1)}, f32[32]{0:T(128)}, u32[]{:S(2)}) copy-start(f32[32]{0:T(128)} %param.23) | copy-start | bytes 388
  28.4 9.4 %collective-permute-start.3 = (bf16[3,528,128]{2,1,0:T(8,128)(2,1)S(1)}, bf16[3,528,128]{2,1,0:T(8,128)(2,1)S(1)}, u32[]{:S(2)}, u32[]{:S(2)}) collective-permute-start(bf16[3,528,128]{2,1,0:T(8,128)(2,1)S(1)} %pad_maximum_fusion.1), channel_id=1, source_target_pairs={{1,0},{2,1},{3,2},{4,3},{5,4},{6,5},{7,6},{9,8},{10,9},{11,10},{12... | collective-permute-start | bytes 1216520 | tf_op jit(solution)/shard_map/ppermute | solution.py:738
  40.0 6.1 %collective-permute-start.4 = (bf16[4,16,128]{2,1,0:T(8,128)(2,1)S(1)}, bf16[4,16,128]{2,1,0:T(8,128)(2,1)S(1)}, u32[]{:S(2)}, u32[]{:S(2)}) collective-permute-start(bf16[4,16,128]{2,1,0:T(8,128)(2,1)S(1)} %get-tuple-element.45), channel_id=1, source_target_pairs={{0,1},{1,2},{2,3},{3,4},{4,5},{5,6},{6,7},{8,9},{9,10},{10,11},{11... | collective-permute-start | bytes 49160 | tf_op jit(solution)/shard_map/ppermute | solution.py:738
  42.0 5.4 %collective-permute-start.5 = (bf16[4,16,128]{2,1,0:T(8,128)(2,1)S(1)}, bf16[4,16,128]{2,1,0:T(8,128)(2,1)S(1)}, u32[]{:S(2)}, u32[]{:S(2)}) collective-permute-start(bf16[4,16,128]{2,1,0:T(8,128)(2,1)S(1)} %get-tuple-element.46), channel_id=1, source_target_pairs={{1,0},{2,1},{3,2},{4,3},{5,4},{6,5},{7,6},{9,8},{10,9},{11,10},{12... | collective-permute-start | bytes 49160 | tf_op jit(solution)/shard_map/ppermute | solution.py:738
  48.1 16.4 %collective-permute-start.6 = (bf16[8,144,128]{2,1,0:T(8,128)(2,1)S(1)}, bf16[8,144,128]{2,1,0:T(8,128)(2,1)S(1)}, u32[]{:S(2)}, u32[]{:S(2)}) collective-permute-start(bf16[8,144,128]{2,1,0:T(8,128)(2,1)S(1)} %get-tuple-element.47), channel_id=1, source_target_pairs={{0,8},{8,16},{16,24},{24,32},{32,40},{40,48},{48,56},{56,64},{64,7... | collective-permute-start | bytes 884744 | tf_op jit(solution)/shard_map/ppermute | solution.py:738
  51.1 13.4 %collective-permute-start.7 = (bf16[8,144,128]{2,1,0:T(8,128)(2,1)S(1)}, bf16[8,144,128]{2,1,0:T(8,128)(2,1)S(1)}, u32[]{:S(2)}, u32[]{:S(2)}) collective-permute-start(bf16[8,144,128]{2,1,0:T(8,128)(2,1)S(1)} %get-tuple-element.48), channel_id=1, source_target_pairs={{8,0},{16,8},{24,16},{32,24},{40,32},{48,40},{56,48},{64,56},{72,6... | collective-permute-start | bytes 884744 | tf_op jit(solution)/shard_map/ppermute | solution.py:738
  70.8 15.7 %copy-start.8 = (s32[256]{0:T(256)S(1)}, s32[256]{0:T(256)}, u32[]{:S(2)}) copy-start(s32[256]{0:T(256)} %ids.3) | copy-start | bytes 3076
  70.8 6.4 %collective-permute-start.8 = (bf16[3,64,128]{2,1,0:T(8,128)(2,1)S(1)}, bf16[3,64,128]{2,1,0:T(8,128)(2,1)S(1)}, u32[]{:S(2)}, u32[]{:S(2)}) collective-permute-start(bf16[3,64,128]{2,1,0:T(8,128)(2,1)S(1)} %get-tuple-element.62), channel_id=1, source_target_pairs={{0,1},{1,2},{2,3},{3,4},{4,5},{5,6},{6,7},{8,9},{9,10},{10,11},{11... | collective-permute-start | bytes 147464 | tf_op jit(solution)/shard_map/ppermute | solution.py:738
  73.4 5.4 %collective-permute-start.9 = (bf16[3,64,128]{2,1,0:T(8,128)(2,1)S(1)}, bf16[3,64,128]{2,1,0:T(8,128)(2,1)S(1)}, u32[]{:S(2)}, u32[]{:S(2)}) collective-permute-start(bf16[3,64,128]{2,1,0:T(8,128)(2,1)S(1)} %get-tuple-element.63), channel_id=1, source_target_pairs={{1,0},{2,1},{3,2},{4,3},{5,4},{6,5},{7,6},{9,8},{10,9},{11,10},{12... | collective-permute-start | bytes 147464 | tf_op jit(solution)/shard_map/ppermute | solution.py:738
  78.8 12.0 %collective-permute-start.10 = (bf16[3,64,128]{2,1,0:T(8,128)(2,1)S(1)}, bf16[3,64,128]{2,1,0:T(8,128)(2,1)S(1)}, u32[]{:S(2)}, u32[]{:S(2)}) collective-permute-start(bf16[3,64,128]{2,1,0:T(8,128)(2,1)S(1)} %pad_maximum_fusion.2), channel_id=1, source_target_pairs={{0,8},{8,16},{16,24},{24,32},{32,40},{40,48},{48,56},{56,64},{64,7... | collective-permute-start | bytes 147464 | tf_op jit(solution)/shard_map/ppermute | solution.py:738
  81.1 9.7 %collective-permute-start.11 = (bf16[3,64,128]{2,1,0:T(8,128)(2,1)S(1)}, bf16[3,64,128]{2,1,0:T(8,128)(2,1)S(1)}, u32[]{:S(2)}, u32[]{:S(2)}) collective-permute-start(bf16[3,64,128]{2,1,0:T(8,128)(2,1)S(1)} %pad_maximum_fusion.3), channel_id=1, source_target_pairs={{8,0},{16,8},{24,16},{32,24},{40,32},{48,40},{56,48},{64,56},{72,6... | collective-permute-start | bytes 147464 | tf_op jit(solution)/shard_map/ppermute | solution.py:738
  86.5 4.3 %copy-start.12 = (s32[128]{0:T(128)S(1)}, s32[128]{0:T(128)}, u32[]{:S(2)}) copy-start(s32[128]{0:T(128)} %get-tuple-element.65.slots) | copy-start | bytes 1540

commit v3 on v2

--- a/solution.py
+++ b/solution.py
@@ -202,94 +202,163 @@
     )(ids, features, weights)
 
 
-def sum_kernel(own, from_ylo, from_yhi, from_xlo, from_xhi, g, ylo, yhi, ids, grid, idv, sem):
-    groups = [(from_ylo, 0), (from_ylo, 1), (from_ylo, 2)]
-    groups += [(from_yhi, 0), (from_yhi, 1), (from_yhi, 2)]
-    groups += [(from_xlo, 1), (from_xhi, 1)]
-    rows = [ref[k, SLOTS * 32 : PAY, :].astype(F32)[0:1] for ref, k in groups]
-    idv[...] = jnp.concatenate(rows, 0).astype(jnp.int32)
+BUNDLE = 3 * PAY + 64
+
+
+def ids_of(groups):
+    rows = [ref[at + SLOTS * 32 : at + PAY, :].astype(F32)[0:1] for ref, at in groups]
+    return jnp.concatenate(rows, 0).astype(jnp.int32)
+
+
+def tile_of(ref, at, j):
+    rows = ref[pl.ds(pl.multiple_of(at + j * 32, 16), 32), :]
+    return rows.astype(F32).reshape(4, 8, 128)
+
+
+def add_tiles(grid, ids, n, ref, at):
+    def add(j, carry):
+        z, tx, y = tile_place(ids[n, j])
+        grid[tx, pl.ds(z, 4), pl.ds(y, 8), :] += tile_of(ref, at, j)
+        return carry
+
+    lax.fori_loop(0, SLOTS, add, 0, unroll=4)
+
+
+def column_kernel(
+    own, xlo, xhi, mid, g, ids, to_lo, to_hi, fwd_lo, fwd_hi, keep_lo, keep_hi, acc, idv, sem
+):
+    zero, one, two = 0, PAY, 2 * PAY
+    groups = [(xlo, one), (xhi, one)]
+    groups += [(xlo, two), (mid, two), (xhi, two), (xlo, zero), (mid, zero), (xhi, zero)]
+    idv[...] = ids_of(groups)
     copy = pltpu.make_async_copy(idv, ids, sem)
     copy.start()
-    grid[...] = own[...].astype(F32)
+    g[...] = own[...].astype(F32)
+    acc[...] = jnp.zeros_like(acc)
+    for n, (ref, at) in enumerate(groups[2:]):
+        out, k = (to_hi, n) if n < 3 else (to_lo, n - 3)
+        out[k * PAY : (k + 1) * PAY, :] = ref[at : at + PAY, :]
     copy.wait()
-    for n, (ref, k) in enumerate(groups):
-
-        def add(j, carry, n=n, ref=ref, k=k):
-            z, tx, y = tile_place(ids[n, j])
-            tile = ref[k, pl.ds(pl.multiple_of(j * 32, 32), 32), :].astype(F32).reshape(4, 8, 128)
-            grid[tx, pl.ds(z, 4), pl.ds(y, 8), :] += tile
+    for n, (ref, at) in enumerate(groups):
+        if n < 2:
+            add_tiles(g, ids, n, ref, at)
+            continue
+
+        def add(j, carry, n=n, ref=ref, at=at):
+            tile = ids[n, j]
+            ty = tile & 15
+            place = jnp.where(ty == 0, 0, jnp.where(ty == 15, 1, 2)) + (0 if n < 5 else 3)
+            acc[place, (tile >> 4) & 1, pl.ds((tile >> 5) * 4, 4)] += tile_of(ref, at, j)
             return carry
 
         lax.fori_loop(0, SLOTS, add, 0, unroll=4)
-    g[...] = grid[...].astype(BF16)
     for tx in range(2):
         for r in range(2):
-            ylo[tx * 2 + r] = grid[tx, :, r, :].astype(BF16)
-            yhi[tx * 2 + r] = grid[tx, :, BY - 2 + r, :].astype(BF16)
-
-
-def sum_tiles(own, from_ylo, from_yhi, from_xlo, from_xhi):
+            k = tx * 2 + r
+            rows = slice(3 * PAY + k * 16, 3 * PAY + k * 16 + 16)
+            to_lo[rows, :] = g[tx, :, r, :].astype(BF16)
+            to_hi[rows, :] = g[tx, :, BY - 2 + r, :].astype(BF16)
+            keep_hi[k] = acc[0, tx, :, r, :]
+            fwd_hi[k] = acc[1, tx, :, 6 + r, :].astype(BF16)
+            fwd_lo[k] = acc[3, tx, :, r, :].astype(BF16)
+            keep_lo[k] = acc[4, tx, :, 6 + r, :]
+
+
+def column(own, xlo, xhi, mid):
     vm = pl.BlockSpec(memory_space=VMEM)
-    edge = jax.ShapeDtypeStruct((4, SLAB, 128), BF16)
+    bundle = jax.ShapeDtypeStruct((BUNDLE, 128), BF16)
+    flat = [v.reshape(3 * PAY, 128) for v in (xlo, xhi, mid)]
+    return pl.pallas_call(
+        column_kernel,
+        in_specs=[vm] * 4,
+        out_specs=[vm, pl.BlockSpec(memory_space=SMEM)] + [vm] * 6,
+        out_shape=[
+            jax.ShapeDtypeStruct((2, SLAB, BY, 128), F32),
+            jax.ShapeDtypeStruct((8, 128), jnp.int32),
+            bundle,
+            bundle,
+            jax.ShapeDtypeStruct((4, SLAB, 128), BF16),
+            jax.ShapeDtypeStruct((4, SLAB, 128), BF16),
+            jax.ShapeDtypeStruct((4, SLAB, 128), F32),
+            jax.ShapeDtypeStruct((4, SLAB, 128), F32),
+        ],
+        scratch_shapes=[
+            VMEM((6, 2, SLAB, 8, 128), F32),
+            VMEM((8, 128), jnp.int32),
+            pltpu.SemaphoreType.DMA,
+        ],
+        compiler_params=params(16),
+        cost_estimate=cost(1000, 4 * MIB),
+        name="column",
+    )(own, *flat)
+
+
+def sum_kernel(
+    part, ylo, yhi, far_lo, far_hi, keep_lo, keep_hi, g, x, slo, shi, ids, grid, edge, idv, sem
+):
+    groups = [(ref, k * PAY) for ref in (ylo, yhi) for k in range(3)]
+    idv[0:6, :] = ids_of(groups)
+    idv[6:8, :] = jnp.zeros((2, 128), jnp.int32)
+    copy = pltpu.make_async_copy(idv, ids, sem)
+    copy.start()
+    grid[...] = part[...]
+    edge[...] = jnp.zeros_like(edge)
+    for tx in range(2):
+        for r in range(2):
+            k = tx * 2 + r
+            rows = slice(3 * PAY + k * 16, 3 * PAY + k * 16 + 16)
+            low = ylo[rows, :].astype(F32) + far_lo[k].astype(F32) + keep_lo[k]
+            high = yhi[rows, :].astype(F32) + far_hi[k].astype(F32) + keep_hi[k]
+            edge[tx, 0, :, 6 + r, :] = low
+            edge[tx, 1, :, r, :] = high
+    copy.wait()
+    for n, (ref, at) in enumerate(groups):
+        add_tiles(grid, ids, n, ref, at)
+    lane = lanes_of((ROWS, 128))
+
+    def plane(tx, z):
+        return jnp.concatenate([edge[tx, 0, z], grid[tx, z], edge[tx, 1, z]], 0)
+
+    def pair(z, carry):
+        for tx, ref in enumerate((slo, shi)):
+            a, b = plane(tx, z), plane(tx, z + 8)
+            x[tx, z] = a.astype(BF16)
+            x[tx, z + 8] = b.astype(BF16)
+            g[tx, z] = a[8 : 8 + BY].astype(BF16)
+            g[tx, z + 8] = b[8 : 8 + BY].astype(BF16)
+            if tx == 0:
+                ref[z] = jnp.where(lane < 64, a, pltpu.roll(b, 64, 1)).astype(BF16)
+            else:
+                ref[z] = jnp.where(lane < 64, pltpu.roll(a, 64, 1), b).astype(BF16)
+        return carry
+
+    lax.fori_loop(0, 8, pair, 0, unroll=2)
+
+
+def sum_tiles(part, ylo, yhi, far_lo, far_hi, keep_lo, keep_hi):
+    vm = pl.BlockSpec(memory_space=VMEM)
+    side = jax.ShapeDtypeStruct((SLAB // 2, ROWS, 128), BF16)
     return pl.pallas_call(
         sum_kernel,
-        in_specs=[vm] * 5,
-        out_specs=[vm, vm, vm, pl.BlockSpec(memory_space=SMEM)],
+        in_specs=[vm] * 7,
+        out_specs=[vm] * 4 + [pl.BlockSpec(memory_space=SMEM)],
         out_shape=[
             jax.ShapeDtypeStruct((2, SLAB, BY, 128), BF16),
-            edge,
-            edge,
+            jax.ShapeDtypeStruct((2, SLAB, ROWS, 128), BF16),
+            side,
+            side,
             jax.ShapeDtypeStruct((8, 128), jnp.int32),
         ],
         scratch_shapes=[
             VMEM((2, SLAB, BY, 128), F32),
+            VMEM((2, 2, SLAB, 8, 128), F32),
             VMEM((8, 128), jnp.int32),
             pltpu.SemaphoreType.DMA,
         ],
         compiler_params=params(16),
         cost_estimate=cost(1000, 4 * MIB),
         name="sum_tiles",
-    )(own, from_ylo, from_yhi, from_xlo, from_xhi)
-
-
-def widen_kernel(g, rlo, rhi, x, slo, shi, edge):
-    edge[...] = jnp.zeros_like(edge)
-    for tx in range(2):
-        for r in range(2):
-            edge[tx, 0, :, 6 + r, :] = rlo[tx * 2 + r].astype(F32)
-            edge[tx, 1, :, r, :] = rhi[tx * 2 + r].astype(F32)
-    lane = lanes_of((ROWS, 128))
-
-    def plane(tx, z):
-        return jnp.concatenate([edge[tx, 0, z], g[tx, z].astype(F32), edge[tx, 1, z]], 0)
-
-    def pair(z, carry):
-        a, b = plane(0, z), plane(0, z + 8)
-        x[0, z] = a.astype(BF16)
-        x[0, z + 8] = b.astype(BF16)
-        slo[z] = jnp.where(lane < 64, a, pltpu.roll(b, 64, 1)).astype(BF16)
-        a, b = plane(1, z), plane(1, z + 8)
-        x[1, z] = a.astype(BF16)
-        x[1, z + 8] = b.astype(BF16)
-        shi[z] = jnp.where(lane < 64, pltpu.roll(a, 64, 1), b).astype(BF16)
-        return carry
-
-    lax.fori_loop(0, 8, pair, 0)
-
-
-def widen_y(g, rlo, rhi):
-    vm = pl.BlockSpec(memory_space=VMEM)
-    side = jax.ShapeDtypeStruct((SLAB // 2, ROWS, 128), BF16)
-    return pl.pallas_call(
-        widen_kernel,
-        in_specs=[vm] * 3,
-        out_specs=[vm] * 3,
-        out_shape=[jax.ShapeDtypeStruct((2, SLAB, ROWS, 128), BF16), side, side],
-        scratch_shapes=[VMEM((2, 2, SLAB, 8, 128), F32)],
-        compiler_params=params(8),
-        cost_estimate=cost(1000, 3 * MIB),
-        name="widen_y",
-    )(g, rlo, rhi)
+    )(part, ylo, yhi, far_lo, far_hi, keep_lo, keep_hi)
 
 
 def rows_inside(shape, iy):
@@ -376,7 +445,7 @@
 
 
 def edge_kernel(
-    rlo, rhi, part, pre, t1, t2, headx, ids, total, table, ans_ylo, ans_yhi, ans_x, es, hs, vel
+    rlo, rhi, part, pre, t1, t2, headx, ids, idx, total, table, ans_ylo, ans_yhi, ans_x, es, hs, vel
 ):
     ix = lax.axis_index("gx")
     iy = lax.axis_index("gy")
@@ -447,12 +516,13 @@
     places = [(ans_ylo, 0), (ans_ylo, 1), (ans_ylo, 2), (ans_yhi, 0), (ans_yhi, 1), (ans_yhi, 2)]
     places += [(ans_x, 0), (ans_x, 1)]
     for n, (ref, k) in enumerate(places):
-
-        def answer(j, carry, n=n, ref=ref, k=k):
+        source, row = (ids, n) if n < 6 else (idx, n - 6)
+
+        def answer(j, carry, source=source, row=row, ref=ref, k=k):
             halves = []
             for h in range(2):
-                r0 = table[tile_row(ids[n, j * 4 + 2 * h])]
-                r1 = table[tile_row(ids[n, j * 4 + 2 * h + 1])]
+                r0 = table[tile_row(source[row, j * 4 + 2 * h])]
+                r1 = table[tile_row(source[row, j * 4 + 2 * h + 1])]
                 halves.append(two_blocks(r0, r1))
             ref[k, pl.ds(pl.multiple_of(j * 16, 16), 16), :] = jnp.concatenate(halves, 0).astype(
                 BF16
@@ -462,12 +532,12 @@
         lax.fori_loop(0, SLOTS // 4, answer, 0, unroll=4)
 
 
-def edge_convs(rlo, rhi, part, pre, t1, t2, headx, ids):
+def edge_convs(rlo, rhi, part, pre, t1, t2, headx, ids, idx):
     vm = pl.BlockSpec(memory_space=VMEM)
     ans = jax.ShapeDtypeStruct((3, 64, 128), BF16)
     return pl.pallas_call(
         edge_kernel,
-        in_specs=[vm] * 7 + [pl.BlockSpec(memory_space=SMEM)],
+        in_specs=[vm] * 7 + [pl.BlockSpec(memory_space=SMEM)] * 2,
         out_specs=[vm] * 5,
         out_shape=[
             jax.ShapeDtypeStruct((SLAB // 2, 2, BY, 256), BF16),
@@ -484,7 +554,7 @@
         compiler_params=params(32),
         cost_estimate=cost(2 * 9 * 256 * 256 * 2304, 6 * MIB),
         name="edge_convs",
-    )(rlo, rhi, part, pre, t1, t2, headx, ids)
+    )(rlo, rhi, part, pre, t1, t2, headx, ids, idx)
 
 
 def turn_kernel(total, out):
@@ -746,21 +816,22 @@
         conv_first, conv_second, bias_first, bias_second, head
     )
     own = own_splat(features, weights, tile_ids)
-    own, from_xlo, from_xhi, mid = lax.optimization_barrier((own, from_xlo, from_xhi, mid))
-    to_hi = jnp.stack([from_xlo[2], mid[2], from_xhi[2]])
-    to_lo = jnp.stack([from_xlo[0], mid[0], from_xhi[0]])
+    made = (t1a, t1o, t1r, t2a, t2b, headx, b1, b2)
+    own, made, from_xlo, from_xhi = lax.optimization_barrier((own, made, from_xlo, from_xhi))
+    t1a, t1o, t1r, t2a, t2b, headx, b1, b2 = made
+
+    g, idx, to_lo, to_hi, fwd_lo, fwd_hi, keep_lo, keep_hi = column(own, from_xlo, from_xhi, mid)
     from_ylo = step(to_hi, "gy", 1)
     from_yhi = step(to_lo, "gy", -1)
-    g, ylo, yhi, ids = sum_tiles(own, from_ylo, from_yhi, from_xlo, from_xhi)
-
-    rlo = step(yhi, "gy", 1)
-    rhi = step(ylo, "gy", -1)
-    x, slo, shi = widen_y(g, rlo, rhi)
+    far_lo = step(fwd_hi, "gy", 2)
+    far_hi = step(fwd_lo, "gy", -2)
+    g, x, slo, shi, ids = sum_tiles(g, from_ylo, from_yhi, far_lo, far_hi, keep_lo, keep_hi)
+
     xlo = step(shi, "gx", 1)
     xhi = step(slo, "gx", -1)
     part, pre = inner_convs(x, g, t1a, t1o, b1, t2a, b2)
     total, table, ans_ylo, ans_yhi, ans_x = edge_convs(
-        xlo, xhi, part, pre, t1r, t2b, headx, ids
+        xlo, xhi, part, pre, t1r, t2b, headx, ids, idx
     )
 
     back_yhi = step(ans_ylo, "gy", -1)

time: 94 us -> 91.5 us (0.973)
  the two profiles are of different devices: /device:TPU:3 before, /device:TPU:5 now
where the time goes in v3:
time: 91.5 us; the launch traced here: 91.1 us
  starting transfers between devices  42.4 us (46%)
  Pallas kernels  41.9 us (46%)
  waiting for transfers between devices  4.85 us (5%)
  between operations  1.73 us (2%)
    ppermute x12, starting transfers between devices, step(): lax.ppermute(x, axis, [(i, i + by) for i in range(size) if 0 <= i + by <...  42.4 us
    pallas_call x1, Pallas kernels, inner_convs(): pl.pallas_call(inner_kernel, in_specs=[vm] * 7, out_specs=[vm, vm], out_s...  8.19 us
    pallas_call x1, Pallas kernels, own_splat(): pl.pallas_call(own_splat_kernel, in_specs=[pl.BlockSpec(memory_space=SMEM...  6.45 us
    pallas_call x1, Pallas kernels, edge_convs(): pl.pallas_call(edge_kernel, in_specs=[vm] * 7 + [pl.BlockSpec(memory_spac...  6.28 us
    pallas_call x1, Pallas kernels, far_splat(): pl.pallas_call(far_splat_kernel, in_specs=[anywhere] * 5, out_specs=[vm,...  5.82 us
    ppermute x12, waiting for transfers between devices, step(): lax.ppermute(x, axis, [(i, i + by) for i in range(size) if 0 <= i + by <...  4.85 us
    pallas_call x1, Pallas kernels, own_read(): pl.pallas_call(own_read_kernel, in_specs=[pl.BlockSpec(memory_space=SMEM)...  4.28 us
    pallas_call x1, Pallas kernels, far_read(): pl.pallas_call(far_read_kernel, in_specs=[smem, smem] + [vm] * 6, out_spe...  2.76 us
  transfers between devices with their start and end apart: 12, of which 2 were waited for; matrix products, arithmetic and copies ran while one was open for 0% of the time, Pallas kernels for 25%

profile of v3, /device:TPU:5, one launch (start us, length us, event | category | flops | bytes accessed | tf_op | source)
XLA Modules:
  0.0 91.1 jit_solution(82959482035998118)
XLA Ops:
  1.3 5.8 %far_splat.1 = (bf16[3,528,128]{2,1,0:T(8,128)(2,1)}, bf16[3,528,128]{2,1,0:T(8,128)(2,1)}, bf16[3,528,128]{2,1,0:T(8,128)(2,1)}, s32[128]{0:T(128)}) custom-call(s32[256]{0:T(256)} %owners_h.1, s32[256]{0:T(256)} %ids.3, s32[1]{0:T(128)S(6)} %copy.17.counts_h.counts, bf16[32,32768]{1,0:T(8,128)(2,1)} %f_hbm.3, bf16[32768,128]{1,0:T(8,128)(2,1)} %w_hbm.5), custom_call_target="tpu_custom_call" | custom-call | flops 134217728 | bytes 6291456 | tf_op jit(solution)/shard_map/far_splat/pallas_call | solution.py:142
  7.1 3.2 %collective-permute-start = (bf16[3,528,128]{2,1,0:T(8,128)(2,1)}, bf16[3,528,128]{2,1,0:T(8,128)(2,1)S(1)}, u32[]{:S(2)}, u32[]{:S(2)}) collective-permute-start(bf16[3,528,128]{2,1,0:T(8,128)(2,1)} %get-tuple-element.58), channel_id=1, source_target_pairs={{0,8},{8,16},{16,24},{24,32},{32,40},{40,48},{48,56},{56,64},{64,7... | collective-permute-start | bytes 1216520 | tf_op jit(solution)/shard_map/ppermute | solution.py:808
  10.4 0.0 copy-start.1
  10.4 0.0 copy-start.2
  10.4 0.0 copy-start.4
  10.4 0.0 copy-start.5
  10.4 0.0 copy-start.7
  10.4 0.0 copy-start.8
  10.4 0.0 copy-start.10
  10.5 0.0 copy-start.11
  10.5 4.3 %collective-permute-start.1 = (bf16[3,528,128]{2,1,0:T(8,128)(2,1)}, bf16[3,528,128]{2,1,0:T(8,128)(2,1)S(1)}, u32[]{:S(2)}, u32[]{:S(2)}) collective-permute-start(bf16[3,528,128]{2,1,0:T(8,128)(2,1)} %get-tuple-element.59), channel_id=1, source_target_pairs={{8,0},{16,8},{24,16},{32,24},{40,32},{48,40},{56,48},{64,56},{72,6... | collective-permute-start | bytes 1216520 | tf_op jit(solution)/shard_map/ppermute | solution.py:808
  14.8 6.4 %own_splat.1.own = bf16[2,16,128,128]{3,2,1,0:T(8,128)(2,1)} custom-call(s32[256]{0:T(256)} %ids.3, bf16[32,32768]{1,0:T(8,128)(2,1)} %f_hbm.3, bf16[32768,128]{1,0:T(8,128)(2,1)} %w_hbm.5), custom_call_target="tpu_custom_call" | custom-call | flops 134217728 | bytes 6291456 | tf_op jit(solution)/shard_map/own_splat/pallas_call | solution.py:188
  21.3 1.7 %prepare.1 = (bf16[2304,256]{1,0:T(8,128)(2,1)S(1)}, bf16[3072,256]{1,0:T(8,128)(2,1)S(1)}, bf16[1536,256]{1,0:T(8,128)(2,1)S(1)}, bf16[2560,256]{1,0:T(8,128)(2...) custom-call(bf16[27,32,32]{2,1,0:T(8,128)(2,1)S(1)} %copy-done.6, ...), custom_call_target="tpu_custom_call" | custom-call | flops 471859200 | bytes 5242880 | tf_op jit(solution)/shard_map/prepare/pallas_call | solution.py:772
  23.1 2.3 %column.1 = (f32[2,16,128,128]{3,2,1,0:T(8,128)S(1)}, s32[8,128]{1,0:T(8,128)S(1)}, bf16[1648,128]{1,0:T(8,128)(2,1)S(1)}, bf16[1648,128]{1,0:T(8,128)(2,1)S(1)}...) custom-call(bf16[2,16,128,128]{3,2,1,0:T(8,128)(2,1)S(1)} %copy-done, ...), custom_call_target="tpu_custom_call" | custom-call | flops 1000 | bytes 4194304 | tf_op jit(solution)/shard_map/column/pallas_call | solution.py:271
  25.4 5.0 %collective-permute-start.2 = (bf16[1648,128]{1,0:T(8,128)(2,1)S(1)}, bf16[1648,128]{1,0:T(8,128)(2,1)S(1)}, u32[]{:S(2)}, u32[]{:S(2)}) collective-permute-start(bf16[1648,128]{1,0:T(8,128)(2,1)S(1)} %get-tuple-element.65), channel_id=1, source_target_pairs={{0,1},{1,2},{2,3},{3,4},{4,5},{5,6},{6,7},{8,9},{9,10},{10,11},{11... | collective-permute-start | bytes 1265672 | tf_op jit(solution)/shard_map/ppermute | solution.py:808
  30.4 1.9 %collective-permute-start.3 = (bf16[1648,128]{1,0:T(8,128)(2,1)S(1)}, bf16[1648,128]{1,0:T(8,128)(2,1)S(1)}, u32[]{:S(2)}, u32[]{:S(2)}) collective-permute-start(bf16[1648,128]{1,0:T(8,128)(2,1)S(1)} %get-tuple-element.66), channel_id=1, source_target_pairs={{1,0},{2,1},{3,2},{4,3},{5,4},{6,5},{7,6},{9,8},{10,9},{11,10},{12... | collective-permute-start | bytes 1265672 | tf_op jit(solution)/shard_map/ppermute | solution.py:808
  32.3 3.6 %collective-permute-start.4 = (bf16[4,16,128]{2,1,0:T(8,128)(2,1)S(1)}, bf16[4,16,128]{2,1,0:T(8,128)(2,1)S(1)}, u32[]{:S(2)}, u32[]{:S(2)}) collective-permute-start(bf16[4,16,128]{2,1,0:T(8,128)(2,1)S(1)} %get-tuple-element.67), channel_id=1, source_target_pairs={{0,2},{1,3},{2,4},{3,5},{4,6},{5,7},{8,10},{9,11},{10,12},{11,13},... | collective-permute-start | bytes 49160 | tf_op jit(solution)/shard_map/ppermute | solution.py:808
  35.9 1.3 %collective-permute-start.5 = (bf16[4,16,128]{2,1,0:T(8,128)(2,1)S(1)}, bf16[4,16,128]{2,1,0:T(8,128)(2,1)S(1)}, u32[]{:S(2)}, u32[]{:S(2)}) collective-permute-start(bf16[4,16,128]{2,1,0:T(8,128)(2,1)S(1)} %get-tuple-element.68), channel_id=1, source_target_pairs={{2,0},{3,1},{4,2},{5,3},{6,4},{7,5},{10,8},{11,9},{12,10},{13,11},... | collective-permute-start | bytes 49160 | tf_op jit(solution)/shard_map/ppermute | solution.py:808
  37.2 3.2 %collective-permute-done.5.far_hi = bf16[4,16,128]{2,1,0:T(8,128)(2,1)S(1)} collective-permute-done((bf16[4,16,128]{2,1,0:T(8,128)(2,1)S(1)}, bf16[4,16,128]{2,1,0:T(8,128)(2,1)S(1)}, u32[]{:S(2)}, u32[]{:S(2)}) %collective-permute-start.5) | collective-permute-done | bytes 16416 | tf_op jit(solution)/shard_map/ppermute | solution.py:808
  40.4 2.4 %sum_tiles.1 = (bf16[2,16,128,128]{3,2,1,0:T(8,128)(2,1)S(1)}, bf16[2,16,144,128]{3,2,1,0:T(8,128)(2,1)S(1)}, bf16[8,144,128]{2,1,0:T(8,128)(2,1)S(1)}, bf16[8,144,128]{2,1,0:T(8,128)(2,1)S(1)}, s32[8,128]{1,0:T(8,128)S(1)}) custom-call(f32[2,16,128,128]{3,2,1,0:T(8,128)S(1)} %get-tuple-element.64.part, bf16[1648,128]{1,0:T(8,128)(2,1)S(1)} %collective-permute-done.2.ylo, ...), custom_call_target="tpu_custom_call" | custom-call | flops 1000 | bytes 4194304 | tf_op jit(solution)/shard_map/sum_tiles/pallas_call | solution.py:341
  42.8 3.0 %collective-permute-start.6 = (bf16[8,144,128]{2,1,0:T(8,128)(2,1)S(1)}, bf16[8,144,128]{2,1,0:T(8,128)(2,1)S(1)}, u32[]{:S(2)}, u32[]{:S(2)}) collective-permute-start(bf16[8,144,128]{2,1,0:T(8,128)(2,1)S(1)} %get-tuple-element.71), channel_id=1, source_target_pairs={{0,8},{8,16},{16,24},{24,32},{32,40},{40,48},{48,56},{56,64},{64,7... | collective-permute-start | bytes 884744 | tf_op jit(solution)/shard_map/ppermute | solution.py:808
  45.8 5.2 %collective-permute-start.7 = (bf16[8,144,128]{2,1,0:T(8,128)(2,1)S(1)}, bf16[8,144,128]{2,1,0:T(8,128)(2,1)S(1)}, u32[]{:S(2)}, u32[]{:S(2)}) collective-permute-start(bf16[8,144,128]{2,1,0:T(8,128)(2,1)S(1)} %get-tuple-element.72), channel_id=1, source_target_pairs={{8,0},{16,8},{24,16},{32,24},{40,32},{48,40},{56,48},{64,56},{72,6... | collective-permute-start | bytes 884744 | tf_op jit(solution)/shard_map/ppermute | solution.py:808
  51.0 8.2 %inner_convs.1 = (f32[8,2,128,256]{3,2,1,0:T(8,128)S(1)}, f32[2,576,256]{2,1,0:T(8,128)S(1)}) custom-call(bf16[2,16,144,128]{3,2,1,0:T(8,128)(2,1)S(1)} %get-tuple-element.73.x, bf16[2,8,2,128,128]{4,3,2,1,0:T(8,128)(2,1)S(1)} %bitcast.11, bf16[2304,256]{1,0:T(8,128)(2,1)S(1)} %get-tuple-element.75.t1, bf16[3072,256]{1,0:T(8,128)(2,1)S(1)} %get-tuple-element.76.t1o, ...), custom_call_target="tpu_custom_call" | custom-call | flops 6039797760 | bytes 6291456 | tf_op jit(solution)/shard_map/inner_convs/pallas_call | solution.py:425
  59.2 6.3 %edge_convs.1 = (bf16[8,2,128,256]{3,2,1,0:T(8,128)(2,1)S(1)}, f32[128,8,128]{2,1,0:T(8,128)S(1)}, bf16[3,64,128]{2,1,0:T(8,128)(2,1)S(1)}, bf16[3,64,128]{2,1,0:T(8,128)(2,1)S(1)}, bf16[2,64,128]{2,1,0:T(8,128)(2,1)S(1)}) custom-call(bf16[8,144,128]{2,1,0:T(8,128)(2,1)S(1)} %collective-permute-done.6.rlo, ...), custom_call_target="tpu_custom_call" | custom-call | flops 2717908992 | bytes 6291456 | tf_op jit(solution)/shard_map/edge_convs/pallas_call | solution.py:538
  65.5 5.3 %collective-permute-start.8 = (bf16[3,64,128]{2,1,0:T(8,128)(2,1)S(1)}, bf16[3,64,128]{2,1,0:T(8,128)(2,1)S(1)}, u32[]{:S(2)}, u32[]{:S(2)}) collective-permute-start(bf16[3,64,128]{2,1,0:T(8,128)(2,1)S(1)} %get-tuple-element.88), channel_id=1, source_target_pairs={{0,1},{1,2},{2,3},{3,4},{4,5},{5,6},{6,7},{8,9},{9,10},{10,11},{11... | collective-permute-start | bytes 147464 | tf_op jit(solution)/shard_map/ppermute | solution.py:808
  70.9 1.9 %collective-permute-start.9 = (bf16[3,64,128]{2,1,0:T(8,128)(2,1)S(1)}, bf16[3,64,128]{2,1,0:T(8,128)(2,1)S(1)}, u32[]{:S(2)}, u32[]{:S(2)}) collective-permute-start(bf16[3,64,128]{2,1,0:T(8,128)(2,1)S(1)} %get-tuple-element.89), channel_id=1, source_target_pairs={{1,0},{2,1},{3,2},{4,3},{5,4},{6,5},{7,6},{9,8},{10,9},{11,10},{12... | collective-permute-start | bytes 147464 | tf_op jit(solution)/shard_map/ppermute | solution.py:808
  72.8 1.8 %turn.1 = bf16[32,16,8,128]{3,2,1,0:T(8,128)(2,1)} custom-call(bf16[8,2,128,256]{3,2,1,0:T(8,128)(2,1)S(1)} %get-tuple-element.87.total), custom_call_target="tpu_custom_call" | custom-call | flops 1000 | bytes 8388608 | tf_op jit(solution)/shard_map/turn/pallas_call | solution.py:566
  74.6 1.7 %collective-permute-done.9.yhi = bf16[3,64,128]{2,1,0:T(8,128)(2,1)S(1)} collective-permute-done((bf16[3,64,128]{2,1,0:T(8,128)(2,1)S(1)}, bf16[3,64,128]{2,1,0:T(8,128)(2,1)S(1)}, u32[]{:S(2)}, u32[]{:S(2)}) %collective-permute-start.9) | collective-permute-done | bytes 49184 | tf_op jit(solution)/shard_map/ppermute | solution.py:808
  76.3 1.9 %collective-permute-start.10 = (bf16[3,64,128]{2,1,0:T(8,128)(2,1)S(1)}, bf16[3,64,128]{2,1,0:T(8,128)(2,1)S(1)}, u32[]{:S(2)}, u32[]{:S(2)}) collective-permute-start(bf16[3,64,128]{2,1,0:T(8,128)(2,1)S(1)} %pad_maximum_fusion), channel_id=1, source_target_pairs={{0,8},{8,16},{16,24},{24,32},{32,40},{40,48},{48,56},{56,64},{64,7... | collective-permute-start | bytes 147464 | tf_op jit(solution)/shard_map/ppermute | solution.py:808
  78.3 5.7 %collective-permute-start.11 = (bf16[3,64,128]{2,1,0:T(8,128)(2,1)S(1)}, bf16[3,64,128]{2,1,0:T(8,128)(2,1)S(1)}, u32[]{:S(2)}, u32[]{:S(2)}) collective-permute-start(bf16[3,64,128]{2,1,0:T(8,128)(2,1)S(1)} %pad_maximum_fusion.1), channel_id=1, source_target_pairs={{8,0},{16,8},{24,16},{32,24},{40,32},{48,40},{56,48},{64,56},{72,6... | collective-permute-start | bytes 147464 | tf_op jit(solution)/shard_map/ppermute | solution.py:808
  84.0 4.3 %own_read.1 = (f32[3,16384]{1,0:T(4,128)S(1)}, bf16[16384,128]{1,0:T(8,128)(2,1)S(1)}) custom-call(s32[256]{0:T(256)S(1)} %copy-done.9, f32[128,8,128]{2,1,0:T(8,128)S(1)} %get-tuple-element.95.table, bf16[32768,128]{1,0:T(8,128)(2,1)} %w_hbm.5), custom_call_target="tpu_custom_call" | custom-call | flops 134217728 | bytes 9437184 | tf_op jit(solution)/shard_map/own_read/pallas_call | solution.py:634
  88.3 2.8 %far_read.1 = f32[3,32768]{1,0:T(4,128)} custom-call(s32[128]{0:T(128)S(1)} %copy-done.13, s32[1]{0:T(128)S(6)} %copy.17.counts_h.counts, bf16[3,64,128]{2,1,0:T(8,128)(2,1)S(1)} %collective-permute-done.10.blo, bf16[3,64,128]{2,1,0:T(8,128)(2,1)S(1)} %collective-permute-done.11.bhi, bf16[3,64,128]{2,1,0:T(8,128)(2,1)S(1)} %collective-permute-done.8.ylo, ...), custom_call_target="tpu_custom_call" | custom-call | flops 134217728 | bytes 5242880 | tf_op jit(solution)/shard_map/far_read/pallas_call | solution.py:680
  (34 shorter events, 0.1 us)
Async XLA Ops:
  7.1 15.9 %collective-permute-start = (bf16[3,528,128]{2,1,0:T(8,128)(2,1)}, bf16[3,528,128]{2,1,0:T(8,128)(2,1)S(1)}, u32[]{:S(2)}, u32[]{:S(2)}) collective-permute-start(bf16[3,528,128]{2,1,0:T(8,128)(2,1)} %get-tuple-element.58), channel_id=1, source_target_pairs={{0,8},{8,16},{16,24},{24,32},{32,40},{40,48},{48,56},{56,64},{64,7... | collective-permute-start | bytes 1216520 | tf_op jit(solution)/shard_map/ppermute | solution.py:808
  10.4 10.9 %copy-start.1 = (bf16[128,2048]{1,0:T(8,128)(2,1)S(1)}, bf16[128,2048]{1,0:T(8,128)(2,1)}, u32[]{:S(2)}) copy-start(bf16[128,2048]{1,0:T(8,128)(2,1)} %constant.13.clone.e2a) | copy-start | bytes 1572868
  10.4 10.9 %copy-start.2 = (bf16[128,2048]{1,0:T(8,128)(2,1)S(1)}, bf16[128,2048]{1,0:T(8,128)(2,1)}, u32[]{:S(2)}) copy-start(bf16[128,2048]{1,0:T(8,128)(2,1)} %constant.10.clone.e1a) | copy-start | bytes 1572868
  10.4 10.9 %copy-start.4 = (bf16[128,1024]{1,0:T(8,128)(2,1)S(1)}, bf16[128,1024]{1,0:T(8,128)(2,1)}, u32[]{:S(2)}) copy-start(bf16[128,1024]{1,0:T(8,128)(2,1)} %constant.14.clone.e2b) | copy-start | bytes 786436
  10.4 10.9 %copy-start.5 = (bf16[128,1024]{1,0:T(8,128)(2,1)S(1)}, bf16[128,1024]{1,0:T(8,128)(2,1)}, u32[]{:S(2)}) copy-start(bf16[128,1024]{1,0:T(8,128)(2,1)} %constant.11.clone.e1o) | copy-start | bytes 786436
  10.4 10.9 %copy-start.6 = (bf16[27,32,32]{2,1,0:T(8,128)(2,1)S(1)}, bf16[27,32,32]{2,1,0:T(8,128)(2,1)}, u32[]{:S(2)}) copy-start(bf16[27,32,32]{2,1,0:T(8,128)(2,1)} %c1.1) | copy-start | bytes 165892
  10.4 10.9 %copy-start.7 = (bf16[27,32,32]{2,1,0:T(8,128)(2,1)S(1)}, bf16[27,32,32]{2,1,0:T(8,128)(2,1)}, u32[]{:S(2)}) copy-start(bf16[27,32,32]{2,1,0:T(8,128)(2,1)} %c2.1) | copy-start | bytes 165892
  10.4 10.9 %copy-start.8 = (bf16[128,512]{1,0:T(8,128)(2,1)S(1)}, bf16[128,512]{1,0:T(8,128)(2,1)}, u32[]{:S(2)}) copy-start(bf16[128,512]{1,0:T(8,128)(2,1)} %constant.12.clone.e1r) | copy-start | bytes 393220
  10.4 10.9 %copy-start.10 = (bf16[3,32]{1,0:T(4,128)(2,1)S(1)}, bf16[3,32]{1,0:T(4,128)(2,1)}, u32[]{:S(2)}) copy-start(bf16[3,32]{1,0:T(4,128)(2,1)} %head.1) | copy-start | bytes 580
  10.5 10.9 %copy-start.11 = (f32[32]{0:T(128)S(1)}, f32[32]{0:T(128)}, u32[]{:S(2)}) copy-start(f32[32]{0:T(128)} %param.21) | copy-start | bytes 388
  10.5 10.9 %copy-start.12 = (f32[32]{0:T(128)S(1)}, f32[32]{0:T(128)}, u32[]{:S(2)}) copy-start(f32[32]{0:T(128)} %param.23) | copy-start | bytes 388
  10.5 12.6 %collective-permute-start.1 = (bf16[3,528,128]{2,1,0:T(8,128)(2,1)}, bf16[3,528,128]{2,1,0:T(8,128)(2,1)S(1)}, u32[]{:S(2)}, u32[]{:S(2)}) collective-permute-start(bf16[3,528,128]{2,1,0:T(8,128)(2,1)} %get-tuple-element.59), channel_id=1, source_target_pairs={{8,0},{16,8},{24,16},{32,24},{40,32},{48,40},{56,48},{64,56},{72,6... | collective-permute-start | bytes 1216520 | tf_op jit(solution)/shard_map/ppermute | solution.py:808
  21.2 1.8 %copy-start = (bf16[2,16,128,128]{3,2,1,0:T(8,128)(2,1)S(1)}, bf16[2,16,128,128]{3,2,1,0:T(8,128)(2,1)}, u32[]{:S(2)}) copy-start(bf16[2,16,128,128]{3,2,1,0:T(8,128)(2,1)} %own_splat.1.own) | copy-start | bytes 3145732
  21.2 1.8 %copy-start.3 = (bf16[3,528,128]{2,1,0:T(8,128)(2,1)S(1)}, bf16[3,528,128]{2,1,0:T(8,128)(2,1)}, u32[]{:S(2)}) copy-start(bf16[3,528,128]{2,1,0:T(8,128)(2,1)} %get-tuple-element.63) | copy-start | bytes 1216516
  25.4 15.0 %collective-permute-start.2 = (bf16[1648,128]{1,0:T(8,128)(2,1)S(1)}, bf16[1648,128]{1,0:T(8,128)(2,1)S(1)}, u32[]{:S(2)}, u32[]{:S(2)}) collective-permute-start(bf16[1648,128]{1,0:T(8,128)(2,1)S(1)} %get-tuple-element.65), channel_id=1, source_target_pairs={{0,1},{1,2},{2,3},{3,4},{4,5},{5,6},{6,7},{8,9},{9,10},{10,11},{11... | collective-permute-start | bytes 1265672 | tf_op jit(solution)/shard_map/ppermute | solution.py:808
  30.4 10.0 %collective-permute-start.3 = (bf16[1648,128]{1,0:T(8,128)(2,1)S(1)}, bf16[1648,128]{1,0:T(8,128)(2,1)S(1)}, u32[]{:S(2)}, u32[]{:S(2)}) collective-permute-start(bf16[1648,128]{1,0:T(8,128)(2,1)S(1)} %get-tuple-element.66), channel_id=1, source_target_pairs={{1,0},{2,1},{3,2},{4,3},{5,4},{6,5},{7,6},{9,8},{10,9},{11,10},{12... | collective-permute-start | bytes 1265672 | tf_op jit(solution)/shard_map/ppermute | solution.py:808
  32.3 4.9 %collective-permute-start.4 = (bf16[4,16,128]{2,1,0:T(8,128)(2,1)S(1)}, bf16[4,16,128]{2,1,0:T(8,128)(2,1)S(1)}, u32[]{:S(2)}, u32[]{:S(2)}) collective-permute-start(bf16[4,16,128]{2,1,0:T(8,128)(2,1)S(1)} %get-tuple-element.67), channel_id=1, source_target_pairs={{0,2},{1,3},{2,4},{3,5},{4,6},{5,7},{8,10},{9,11},{10,12},{11,13},... | collective-permute-start | bytes 49160 | tf_op jit(solution)/shard_map/ppermute | solution.py:808
  35.9 4.5 %collective-permute-start.5 = (bf16[4,16,128]{2,1,0:T(8,128)(2,1)S(1)}, bf16[4,16,128]{2,1,0:T(8,128)(2,1)S(1)}, u32[]{:S(2)}, u32[]{:S(2)}) collective-permute-start(bf16[4,16,128]{2,1,0:T(8,128)(2,1)S(1)} %get-tuple-element.68), channel_id=1, source_target_pairs={{2,0},{3,1},{4,2},{5,3},{6,4},{7,5},{10,8},{11,9},{12,10},{13,11},... | collective-permute-start | bytes 49160 | tf_op jit(solution)/shard_map/ppermute | solution.py:808
  42.8 16.4 %collective-permute-start.6 = (bf16[8,144,128]{2,1,0:T(8,128)(2,1)S(1)}, bf16[8,144,128]{2,1,0:T(8,128)(2,1)S(1)}, u32[]{:S(2)}, u32[]{:S(2)}) collective-permute-start(bf16[8,144,128]{2,1,0:T(8,128)(2,1)S(1)} %get-tuple-element.71), channel_id=1, source_target_pairs={{0,8},{8,16},{16,24},{24,32},{32,40},{40,48},{48,56},{56,64},{64,7... | collective-permute-start | bytes 884744 | tf_op jit(solution)/shard_map/ppermute | solution.py:808
  45.8 13.4 %collective-permute-start.7 = (bf16[8,144,128]{2,1,0:T(8,128)(2,1)S(1)}, bf16[8,144,128]{2,1,0:T(8,128)(2,1)S(1)}, u32[]{:S(2)}, u32[]{:S(2)}) collective-permute-start(bf16[8,144,128]{2,1,0:T(8,128)(2,1)S(1)} %get-tuple-element.72), channel_id=1, source_target_pairs={{8,0},{16,8},{24,16},{32,24},{40,32},{48,40},{56,48},{64,56},{72,6... | collective-permute-start | bytes 884744 | tf_op jit(solution)/shard_map/ppermute | solution.py:808
  65.5 18.4 %copy-start.9 = (s32[256]{0:T(256)S(1)}, s32[256]{0:T(256)}, u32[]{:S(2)}) copy-start(s32[256]{0:T(256)} %ids.3) | copy-start | bytes 3076
  65.5 9.1 %collective-permute-start.8 = (bf16[3,64,128]{2,1,0:T(8,128)(2,1)S(1)}, bf16[3,64,128]{2,1,0:T(8,128)(2,1)S(1)}, u32[]{:S(2)}, u32[]{:S(2)}) collective-permute-start(bf16[3,64,128]{2,1,0:T(8,128)(2,1)S(1)} %get-tuple-element.88), channel_id=1, source_target_pairs={{0,1},{1,2},{2,3},{3,4},{4,5},{5,6},{6,7},{8,9},{9,10},{10,11},{11... | collective-permute-start | bytes 147464 | tf_op jit(solution)/shard_map/ppermute | solution.py:808
  70.9 5.4 %collective-permute-start.9 = (bf16[3,64,128]{2,1,0:T(8,128)(2,1)S(1)}, bf16[3,64,128]{2,1,0:T(8,128)(2,1)S(1)}, u32[]{:S(2)}, u32[]{:S(2)}) collective-permute-start(bf16[3,64,128]{2,1,0:T(8,128)(2,1)S(1)} %get-tuple-element.89), channel_id=1, source_target_pairs={{1,0},{2,1},{3,2},{4,3},{5,4},{6,5},{7,6},{9,8},{10,9},{11,10},{12... | collective-permute-start | bytes 147464 | tf_op jit(solution)/shard_map/ppermute | solution.py:808
  76.3 12.0 %collective-permute-start.10 = (bf16[3,64,128]{2,1,0:T(8,128)(2,1)S(1)}, bf16[3,64,128]{2,1,0:T(8,128)(2,1)S(1)}, u32[]{:S(2)}, u32[]{:S(2)}) collective-permute-start(bf16[3,64,128]{2,1,0:T(8,128)(2,1)S(1)} %pad_maximum_fusion), channel_id=1, source_target_pairs={{0,8},{8,16},{16,24},{24,32},{32,40},{40,48},{48,56},{56,64},{64,7... | collective-permute-start | bytes 147464 | tf_op jit(solution)/shard_map/ppermute | solution.py:808
  78.3 10.0 %collective-permute-start.11 = (bf16[3,64,128]{2,1,0:T(8,128)(2,1)S(1)}, bf16[3,64,128]{2,1,0:T(8,128)(2,1)S(1)}, u32[]{:S(2)}, u32[]{:S(2)}) collective-permute-start(bf16[3,64,128]{2,1,0:T(8,128)(2,1)S(1)} %pad_maximum_fusion.1), channel_id=1, source_target_pairs={{8,0},{16,8},{24,16},{32,24},{40,32},{48,40},{56,48},{64,56},{72,6... | collective-permute-start | bytes 147464 | tf_op jit(solution)/shard_map/ppermute | solution.py:808
  84.0 4.3 %copy-start.13 = (s32[128]{0:T(128)S(1)}, s32[128]{0:T(128)}, u32[]{:S(2)}) copy-start(s32[128]{0:T(128)} %get-tuple-element.91.slots) | copy-start | bytes 1540

commit v4 on v3

--- a/solution.py
+++ b/solution.py
@@ -35,6 +35,10 @@
 
 def cost(flops, nbytes):
     return pl.CostEstimate(flops=flops, bytes_accessed=nbytes, transcendentals=0)
+
+
+def upward(i):
+    return jnp.where(i % 2 == 0, 2, 0)
 
 
 def splat_four(f, w_ref, first):
@@ -80,7 +84,7 @@
 
 
 def far_splat_kernel(
-    owners_h, ids_h, counts_h, f_hbm, w_hbm, lo, mid, hi, slots,
+    owners_h, ids_h, counts_h, f_hbm, w_hbm, out_a, mid, out_b, slots,
     fv, wv, tiles, idrows, filled, owners, ids, counts, sems, isems,
 ):
     ix = lax.axis_index("gx")
@@ -124,14 +128,13 @@
             idrows[pl.ds(target, 1), :] = jnp.where(
                 lane == rank, ids[128 + block].astype(F32), row
             )
-    for dx, out in enumerate((lo, mid, hi)):
+    toward = upward(ix)
+    for dx, out in ((toward, out_a), (1, mid), (2 - toward, out_b)):
         for dy in range(3):
             k = dx * 3 + dy
-            out[dy, 0 : SLOTS * 32, :] = tiles[k * SLOTS : (k + 1) * SLOTS].reshape(
-                SLOTS * 32, 128
-            )
+            out[dy, 0 : SLOTS * 32, :] = tiles[pl.ds(k * SLOTS, SLOTS)].reshape(SLOTS * 32, 128)
             out[dy, SLOTS * 32 : PAY, :] = jnp.broadcast_to(
-                idrows[k : k + 1, :], (16, 128)
+                idrows[pl.ds(k, 1), :], (16, 128)
             ).astype(BF16)
 
 
@@ -206,7 +209,7 @@
 
 
 def ids_of(groups):
-    rows = [ref[at + SLOTS * 32 : at + PAY, :].astype(F32)[0:1] for ref, at in groups]
+    rows = [ref[pl.ds(at + SLOTS * 32, 16), :].astype(F32)[0:1] for ref, at in groups]
     return jnp.concatenate(rows, 0).astype(jnp.int32)
 
 
@@ -225,19 +228,22 @@
 
 
 def column_kernel(
-    own, xlo, xhi, mid, g, ids, to_lo, to_hi, fwd_lo, fwd_hi, keep_lo, keep_hi, acc, idv, sem
+    own, xa, xb, mid, g, ids, to_a, to_b, fwd_a, fwd_b, keep_lo, keep_hi, acc, idv, sem
 ):
-    zero, one, two = 0, PAY, 2 * PAY
-    groups = [(xlo, one), (xhi, one)]
-    groups += [(xlo, two), (mid, two), (xhi, two), (xlo, zero), (mid, zero), (xhi, zero)]
+    iy = lax.axis_index("gy")
+    even = iy % 2 == 0
+    first = pl.multiple_of(upward(iy) * PAY, 16)
+    second = pl.multiple_of((2 - upward(iy)) * PAY, 16)
+    groups = [(xa, PAY), (xb, PAY)]
+    groups += [(xa, first), (mid, first), (xb, first), (xa, second), (mid, second), (xb, second)]
     idv[...] = ids_of(groups)
     copy = pltpu.make_async_copy(idv, ids, sem)
     copy.start()
     g[...] = own[...].astype(F32)
     acc[...] = jnp.zeros_like(acc)
     for n, (ref, at) in enumerate(groups[2:]):
-        out, k = (to_hi, n) if n < 3 else (to_lo, n - 3)
-        out[k * PAY : (k + 1) * PAY, :] = ref[at : at + PAY, :]
+        out, k = (to_a, n) if n < 3 else (to_b, n - 3)
+        out[k * PAY : (k + 1) * PAY, :] = ref[pl.ds(at, PAY), :]
     copy.wait()
     for n, (ref, at) in enumerate(groups):
         if n < 2:
@@ -252,22 +258,28 @@
             return carry
 
         lax.fori_loop(0, SLOTS, add, 0, unroll=4)
+    above = jnp.where(even, 0, 3)
+    below = 3 - above
     for tx in range(2):
         for r in range(2):
             k = tx * 2 + r
             rows = slice(3 * PAY + k * 16, 3 * PAY + k * 16 + 16)
-            to_lo[rows, :] = g[tx, :, r, :].astype(BF16)
-            to_hi[rows, :] = g[tx, :, BY - 2 + r, :].astype(BF16)
-            keep_hi[k] = acc[0, tx, :, r, :]
-            fwd_hi[k] = acc[1, tx, :, 6 + r, :].astype(BF16)
-            fwd_lo[k] = acc[3, tx, :, r, :].astype(BF16)
-            keep_lo[k] = acc[4, tx, :, 6 + r, :]
-
-
-def column(own, xlo, xhi, mid):
+            low, high = g[tx, :, r, :], g[tx, :, BY - 2 + r, :]
+            to_a[rows, :] = jnp.where(even, high, low).astype(BF16)
+            to_b[rows, :] = jnp.where(even, low, high).astype(BF16)
+            keep_hi[k] = acc[above, tx, :, r, :]
+            keep_lo[k] = acc[below + 1, tx, :, 6 + r, :]
+            high = acc[above + 1, tx, :, 6 + r, :]
+            low = acc[below, tx, :, r, :]
+            up = (iy >> 1) % 2 == 0
+            fwd_a[k] = jnp.where(up, high, low).astype(BF16)
+            fwd_b[k] = jnp.where(up, low, high).astype(BF16)
+
+
+def column(own, xa, xb, mid):
     vm = pl.BlockSpec(memory_space=VMEM)
     bundle = jax.ShapeDtypeStruct((BUNDLE, 128), BF16)
-    flat = [v.reshape(3 * PAY, 128) for v in (xlo, xhi, mid)]
+    flat = [v.reshape(3 * PAY, 128) for v in (xa, xb, mid)]
     return pl.pallas_call(
         column_kernel,
         in_specs=[vm] * 4,
@@ -294,9 +306,13 @@
 
 
 def sum_kernel(
-    part, ylo, yhi, far_lo, far_hi, keep_lo, keep_hi, g, x, slo, shi, ids, grid, edge, idv, sem
+    part, ya, yb, far_a, far_b, keep_lo, keep_hi, g, x, to_a, to_b, ids, grid, edge, idv, sem
 ):
-    groups = [(ref, k * PAY) for ref in (ylo, yhi) for k in range(3)]
+    even_x = lax.axis_index("gx") % 2 == 0
+    iy = lax.axis_index("gy")
+    even = iy % 2 == 0
+    up = (iy >> 1) % 2 == 0
+    groups = [(ref, k * PAY) for ref in (ya, yb) for k in range(3)]
     idv[0:6, :] = ids_of(groups)
     idv[6:8, :] = jnp.zeros((2, 128), jnp.int32)
     copy = pltpu.make_async_copy(idv, ids, sem)
@@ -307,10 +323,14 @@
         for r in range(2):
             k = tx * 2 + r
             rows = slice(3 * PAY + k * 16, 3 * PAY + k * 16 + 16)
-            low = ylo[rows, :].astype(F32) + far_lo[k].astype(F32) + keep_lo[k]
-            high = yhi[rows, :].astype(F32) + far_hi[k].astype(F32) + keep_hi[k]
-            edge[tx, 0, :, 6 + r, :] = low
-            edge[tx, 1, :, r, :] = high
+            near_a, near_b = ya[rows, :].astype(F32), yb[rows, :].astype(F32)
+            away_a, away_b = far_a[k].astype(F32), far_b[k].astype(F32)
+            low = jnp.where(iy >= 2, jnp.where(up, away_b, away_a), 0.0)
+            low = low + jnp.where(even, near_b, near_a) + keep_lo[k]
+            high = jnp.where(iy < 6, jnp.where(up, away_a, away_b), 0.0)
+            high = high + jnp.where(even, near_a, near_b) + keep_hi[k]
+            edge[tx, 0, :, 6 + r, :] = jnp.where(iy > 0, low, 0.0)
+            edge[tx, 1, :, r, :] = jnp.where(iy < 7, high, 0.0)
     copy.wait()
     for n, (ref, at) in enumerate(groups):
         add_tiles(grid, ids, n, ref, at)
@@ -320,22 +340,25 @@
         return jnp.concatenate([edge[tx, 0, z], grid[tx, z], edge[tx, 1, z]], 0)
 
     def pair(z, carry):
-        for tx, ref in enumerate((slo, shi)):
+        sides = []
+        for tx in range(2):
             a, b = plane(tx, z), plane(tx, z + 8)
             x[tx, z] = a.astype(BF16)
             x[tx, z + 8] = b.astype(BF16)
             g[tx, z] = a[8 : 8 + BY].astype(BF16)
             g[tx, z + 8] = b[8 : 8 + BY].astype(BF16)
             if tx == 0:
-                ref[z] = jnp.where(lane < 64, a, pltpu.roll(b, 64, 1)).astype(BF16)
+                sides.append(jnp.where(lane < 64, a, pltpu.roll(b, 64, 1)))
             else:
-                ref[z] = jnp.where(lane < 64, pltpu.roll(a, 64, 1), b).astype(BF16)
+                sides.append(jnp.where(lane < 64, pltpu.roll(a, 64, 1), b))
+        to_a[z] = jnp.where(even_x, sides[1], sides[0]).astype(BF16)
+        to_b[z] = jnp.where(even_x, sides[0], sides[1]).astype(BF16)
         return carry
 
     lax.fori_loop(0, 8, pair, 0, unroll=2)
 
 
-def sum_tiles(part, ylo, yhi, far_lo, far_hi, keep_lo, keep_hi):
+def sum_tiles(part, ya, yb, far_a, far_b, keep_lo, keep_hi):
     vm = pl.BlockSpec(memory_space=VMEM)
     side = jax.ShapeDtypeStruct((SLAB // 2, ROWS, 128), BF16)
     return pl.pallas_call(
@@ -358,7 +381,7 @@
         compiler_params=params(16),
         cost_estimate=cost(1000, 4 * MIB),
         name="sum_tiles",
-    )(part, ylo, yhi, far_lo, far_hi, keep_lo, keep_hi)
+    )(part, ya, yb, far_a, far_b, keep_lo, keep_hi)
 
 
 def rows_inside(shape, iy):
@@ -445,7 +468,7 @@
 
 
 def edge_kernel(
-    rlo, rhi, part, pre, t1, t2, headx, ids, idx, total, table, ans_ylo, ans_yhi, ans_x, es, hs, vel
+    ra, rb, part, pre, t1, t2, headx, ids, idx, total, table, ans_ya, ans_yb, ans_x, es, hs, vel
 ):
     ix = lax.axis_index("gx")
     iy = lax.axis_index("gy")
@@ -456,8 +479,9 @@
         hs[dy, PAIRS, 1] = jnp.zeros((BY, 128), BF16)
     lane = lanes_of((1, ROWS, 128))
     for z in range(8):
-        a = rlo[z : z + 1].astype(F32)
-        b = rhi[z : z + 1].astype(F32)
+        va, vb = ra[z : z + 1].astype(F32), rb[z : z + 1].astype(F32)
+        a = jnp.where(ix > 0, jnp.where(ix % 2 == 0, vb, va), 0.0)
+        b = jnp.where(ix < 15, jnp.where(ix % 2 == 0, va, vb), 0.0)
         near = jnp.where(lane < 64, a, pltpu.roll(b, 64, 2))
         far = jnp.where(lane < 64, pltpu.roll(a, 64, 2), b)
         for zz, v in ((z, near), (z + 8, far)):
@@ -513,7 +537,7 @@
                     row = (tz * 4 + k * 2 + kk) * 8
                     table[row : row + 8, a, :] = w[tz]
 
-    places = [(ans_ylo, 0), (ans_ylo, 1), (ans_ylo, 2), (ans_yhi, 0), (ans_yhi, 1), (ans_yhi, 2)]
+    places = [(ans_ya, 0), (ans_ya, 1), (ans_ya, 2), (ans_yb, 0), (ans_yb, 1), (ans_yb, 2)]
     places += [(ans_x, 0), (ans_x, 1)]
     for n, (ref, k) in enumerate(places):
         source, row = (ids, n) if n < 6 else (idx, n - 6)
@@ -532,7 +556,7 @@
         lax.fori_loop(0, SLOTS // 4, answer, 0, unroll=4)
 
 
-def edge_convs(rlo, rhi, part, pre, t1, t2, headx, ids, idx):
+def edge_convs(ra, rb, part, pre, t1, t2, headx, ids, idx):
     vm = pl.BlockSpec(memory_space=VMEM)
     ans = jax.ShapeDtypeStruct((3, 64, 128), BF16)
     return pl.pallas_call(
@@ -554,7 +578,7 @@
         compiler_params=params(32),
         cost_estimate=cost(2 * 9 * 256 * 256 * 2304, 6 * MIB),
         name="edge_convs",
-    )(rlo, rhi, part, pre, t1, t2, headx, ids, idx)
+    )(ra, rb, part, pre, t1, t2, headx, ids, idx)
 
 
 def turn_kernel(total, out):
@@ -650,18 +674,19 @@
     )(ids, table, weights)
 
 
-def far_read_kernel(slots, counts, blo, bhi, ylo, yhi, w, near, out, table):
-    places = [(blo, 0), (blo, 1), (blo, 2), (ylo, 1), None, (yhi, 1)]
-    places += [(bhi, 0), (bhi, 1), (bhi, 2)]
-    for k, place in enumerate(places):
-        if place is None:
-            table[k * SLOTS : (k + 1) * SLOTS] = jnp.zeros((SLOTS, 8, 128), F32)
-            continue
-        v = place[0][place[1]].astype(F32).reshape(8, 8, 128)
+def far_read_kernel(slots, counts, xa, xb, ya, yb, w, near, out, table):
+    dx = upward(lax.axis_index("gx"))
+    dy = upward(lax.axis_index("gy"))
+    places = [(ya, 1, 3 + dy), (yb, 1, 5 - dy)]
+    for ref, d in ((xa, dx), (xb, 2 - dx)):
+        places += [(ref, 0, d * 3 + dy), (ref, 1, d * 3 + 1), (ref, 2, d * 3 + 2 - dy)]
+    table[4 * SLOTS : 5 * SLOTS] = jnp.zeros((SLOTS, 8, 128), F32)
+    for ref, k, place in places:
+        v = ref[k].astype(F32).reshape(8, 8, 128)
         turned = pltpu.roll(v, 4, 1)
         for j in range(8):
-            table[k * SLOTS + 2 * j] = v[j]
-            table[k * SLOTS + 2 * j + 1] = turned[j]
+            table[place * SLOTS + 2 * j] = v[j]
+            table[place * SLOTS + 2 * j + 1] = turned[j]
     half = near.shape[1]
     out[:, 0:half] = near[...]
     for k in range(128 // BATCH):
@@ -674,7 +699,7 @@
         )
 
 
-def far_read(slots, counts, blo, bhi, ylo, yhi, w, near):
+def far_read(slots, counts, xa, xb, ya, yb, w, near):
     vm = pl.BlockSpec(memory_space=VMEM)
     smem = pl.BlockSpec(memory_space=SMEM)
     return pl.pallas_call(
@@ -686,7 +711,7 @@
         compiler_params=params(24),
         cost_estimate=cost(2 * 128 * 32 * 128 * 128, 5 * MIB),
         name="far_read",
-    )(slots, counts, blo, bhi, ylo, yhi, w, near)
+    )(slots, counts, xa, xb, ya, yb, w, near)
 
 
 def band(pin, pout, out_last):
@@ -803,47 +828,44 @@
 ):
     particles = features.shape[1]
 
-    def step(x, axis, by):
+    def swap(x, axis, partner, reach=1):
         size = lax.axis_size(axis)
-        return lax.ppermute(
-            x, axis, [(i, i + by) for i in range(size) if 0 <= i + by < size]
-        )
-
-    lo, mid, hi, slots = far_splat(features, weights, owners, tile_ids, counts)
-    from_xlo = step(hi, "gx", 1)
-    from_xhi = step(lo, "gx", -1)
-    t1a, t1o, t1r, t2a, t2b, headx, b1, b2 = prepare(
-        conv_first, conv_second, bias_first, bias_second, head
-    )
+        route = []
+        for i in range(size):
+            up = (i // reach) % 2 == (0 if partner == "a" else 1)
+            route.append((i, (i + (reach if up else -reach)) % size))
+        return lax.ppermute(x, axis, route)
+
+    to_a, mid, to_b, slots = far_splat(features, weights, owners, tile_ids, counts)
+    from_xb = swap(to_b, "gx", "b")
+    from_xa = swap(to_a, "gx", "a")
+    made = prepare(conv_first, conv_second, bias_first, bias_second, head)
     own = own_splat(features, weights, tile_ids)
-    made = (t1a, t1o, t1r, t2a, t2b, headx, b1, b2)
-    own, made, from_xlo, from_xhi = lax.optimization_barrier((own, made, from_xlo, from_xhi))
+    own, made, from_xa, from_xb = lax.optimization_barrier((own, made, from_xa, from_xb))
     t1a, t1o, t1r, t2a, t2b, headx, b1, b2 = made
 
-    g, idx, to_lo, to_hi, fwd_lo, fwd_hi, keep_lo, keep_hi = column(own, from_xlo, from_xhi, mid)
-    from_ylo = step(to_hi, "gy", 1)
-    from_yhi = step(to_lo, "gy", -1)
-    far_lo = step(fwd_hi, "gy", 2)
-    far_hi = step(fwd_lo, "gy", -2)
-    g, x, slo, shi, ids = sum_tiles(g, from_ylo, from_yhi, far_lo, far_hi, keep_lo, keep_hi)
-
-    xlo = step(shi, "gx", 1)
-    xhi = step(slo, "gx", -1)
+    g, idx, to_a, to_b, fwd_a, fwd_b, keep_lo, keep_hi = column(own, from_xa, from_xb, mid)
+    from_ya = swap(to_a, "gy", "a")
+    from_yb = swap(to_b, "gy", "b")
+    far_a = swap(fwd_a, "gy", "a", 2)
+    far_b = swap(fwd_b, "gy", "b", 2)
+    g, x, to_a, to_b, ids = sum_tiles(g, from_ya, from_yb, far_a, far_b, keep_lo, keep_hi)
+
+    xb = swap(to_b, "gx", "b")
+    xa = swap(to_a, "gx", "a")
     part, pre = inner_convs(x, g, t1a, t1o, b1, t2a, b2)
-    total, table, ans_ylo, ans_yhi, ans_x = edge_convs(
-        xlo, xhi, part, pre, t1r, t2b, headx, ids, idx
-    )
-
-    back_yhi = step(ans_ylo, "gy", -1)
-    back_ylo = step(ans_yhi, "gy", 1)
+    total, table, ans_ya, ans_yb, ans_x = edge_convs(xa, xb, part, pre, t1r, t2b, headx, ids, idx)
+
+    back_ya = swap(ans_ya, "gy", "a")
+    back_yb = swap(ans_yb, "gy", "b")
     grid_out = turn(total)
-    grid_out, back_ylo, back_yhi = lax.optimization_barrier((grid_out, back_ylo, back_yhi))
+    grid_out, back_ya, back_yb = lax.optimization_barrier((grid_out, back_ya, back_yb))
     near, far_w = own_read(tile_ids, table, weights, particles)
-    to_lo = jnp.stack([back_ylo[0], ans_x[0], back_yhi[0]])
-    to_hi = jnp.stack([back_ylo[2], ans_x[1], back_yhi[2]])
-    back_xhi = step(to_lo, "gx", -1)
-    back_xlo = step(to_hi, "gx", 1)
-    velocity = far_read(slots, counts, back_xlo, back_xhi, back_ylo, back_yhi, far_w, near)
+    to_a = jnp.stack([back_ya[0], ans_x[0], back_yb[0]])
+    to_b = jnp.stack([back_ya[2], ans_x[1], back_yb[2]])
+    back_xb = swap(to_b, "gx", "b")
+    back_xa = swap(to_a, "gx", "a")
+    velocity = far_read(slots, counts, back_xa, back_xb, back_ya, back_yb, far_w, near)
     return grid_out, velocity
 
 

time: 91.5 us -> 74.7 us (0.82)
  the two profiles are of different devices: /device:TPU:5 before, /device:TPU:0 now
where the time goes in v4:
time: 74.7 us; the launch traced here: 74.6 us
  Pallas kernels  42.2 us (56%)
  starting transfers between devices  23.6 us (32%)
  waiting for transfers between devices  7.19 us (10%)
  between operations  1.6 us (2%)
    ppermute x12, starting transfers between devices, swap(): return lax.ppermute(x, axis, route)  23.6 us
    pallas_call x1, Pallas kernels, inner_convs(): pl.pallas_call(inner_kernel, in_specs=[vm] * 7, out_specs=[vm, vm], out_s...  8.18 us
    ppermute x12, waiting for transfers between devices, swap(): return lax.ppermute(x, axis, route)  7.19 us
    pallas_call x1, Pallas kernels, own_splat(): pl.pallas_call(own_splat_kernel, in_specs=[pl.BlockSpec(memory_space=SMEM...  6.4 us
    pallas_call x1, Pallas kernels, edge_convs(): pl.pallas_call(edge_kernel, in_specs=[vm] * 7 + [pl.BlockSpec(memory_spac...  6.38 us
    pallas_call x1, Pallas kernels, far_splat(): pl.pallas_call(far_splat_kernel, in_specs=[anywhere] * 5, out_specs=[vm,...  5.87 us
    pallas_call x1, Pallas kernels, own_read(): pl.pallas_call(own_read_kernel, in_specs=[pl.BlockSpec(memory_space=SMEM)...  4.28 us
    pallas_call x1, Pallas kernels, far_read(): pl.pallas_call(far_read_kernel, in_specs=[smem, smem] + [vm] * 6, out_spe...  2.77 us
  transfers between devices with their start and end apart: 12, of which 3 were waited for; matrix products, arithmetic and copies ran while one was open for 0% of the time, Pallas kernels for 30%

profile of v4, /device:TPU:0, one launch (start us, length us, event | category | flops | bytes accessed | tf_op | source)
XLA Modules:
  0.0 74.6 jit_solution(1236550344084137917)
XLA Ops:
  1.3 5.9 %far_splat.1 = (bf16[3,528,128]{2,1,0:T(8,128)(2,1)}, bf16[3,528,128]{2,1,0:T(8,128)(2,1)}, bf16[3,528,128]{2,1,0:T(8,128)(2,1)}, s32[128]{0:T(128)}) custom-call(s32[256]{0:T(256)} %owners_h.1, s32[256]{0:T(256)} %ids.3, s32[1]{0:T(128)S(6)} %copy.17.counts_h.counts, bf16[32,32768]{1,0:T(8,128)(2,1)} %f_hbm.3, bf16[32768,128]{1,0:T(8,128)(2,1)} %w_hbm.5), custom_call_target="tpu_custom_call" | custom-call | flops 134217728 | bytes 6291456 | tf_op jit(solution)/shard_map/far_splat/pallas_call | solution.py:145
  7.2 1.7 %collective-permute-start = (bf16[3,528,128]{2,1,0:T(8,128)(2,1)}, bf16[3,528,128]{2,1,0:T(8,128)(2,1)S(1)}, u32[]{:S(2)}, u32[]{:S(2)}) collective-permute-start(bf16[3,528,128]{2,1,0:T(8,128)(2,1)} %get-tuple-element.58), channel_id=1, source_target_pairs={{0,8},{8,0},{16,24},{24,16},{32,40},{40,32},{48,56},{56,48},{64,72... | collective-permute-start | bytes 1216520 | tf_op jit(solution)/shard_map/ppermute | solution.py:837
  8.9 0.0 copy-start.6
  8.9 0.0 copy-start.7
  8.9 0.0 copy-start.8
  8.9 0.0 copy-start.10
  8.9 0.0 copy-start.11
  8.9 0.0 copy-start.12
  9.0 4.5 %collective-permute-start.1 = (bf16[3,528,128]{2,1,0:T(8,128)(2,1)}, bf16[3,528,128]{2,1,0:T(8,128)(2,1)S(1)}, u32[]{:S(2)}, u32[]{:S(2)}) collective-permute-start(bf16[3,528,128]{2,1,0:T(8,128)(2,1)} %get-tuple-element.59), channel_id=1, source_target_pairs={{0,120},{8,16},{16,8},{24,32},{32,24},{40,48},{48,40},{56,64},{64,... | collective-permute-start | bytes 1216520 | tf_op jit(solution)/shard_map/ppermute | solution.py:837
  13.4 6.4 %own_splat.1.own = bf16[2,16,128,128]{3,2,1,0:T(8,128)(2,1)} custom-call(s32[256]{0:T(256)} %ids.3, bf16[32,32768]{1,0:T(8,128)(2,1)} %f_hbm.3, bf16[32768,128]{1,0:T(8,128)(2,1)} %w_hbm.5), custom_call_target="tpu_custom_call" | custom-call | flops 134217728 | bytes 6291456 | tf_op jit(solution)/shard_map/own_splat/pallas_call | solution.py:191
  19.8 0.0 copy-start
  20.0 1.7 %prepare.1 = (bf16[2304,256]{1,0:T(8,128)(2,1)S(1)}, bf16[3072,256]{1,0:T(8,128)(2,1)S(1)}, bf16[1536,256]{1,0:T(8,128)(2,1)S(1)}, bf16[2560,256]{1,0:T(8,128)(2...) custom-call(bf16[27,32,32]{2,1,0:T(8,128)(2,1)S(1)} %copy-done.6, ...), custom_call_target="tpu_custom_call" | custom-call | flops 471859200 | bytes 5242880 | tf_op jit(solution)/shard_map/prepare/pallas_call | solution.py:797
  21.7 1.7 %collective-permute-done.1 = bf16[3,528,128]{2,1,0:T(8,128)(2,1)S(1)} collective-permute-done((bf16[3,528,128]{2,1,0:T(8,128)(2,1)}, bf16[3,528,128]{2,1,0:T(8,128)(2,1)S(1)}, u32[]{:S(2)}, u32[]{:S(2)}) %collective-permute-start.1) | collective-permute-done | bytes 405536 | tf_op jit(solution)/shard_map/ppermute | solution.py:837
  23.4 2.4 %column.1 = (f32[2,16,128,128]{3,2,1,0:T(8,128)S(1)}, s32[8,128]{1,0:T(8,128)S(1)}, bf16[1648,128]{1,0:T(8,128)(2,1)S(1)}, bf16[1648,128]{1,0:T(8,128)(2,1)S(1)}...) custom-call(bf16[2,16,128,128]{3,2,1,0:T(8,128)(2,1)S(1)} %copy-done, ...), custom_call_target="tpu_custom_call" | custom-call | flops 1000 | bytes 4194304 | tf_op jit(solution)/shard_map/column/pallas_call | solution.py:283
  25.8 0.1 collective-permute-start.2
  25.9 4.1 %collective-permute-start.3 = (bf16[1648,128]{1,0:T(8,128)(2,1)S(1)}, bf16[1648,128]{1,0:T(8,128)(2,1)S(1)}, u32[]{:S(2)}, u32[]{:S(2)}) collective-permute-start(bf16[1648,128]{1,0:T(8,128)(2,1)S(1)} %get-tuple-element.66), channel_id=1, source_target_pairs={{0,7},{1,2},{2,1},{3,4},{4,3},{5,6},{6,5},{7,0},{8,15},{9,10},{10,... | collective-permute-start | bytes 1265672 | tf_op jit(solution)/shard_map/ppermute | solution.py:837
  30.0 0.5 collective-permute-start.5
  30.5 3.9 %collective-permute-done.4.far_a = bf16[4,16,128]{2,1,0:T(8,128)(2,1)S(1)} collective-permute-done((bf16[4,16,128]{2,1,0:T(8,128)(2,1)S(1)}, bf16[4,16,128]{2,1,0:T(8,128)(2,1)S(1)}, u32[]{:S(2)}, u32[]{:S(2)}) %collective-permute-start.4) | collective-permute-done | bytes 16416 | tf_op jit(solution)/shard_map/ppermute | solution.py:837
  34.4 1.6 %collective-permute-done.5.far_b = bf16[4,16,128]{2,1,0:T(8,128)(2,1)S(1)} collective-permute-done((bf16[4,16,128]{2,1,0:T(8,128)(2,1)S(1)}, bf16[4,16,128]{2,1,0:T(8,128)(2,1)S(1)}, u32[]{:S(2)}, u32[]{:S(2)}) %collective-permute-start.5) | collective-permute-done | bytes 16416 | tf_op jit(solution)/shard_map/ppermute | solution.py:837
  36.0 2.5 %sum_tiles.1 = (bf16[2,16,128,128]{3,2,1,0:T(8,128)(2,1)S(1)}, bf16[2,16,144,128]{3,2,1,0:T(8,128)(2,1)S(1)}, bf16[8,144,128]{2,1,0:T(8,128)(2,1)S(1)}, bf16[8,144,128]{2,1,0:T(8,128)(2,1)S(1)}, s32[8,128]{1,0:T(8,128)S(1)}) custom-call(f32[2,16,128,128]{3,2,1,0:T(8,128)S(1)} %get-tuple-element.64.part, bf16[1648,128]{1,0:T(8,128)(2,1)S(1)} %collective-permute-done.2.ya, ...), custom_call_target="tpu_custom_call" | custom-call | flops 1000 | bytes 4194304 | tf_op jit(solution)/shard_map/sum_tiles/pallas_call | solution.py:364
  38.4 0.1 collective-permute-start.6
  38.5 4.6 %collective-permute-start.7 = (bf16[8,144,128]{2,1,0:T(8,128)(2,1)S(1)}, bf16[8,144,128]{2,1,0:T(8,128)(2,1)S(1)}, u32[]{:S(2)}, u32[]{:S(2)}) collective-permute-start(bf16[8,144,128]{2,1,0:T(8,128)(2,1)S(1)} %get-tuple-element.72), channel_id=1, source_target_pairs={{0,120},{8,16},{16,8},{24,32},{32,24},{40,48},{48,40},{56,64},{64,... | collective-permute-start | bytes 884744 | tf_op jit(solution)/shard_map/ppermute | solution.py:837
  43.1 8.2 %inner_convs.1 = (f32[8,2,128,256]{3,2,1,0:T(8,128)S(1)}, f32[2,576,256]{2,1,0:T(8,128)S(1)}) custom-call(bf16[2,16,144,128]{3,2,1,0:T(8,128)(2,1)S(1)} %get-tuple-element.73.x, bf16[2,8,2,128,128]{4,3,2,1,0:T(8,128)(2,1)S(1)} %bitcast.11, bf16[2304,256]{1,0:T(8,128)(2,1)S(1)} %get-tuple-element.75.t1, bf16[3072,256]{1,0:T(8,128)(2,1)S(1)} %get-tuple-element.76.t1o, ...), custom_call_target="tpu_custom_call" | custom-call | flops 6039797760 | bytes 6291456 | tf_op jit(solution)/shard_map/inner_convs/pallas_call | solution.py:448
  51.3 6.4 %edge_convs.1 = (bf16[8,2,128,256]{3,2,1,0:T(8,128)(2,1)S(1)}, f32[128,8,128]{2,1,0:T(8,128)S(1)}, bf16[3,64,128]{2,1,0:T(8,128)(2,1)S(1)}, bf16[3,64,128]{2,1,0:T(8,128)(2,1)S(1)}, bf16[2,64,128]{2,1,0:T(8,128)(2,1)S(1)}) custom-call(bf16[8,144,128]{2,1,0:T(8,128)(2,1)S(1)} %collective-permute-done.6.ra, ...), custom_call_target="tpu_custom_call" | custom-call | flops 2717908992 | bytes 6291456 | tf_op jit(solution)/shard_map/edge_convs/pallas_call | solution.py:562
  57.7 0.0 copy-start.9
  57.7 0.1 collective-permute-start.8
  57.8 3.8 %collective-permute-start.9 = (bf16[3,64,128]{2,1,0:T(8,128)(2,1)S(1)}, bf16[3,64,128]{2,1,0:T(8,128)(2,1)S(1)}, u32[]{:S(2)}, u32[]{:S(2)}) collective-permute-start(bf16[3,64,128]{2,1,0:T(8,128)(2,1)S(1)} %get-tuple-element.89), channel_id=1, source_target_pairs={{0,7},{1,2},{2,1},{3,4},{4,3},{5,6},{6,5},{7,0},{8,15},{9,10},{10,... | collective-permute-start | bytes 147464 | tf_op jit(solution)/shard_map/ppermute | solution.py:837
  61.6 1.8 %turn.1 = bf16[32,16,8,128]{3,2,1,0:T(8,128)(2,1)} custom-call(bf16[8,2,128,256]{3,2,1,0:T(8,128)(2,1)S(1)} %get-tuple-element.87.total), custom_call_target="tpu_custom_call" | custom-call | flops 1000 | bytes 8388608 | tf_op jit(solution)/shard_map/turn/pallas_call | solution.py:590
  63.4 0.1 collective-permute-start.10
  63.5 4.0 %collective-permute-start.11 = (bf16[3,64,128]{2,1,0:T(8,128)(2,1)S(1)}, bf16[3,64,128]{2,1,0:T(8,128)(2,1)S(1)}, u32[]{:S(2)}, u32[]{:S(2)}) collective-permute-start(bf16[3,64,128]{2,1,0:T(8,128)(2,1)S(1)} %pad_maximum_fusion.1), channel_id=1, source_target_pairs={{0,120},{8,16},{16,8},{24,32},{32,24},{40,48},{48,40},{56,64},{64,... | collective-permute-start | bytes 147464 | tf_op jit(solution)/shard_map/ppermute | solution.py:837
  67.5 4.3 %own_read.1 = (f32[3,16384]{1,0:T(4,128)S(1)}, bf16[16384,128]{1,0:T(8,128)(2,1)S(1)}) custom-call(s32[256]{0:T(256)S(1)} %copy-done.9, f32[128,8,128]{2,1,0:T(8,128)S(1)} %get-tuple-element.95.table, bf16[32768,128]{1,0:T(8,128)(2,1)} %w_hbm.5), custom_call_target="tpu_custom_call" | custom-call | flops 134217728 | bytes 9437184 | tf_op jit(solution)/shard_map/own_read/pallas_call | solution.py:658
  71.8 2.8 %far_read.1 = f32[3,32768]{1,0:T(4,128)} custom-call(s32[128]{0:T(128)S(1)} %copy-done.13, s32[1]{0:T(128)S(6)} %copy.17.counts_h.counts, bf16[3,64,128]{2,1,0:T(8,128)(2,1)S(1)} %collective-permute-done.10.xa, bf16[3,64,128]{2,1,0:T(8,128)(2,1)S(1)} %collective-permute-done.11.xb, bf16[3,64,128]{2,1,0:T(8,128)(2,1)S(1)} %collective-permute-done.8.ya, ...), custom_call_target="tpu_custom_call" | custom-call | flops 134217728 | bytes 5242880 | tf_op jit(solution)/shard_map/far_read/pallas_call | solution.py:705
  (34 shorter events, 0.1 us)
Async XLA Ops:
  7.2 14.5 %collective-permute-start = (bf16[3,528,128]{2,1,0:T(8,128)(2,1)}, bf16[3,528,128]{2,1,0:T(8,128)(2,1)S(1)}, u32[]{:S(2)}, u32[]{:S(2)}) collective-permute-start(bf16[3,528,128]{2,1,0:T(8,128)(2,1)} %get-tuple-element.58), channel_id=1, source_target_pairs={{0,8},{8,0},{16,24},{24,16},{32,40},{40,32},{48,56},{56,48},{64,72... | collective-permute-start | bytes 1216520 | tf_op jit(solution)/shard_map/ppermute | solution.py:837
  8.9 11.0 %copy-start.1 = (bf16[128,2048]{1,0:T(8,128)(2,1)S(1)}, bf16[128,2048]{1,0:T(8,128)(2,1)}, u32[]{:S(2)}) copy-start(bf16[128,2048]{1,0:T(8,128)(2,1)} %constant.13.clone.e2a) | copy-start | bytes 1572868
  8.9 11.0 %copy-start.2 = (bf16[128,2048]{1,0:T(8,128)(2,1)S(1)}, bf16[128,2048]{1,0:T(8,128)(2,1)}, u32[]{:S(2)}) copy-start(bf16[128,2048]{1,0:T(8,128)(2,1)} %constant.10.clone.e1a) | copy-start | bytes 1572868
  8.9 11.0 %copy-start.4 = (bf16[128,1024]{1,0:T(8,128)(2,1)S(1)}, bf16[128,1024]{1,0:T(8,128)(2,1)}, u32[]{:S(2)}) copy-start(bf16[128,1024]{1,0:T(8,128)(2,1)} %constant.14.clone.e2b) | copy-start | bytes 786436
  8.9 11.0 %copy-start.5 = (bf16[128,1024]{1,0:T(8,128)(2,1)S(1)}, bf16[128,1024]{1,0:T(8,128)(2,1)}, u32[]{:S(2)}) copy-start(bf16[128,1024]{1,0:T(8,128)(2,1)} %constant.11.clone.e1o) | copy-start | bytes 786436
  8.9 11.0 %copy-start.6 = (bf16[27,32,32]{2,1,0:T(8,128)(2,1)S(1)}, bf16[27,32,32]{2,1,0:T(8,128)(2,1)}, u32[]{:S(2)}) copy-start(bf16[27,32,32]{2,1,0:T(8,128)(2,1)} %c1.1) | copy-start | bytes 165892
  8.9 11.0 %copy-start.7 = (bf16[27,32,32]{2,1,0:T(8,128)(2,1)S(1)}, bf16[27,32,32]{2,1,0:T(8,128)(2,1)}, u32[]{:S(2)}) copy-start(bf16[27,32,32]{2,1,0:T(8,128)(2,1)} %c2.1) | copy-start | bytes 165892
  8.9 11.0 %copy-start.8 = (bf16[128,512]{1,0:T(8,128)(2,1)S(1)}, bf16[128,512]{1,0:T(8,128)(2,1)}, u32[]{:S(2)}) copy-start(bf16[128,512]{1,0:T(8,128)(2,1)} %constant.12.clone.e1r) | copy-start | bytes 393220
  8.9 11.0 %copy-start.10 = (bf16[3,32]{1,0:T(4,128)(2,1)S(1)}, bf16[3,32]{1,0:T(4,128)(2,1)}, u32[]{:S(2)}) copy-start(bf16[3,32]{1,0:T(4,128)(2,1)} %head.1) | copy-start | bytes 580
  8.9 11.0 %copy-start.11 = (f32[32]{0:T(128)S(1)}, f32[32]{0:T(128)}, u32[]{:S(2)}) copy-start(f32[32]{0:T(128)} %param.21) | copy-start | bytes 388
  8.9 11.0 %copy-start.12 = (f32[32]{0:T(128)S(1)}, f32[32]{0:T(128)}, u32[]{:S(2)}) copy-start(f32[32]{0:T(128)} %param.23) | copy-start | bytes 388
  9.0 14.4 %collective-permute-start.1 = (bf16[3,528,128]{2,1,0:T(8,128)(2,1)}, bf16[3,528,128]{2,1,0:T(8,128)(2,1)S(1)}, u32[]{:S(2)}, u32[]{:S(2)}) collective-permute-start(bf16[3,528,128]{2,1,0:T(8,128)(2,1)} %get-tuple-element.59), channel_id=1, source_target_pairs={{0,120},{8,16},{16,8},{24,32},{32,24},{40,48},{48,40},{56,64},{64,... | collective-permute-start | bytes 1216520 | tf_op jit(solution)/shard_map/ppermute | solution.py:837
  19.8 3.6 %copy-start = (bf16[2,16,128,128]{3,2,1,0:T(8,128)(2,1)S(1)}, bf16[2,16,128,128]{3,2,1,0:T(8,128)(2,1)}, u32[]{:S(2)}) copy-start(bf16[2,16,128,128]{3,2,1,0:T(8,128)(2,1)} %own_splat.1.own) | copy-start | bytes 3145732
  19.9 3.6 %copy-start.3 = (bf16[3,528,128]{2,1,0:T(8,128)(2,1)S(1)}, bf16[3,528,128]{2,1,0:T(8,128)(2,1)}, u32[]{:S(2)}) copy-start(bf16[3,528,128]{2,1,0:T(8,128)(2,1)} %get-tuple-element.63) | copy-start | bytes 1216516
  25.8 10.2 %collective-permute-start.2 = (bf16[1648,128]{1,0:T(8,128)(2,1)S(1)}, bf16[1648,128]{1,0:T(8,128)(2,1)S(1)}, u32[]{:S(2)}, u32[]{:S(2)}) collective-permute-start(bf16[1648,128]{1,0:T(8,128)(2,1)S(1)} %get-tuple-element.65), channel_id=1, source_target_pairs={{0,1},{1,0},{2,3},{3,2},{4,5},{5,4},{6,7},{7,6},{8,9},{9,8},{10,11... | collective-permute-start | bytes 1265672 | tf_op jit(solution)/shard_map/ppermute | solution.py:837
  25.9 10.1 %collective-permute-start.3 = (bf16[1648,128]{1,0:T(8,128)(2,1)S(1)}, bf16[1648,128]{1,0:T(8,128)(2,1)S(1)}, u32[]{:S(2)}, u32[]{:S(2)}) collective-permute-start(bf16[1648,128]{1,0:T(8,128)(2,1)S(1)} %get-tuple-element.66), channel_id=1, source_target_pairs={{0,7},{1,2},{2,1},{3,4},{4,3},{5,6},{6,5},{7,0},{8,15},{9,10},{10,... | collective-permute-start | bytes 1265672 | tf_op jit(solution)/shard_map/ppermute | solution.py:837
  30.0 4.4 %collective-permute-start.4 = (bf16[4,16,128]{2,1,0:T(8,128)(2,1)S(1)}, bf16[4,16,128]{2,1,0:T(8,128)(2,1)S(1)}, u32[]{:S(2)}, u32[]{:S(2)}) collective-permute-start(bf16[4,16,128]{2,1,0:T(8,128)(2,1)S(1)} %get-tuple-element.67), channel_id=1, source_target_pairs={{0,2},{1,3},{2,0},{3,1},{4,6},{5,7},{6,4},{7,5},{8,10},{9,11},{10,... | collective-permute-start | bytes 49160 | tf_op jit(solution)/shard_map/ppermute | solution.py:837
  30.0 6.0 %collective-permute-start.5 = (bf16[4,16,128]{2,1,0:T(8,128)(2,1)S(1)}, bf16[4,16,128]{2,1,0:T(8,128)(2,1)S(1)}, u32[]{:S(2)}, u32[]{:S(2)}) collective-permute-start(bf16[4,16,128]{2,1,0:T(8,128)(2,1)S(1)} %get-tuple-element.68), channel_id=1, source_target_pairs={{0,6},{1,7},{2,4},{3,5},{4,2},{5,3},{6,0},{7,1},{8,14},{9,15},{10,... | collective-permute-start | bytes 49160 | tf_op jit(solution)/shard_map/ppermute | solution.py:837
  38.4 12.9 %collective-permute-start.6 = (bf16[8,144,128]{2,1,0:T(8,128)(2,1)S(1)}, bf16[8,144,128]{2,1,0:T(8,128)(2,1)S(1)}, u32[]{:S(2)}, u32[]{:S(2)}) collective-permute-start(bf16[8,144,128]{2,1,0:T(8,128)(2,1)S(1)} %get-tuple-element.71), channel_id=1, source_target_pairs={{0,8},{8,0},{16,24},{24,16},{32,40},{40,32},{48,56},{56,48},{64,72... | collective-permute-start | bytes 884744 | tf_op jit(solution)/shard_map/ppermute | solution.py:837
  38.5 12.8 %collective-permute-start.7 = (bf16[8,144,128]{2,1,0:T(8,128)(2,1)S(1)}, bf16[8,144,128]{2,1,0:T(8,128)(2,1)S(1)}, u32[]{:S(2)}, u32[]{:S(2)}) collective-permute-start(bf16[8,144,128]{2,1,0:T(8,128)(2,1)S(1)} %get-tuple-element.72), channel_id=1, source_target_pairs={{0,120},{8,16},{16,8},{24,32},{32,24},{40,48},{48,40},{56,64},{64,... | collective-permute-start | bytes 884744 | tf_op jit(solution)/shard_map/ppermute | solution.py:837
  57.7 9.8 %copy-start.9 = (s32[256]{0:T(256)S(1)}, s32[256]{0:T(256)}, u32[]{:S(2)}) copy-start(s32[256]{0:T(256)} %ids.3) | copy-start | bytes 3076
  57.7 5.7 %collective-permute-start.8 = (bf16[3,64,128]{2,1,0:T(8,128)(2,1)S(1)}, bf16[3,64,128]{2,1,0:T(8,128)(2,1)S(1)}, u32[]{:S(2)}, u32[]{:S(2)}) collective-permute-start(bf16[3,64,128]{2,1,0:T(8,128)(2,1)S(1)} %get-tuple-element.88), channel_id=1, source_target_pairs={{0,1},{1,0},{2,3},{3,2},{4,5},{5,4},{6,7},{7,6},{8,9},{9,8},{10,11... | collective-permute-start | bytes 147464 | tf_op jit(solution)/shard_map/ppermute | solution.py:837
  57.8 5.6 %collective-permute-start.9 = (bf16[3,64,128]{2,1,0:T(8,128)(2,1)S(1)}, bf16[3,64,128]{2,1,0:T(8,128)(2,1)S(1)}, u32[]{:S(2)}, u32[]{:S(2)}) collective-permute-start(bf16[3,64,128]{2,1,0:T(8,128)(2,1)S(1)} %get-tuple-element.89), channel_id=1, source_target_pairs={{0,7},{1,2},{2,1},{3,4},{4,3},{5,6},{6,5},{7,0},{8,15},{9,10},{10,... | collective-permute-start | bytes 147464 | tf_op jit(solution)/shard_map/ppermute | solution.py:837
  63.4 8.4 %collective-permute-start.10 = (bf16[3,64,128]{2,1,0:T(8,128)(2,1)S(1)}, bf16[3,64,128]{2,1,0:T(8,128)(2,1)S(1)}, u32[]{:S(2)}, u32[]{:S(2)}) collective-permute-start(bf16[3,64,128]{2,1,0:T(8,128)(2,1)S(1)} %pad_maximum_fusion), channel_id=1, source_target_pairs={{0,8},{8,0},{16,24},{24,16},{32,40},{40,32},{48,56},{56,48},{64,72... | collective-permute-start | bytes 147464 | tf_op jit(solution)/shard_map/ppermute | solution.py:837
  63.5 8.3 %collective-permute-start.11 = (bf16[3,64,128]{2,1,0:T(8,128)(2,1)S(1)}, bf16[3,64,128]{2,1,0:T(8,128)(2,1)S(1)}, u32[]{:S(2)}, u32[]{:S(2)}) collective-permute-start(bf16[3,64,128]{2,1,0:T(8,128)(2,1)S(1)} %pad_maximum_fusion.1), channel_id=1, source_target_pairs={{0,120},{8,16},{16,8},{24,32},{32,24},{40,48},{48,40},{56,64},{64,... | collective-permute-start | bytes 147464 | tf_op jit(solution)/shard_map/ppermute | solution.py:837
  67.5 4.3 %copy-start.13 = (s32[128]{0:T(128)S(1)}, s32[128]{0:T(128)}, u32[]{:S(2)}) copy-start(s32[128]{0:T(128)} %get-tuple-element.91.slots) | copy-start | bytes 1540

commit v5 on v4

--- a/solution.py
+++ b/solution.py
@@ -12,8 +12,8 @@
 SLOTS = 16
 PAY = SLOTS * 32 + 16
 ROWS = 144
-STEP = 16
-STEPS = 8
+STEP = 32
+STEPS = 4
 MIB = 1 << 20
 F32 = jnp.float32
 BF16 = jnp.bfloat16
@@ -132,14 +132,15 @@
     for dx, out in ((toward, out_a), (1, mid), (2 - toward, out_b)):
         for dy in range(3):
             k = dx * 3 + dy
-            out[dy, 0 : SLOTS * 32, :] = tiles[pl.ds(k * SLOTS, SLOTS)].reshape(SLOTS * 32, 128)
-            out[dy, SLOTS * 32 : PAY, :] = jnp.broadcast_to(
+            at = dy * PAY
+            out[at : at + SLOTS * 32, :] = tiles[pl.ds(k * SLOTS, SLOTS)].reshape(SLOTS * 32, 128)
+            out[at + SLOTS * 32 : at + PAY, :] = jnp.broadcast_to(
                 idrows[pl.ds(k, 1), :], (16, 128)
             ).astype(BF16)
 
 
 def far_splat(features, weights, owners, ids, counts):
-    pay = jax.ShapeDtypeStruct((3, PAY, 128), BF16)
+    pay = jax.ShapeDtypeStruct((3 * PAY, 128), BF16)
     vm = pl.BlockSpec(memory_space=VMEM)
     anywhere = pl.BlockSpec(memory_space=pl.ANY)
     return pl.pallas_call(
@@ -205,7 +206,26 @@
     )(ids, features, weights)
 
 
-BUNDLE = 3 * PAY + 64
+def bundle_kernel(xa, xb, mid, to_a, to_b):
+    toward = upward(lax.axis_index("gy"))
+    for out, dy in ((to_a, toward), (to_b, 2 - toward)):
+        at = pl.multiple_of(dy * PAY, 16)
+        for k, ref in enumerate((xa, mid, xb)):
+            out[k * PAY : (k + 1) * PAY, :] = ref[pl.ds(at, PAY), :]
+
+
+def bundle(xa, xb, mid):
+    vm = pl.BlockSpec(memory_space=VMEM)
+    shape = jax.ShapeDtypeStruct((3 * PAY, 128), BF16)
+    return pl.pallas_call(
+        bundle_kernel,
+        in_specs=[vm] * 3,
+        out_specs=[vm, vm],
+        out_shape=[shape, shape],
+        compiler_params=params(8),
+        cost_estimate=cost(1000, 2 * MIB),
+        name="bundle",
+    )(xa, xb, mid)
 
 
 def ids_of(groups):
@@ -218,17 +238,14 @@
     return rows.astype(F32).reshape(4, 8, 128)
 
 
-def add_tiles(grid, ids, n, ref, at):
-    def add(j, carry):
-        z, tx, y = tile_place(ids[n, j])
-        grid[tx, pl.ds(z, 4), pl.ds(y, 8), :] += tile_of(ref, at, j)
-        return carry
-
-    lax.fori_loop(0, SLOTS, add, 0, unroll=4)
+def put_tile(grid, tile, new):
+    z, tx, y = tile_place(tile)
+    grid[tx, pl.ds(z, 4), pl.ds(y, 8), :] += new
 
 
 def column_kernel(
-    own, xa, xb, mid, g, ids, to_a, to_b, fwd_a, fwd_b, keep_lo, keep_hi, acc, idv, sem
+    own, xa, xb, mid,
+    g, ids, near_a, near_b, fwd_a, fwd_b, keep_lo, keep_hi, acc_a, acc_b, idv, sem,
 ):
     iy = lax.axis_index("gy")
     even = iy % 2 == 0
@@ -240,37 +257,33 @@
     copy = pltpu.make_async_copy(idv, ids, sem)
     copy.start()
     g[...] = own[...].astype(F32)
-    acc[...] = jnp.zeros_like(acc)
-    for n, (ref, at) in enumerate(groups[2:]):
-        out, k = (to_a, n) if n < 3 else (to_b, n - 3)
-        out[k * PAY : (k + 1) * PAY, :] = ref[pl.ds(at, PAY), :]
+    acc_a[...] = jnp.zeros_like(acc_a)
+    acc_b[...] = jnp.zeros_like(acc_b)
     copy.wait()
-    for n, (ref, at) in enumerate(groups):
-        if n < 2:
-            add_tiles(g, ids, n, ref, at)
-            continue
-
-        def add(j, carry, n=n, ref=ref, at=at):
-            tile = ids[n, j]
-            ty = tile & 15
-            place = jnp.where(ty == 0, 0, jnp.where(ty == 15, 1, 2)) + (0 if n < 5 else 3)
-            acc[place, (tile >> 4) & 1, pl.ds((tile >> 5) * 4, 4)] += tile_of(ref, at, j)
+    for k in range(3):
+
+        def add(j, carry, k=k):
+            if k < 2:
+                put_tile(g, ids[k, j], tile_of(groups[k][0], groups[k][1], j))
+            for n, acc in ((2 + k, acc_a), (5 + k, acc_b)):
+                tile = ids[n, j]
+                ty = tile & 15
+                place = jnp.where(ty == 0, 0, jnp.where(ty == 15, 1, 2))
+                new = tile_of(groups[n][0], groups[n][1], j)
+                acc[place, (tile >> 4) & 1, pl.ds((tile >> 5) * 4, 4)] += new
             return carry
 
-        lax.fori_loop(0, SLOTS, add, 0, unroll=4)
-    above = jnp.where(even, 0, 3)
-    below = 3 - above
+        lax.fori_loop(0, SLOTS, add, 0, unroll=8)
     for tx in range(2):
         for r in range(2):
             k = tx * 2 + r
-            rows = slice(3 * PAY + k * 16, 3 * PAY + k * 16 + 16)
             low, high = g[tx, :, r, :], g[tx, :, BY - 2 + r, :]
-            to_a[rows, :] = jnp.where(even, high, low).astype(BF16)
-            to_b[rows, :] = jnp.where(even, low, high).astype(BF16)
-            keep_hi[k] = acc[above, tx, :, r, :]
-            keep_lo[k] = acc[below + 1, tx, :, 6 + r, :]
-            high = acc[above + 1, tx, :, 6 + r, :]
-            low = acc[below, tx, :, r, :]
+            near_a[k] = jnp.where(even, high, low).astype(BF16)
+            near_b[k] = jnp.where(even, low, high).astype(BF16)
+            keep_hi[k] = jnp.where(even, acc_a[0, tx, :, r, :], acc_b[0, tx, :, r, :])
+            keep_lo[k] = jnp.where(even, acc_b[1, tx, :, 6 + r, :], acc_a[1, tx, :, 6 + r, :])
+            high = jnp.where(even, acc_a[1, tx, :, 6 + r, :], acc_b[1, tx, :, 6 + r, :])
+            low = jnp.where(even, acc_b[0, tx, :, r, :], acc_a[0, tx, :, r, :])
             up = (iy >> 1) % 2 == 0
             fwd_a[k] = jnp.where(up, high, low).astype(BF16)
             fwd_b[k] = jnp.where(up, low, high).astype(BF16)
@@ -278,8 +291,6 @@
 
 def column(own, xa, xb, mid):
     vm = pl.BlockSpec(memory_space=VMEM)
-    bundle = jax.ShapeDtypeStruct((BUNDLE, 128), BF16)
-    flat = [v.reshape(3 * PAY, 128) for v in (xa, xb, mid)]
     return pl.pallas_call(
         column_kernel,
         in_specs=[vm] * 4,
@@ -287,26 +298,24 @@
         out_shape=[
             jax.ShapeDtypeStruct((2, SLAB, BY, 128), F32),
             jax.ShapeDtypeStruct((8, 128), jnp.int32),
-            bundle,
-            bundle,
-            jax.ShapeDtypeStruct((4, SLAB, 128), BF16),
-            jax.ShapeDtypeStruct((4, SLAB, 128), BF16),
-            jax.ShapeDtypeStruct((4, SLAB, 128), F32),
-            jax.ShapeDtypeStruct((4, SLAB, 128), F32),
-        ],
+        ]
+        + [jax.ShapeDtypeStruct((4, SLAB, 128), BF16)] * 4
+        + [jax.ShapeDtypeStruct((4, SLAB, 128), F32)] * 2,
         scratch_shapes=[
-            VMEM((6, 2, SLAB, 8, 128), F32),
+            VMEM((3, 2, SLAB, 8, 128), F32),
+            VMEM((3, 2, SLAB, 8, 128), F32),
             VMEM((8, 128), jnp.int32),
             pltpu.SemaphoreType.DMA,
         ],
         compiler_params=params(16),
         cost_estimate=cost(1000, 4 * MIB),
         name="column",
-    )(own, *flat)
+    )(own, xa, xb, mid)
 
 
 def sum_kernel(
-    part, ya, yb, far_a, far_b, keep_lo, keep_hi, g, x, to_a, to_b, ids, grid, edge, idv, sem
+    part, ya, yb, next_a, next_b, far_a, far_b, keep_lo, keep_hi,
+    g, x, to_a, to_b, ids, grid, more, edge, idv, sem,
 ):
     even_x = lax.axis_index("gx") % 2 == 0
     iy = lax.axis_index("gy")
@@ -318,12 +327,12 @@
     copy = pltpu.make_async_copy(idv, ids, sem)
     copy.start()
     grid[...] = part[...]
+    more[...] = jnp.zeros_like(more)
     edge[...] = jnp.zeros_like(edge)
     for tx in range(2):
         for r in range(2):
             k = tx * 2 + r
-            rows = slice(3 * PAY + k * 16, 3 * PAY + k * 16 + 16)
-            near_a, near_b = ya[rows, :].astype(F32), yb[rows, :].astype(F32)
+            near_a, near_b = next_a[k].astype(F32), next_b[k].astype(F32)
             away_a, away_b = far_a[k].astype(F32), far_b[k].astype(F32)
             low = jnp.where(iy >= 2, jnp.where(up, away_b, away_a), 0.0)
             low = low + jnp.where(even, near_b, near_a) + keep_lo[k]
@@ -332,12 +341,18 @@
             edge[tx, 0, :, 6 + r, :] = jnp.where(iy > 0, low, 0.0)
             edge[tx, 1, :, r, :] = jnp.where(iy < 7, high, 0.0)
     copy.wait()
-    for n, (ref, at) in enumerate(groups):
-        add_tiles(grid, ids, n, ref, at)
+    for k in range(3):
+
+        def add(j, carry, k=k):
+            put_tile(grid, ids[k, j], tile_of(ya, k * PAY, j))
+            put_tile(more, ids[3 + k, j], tile_of(yb, k * PAY, j))
+            return carry
+
+        lax.fori_loop(0, SLOTS, add, 0, unroll=8)
     lane = lanes_of((ROWS, 128))
 
     def plane(tx, z):
-        return jnp.concatenate([edge[tx, 0, z], grid[tx, z], edge[tx, 1, z]], 0)
+        return jnp.concatenate([edge[tx, 0, z], grid[tx, z] + more[tx, z], edge[tx, 1, z]], 0)
 
     def pair(z, carry):
         sides = []
@@ -358,12 +373,12 @@
     lax.fori_loop(0, 8, pair, 0, unroll=2)
 
 
-def sum_tiles(part, ya, yb, far_a, far_b, keep_lo, keep_hi):
+def sum_tiles(part, ya, yb, near_a, near_b, far_a, far_b, keep_lo, keep_hi):
     vm = pl.BlockSpec(memory_space=VMEM)
     side = jax.ShapeDtypeStruct((SLAB // 2, ROWS, 128), BF16)
     return pl.pallas_call(
         sum_kernel,
-        in_specs=[vm] * 7,
+        in_specs=[vm] * 9,
         out_specs=[vm] * 4 + [pl.BlockSpec(memory_space=SMEM)],
         out_shape=[
             jax.ShapeDtypeStruct((2, SLAB, BY, 128), BF16),
@@ -374,6 +389,7 @@
         ],
         scratch_shapes=[
             VMEM((2, SLAB, BY, 128), F32),
+            VMEM((2, SLAB, BY, 128), F32),
             VMEM((2, 2, SLAB, 8, 128), F32),
             VMEM((8, 128), jnp.int32),
             pltpu.SemaphoreType.DMA,
@@ -381,7 +397,7 @@
         compiler_params=params(16),
         cost_estimate=cost(1000, 4 * MIB),
         name="sum_tiles",
-    )(part, ya, yb, far_a, far_b, keep_lo, keep_hi)
+    )(part, ya, yb, near_a, near_b, far_a, far_b, keep_lo, keep_hi)
 
 
 def rows_inside(shape, iy):
@@ -499,6 +515,7 @@
             s = s[:, 8 : 8 + BY].astype(BF16)
             hs[dy, n * 4 : n * 4 + 4, 1] = s[:, :, 0:128]
             hs[dy, n * 4 + 1 : n * 4 + 5, 0] = s[:, :, 128:256]
+    rows = []
     for n in range(2):
         for zo in range(2):
             taps = window(hs, n, zo) + window(hs, n, zo + 1) + window(hs, n, zo + 2)
@@ -506,12 +523,15 @@
             acc = acc.reshape(4, BY, 256) + part[n * 4 : n * 4 + 4, zo]
             acc = acc.astype(BF16)
             total[n * 4 : n * 4 + 4, zo] = acc
-            v = jnp.concatenate([acc[p] for p in range(4)], 1)
-            v = jnp.dot(v, headx[...], preferred_element_type=F32).T
+            rows.append(jnp.concatenate([acc[p] for p in range(4)], 1))
+    v = jnp.dot(jnp.concatenate(rows, 0), headx[...], preferred_element_type=F32).T
+    for n in range(2):
+        for zo in range(2):
+            q = (n * 2 + zo) * BY
             for p in range(4):
                 for a in range(3):
                     at = p * 32 + a * 8
-                    vel[a, 2 * (n * 4 + p) + zo] = v[at : at + 8]
+                    vel[a, 2 * (n * 4 + p) + zo] = v[at : at + 8, q : q + BY]
 
     table[...] = jnp.zeros_like(table)
     sub = lax.broadcasted_iota(jnp.int32, (4, 8, 128), 1)
@@ -674,7 +694,7 @@
     )(ids, table, weights)
 
 
-def far_read_kernel(slots, counts, xa, xb, ya, yb, w, near, out, table):
+def far_read_kernel(slots, counts, xa, xb, ya, yb, w, near, out, table, made, sems):
     dx = upward(lax.axis_index("gx"))
     dy = upward(lax.axis_index("gy"))
     places = [(ya, 1, 3 + dy), (yb, 1, 5 - dy)]
@@ -688,15 +708,23 @@
             table[place * SLOTS + 2 * j] = v[j]
             table[place * SLOTS + 2 * j + 1] = turned[j]
     half = near.shape[1]
-    out[:, 0:half] = near[...]
+    size = BATCH * 128
+    copies = [pltpu.make_async_copy(near, out.at[:, pl.ds(0, half)], sems.at[128 // BATCH])]
+    copies[0].start()
     for k in range(128 // BATCH):
         rows = [
             two_blocks(table[slots[k * BATCH + 2 * j]], table[slots[k * BATCH + 2 * j + 1]])
             for j in range(BATCH // 2)
         ]
-        read_batch(
-            jnp.concatenate(rows, 0), w, k * BATCH, out, half + k * BATCH * 128, counts[0]
+        read_batch(jnp.concatenate(rows, 0), w, k * BATCH, made.at[k], 0, counts[0])
+        copies.append(
+            pltpu.make_async_copy(
+                made.at[k], out.at[:, pl.ds(half + k * size, size)], sems.at[k]
+            )
         )
+        copies[-1].start()
+    for copy in copies:
+        copy.wait()
 
 
 def far_read(slots, counts, xa, xb, ya, yb, w, near):
@@ -705,9 +733,13 @@
     return pl.pallas_call(
         far_read_kernel,
         in_specs=[smem, smem] + [vm] * 6,
-        out_specs=vm,
+        out_specs=pl.BlockSpec(memory_space=pl.ANY),
         out_shape=jax.ShapeDtypeStruct((3, 2 * near.shape[1]), F32),
-        scratch_shapes=[VMEM((9 * SLOTS, 8, 128), F32)],
+        scratch_shapes=[
+            VMEM((9 * SLOTS, 8, 128), F32),
+            VMEM((128 // BATCH, 3, BATCH * 128), F32),
+            pltpu.SemaphoreType.DMA((128 // BATCH + 1,)),
+        ],
         compiler_params=params(24),
         cost_estimate=cost(2 * 128 * 32 * 128 * 128, 5 * MIB),
         name="far_read",
@@ -837,19 +869,25 @@
         return lax.ppermute(x, axis, route)
 
     to_a, mid, to_b, slots = far_splat(features, weights, owners, tile_ids, counts)
-    from_xb = swap(to_b, "gx", "b")
-    from_xa = swap(to_a, "gx", "a")
+    xb = swap(to_b, "gx", "b")
+    xa = swap(to_a, "gx", "a")
     made = prepare(conv_first, conv_second, bias_first, bias_second, head)
     own = own_splat(features, weights, tile_ids)
-    own, made, from_xa, from_xb = lax.optimization_barrier((own, made, from_xa, from_xb))
+    own, made, xa, xb = lax.optimization_barrier((own, made, xa, xb))
     t1a, t1o, t1r, t2a, t2b, headx, b1, b2 = made
-
-    g, idx, to_a, to_b, fwd_a, fwd_b, keep_lo, keep_hi = column(own, from_xa, from_xb, mid)
+    to_a, to_b = bundle(xa, xb, mid)
     from_ya = swap(to_a, "gy", "a")
     from_yb = swap(to_b, "gy", "b")
+    own, to_a, to_b = lax.optimization_barrier((own, to_a, to_b))
+
+    g, idx, near_a, near_b, fwd_a, fwd_b, keep_lo, keep_hi = column(own, xa, xb, mid)
+    near_a = swap(near_a, "gy", "a")
+    near_b = swap(near_b, "gy", "b")
     far_a = swap(fwd_a, "gy", "a", 2)
     far_b = swap(fwd_b, "gy", "b", 2)
-    g, x, to_a, to_b, ids = sum_tiles(g, from_ya, from_yb, far_a, far_b, keep_lo, keep_hi)
+    g, x, to_a, to_b, ids = sum_tiles(
+        g, from_ya, from_yb, near_a, near_b, far_a, far_b, keep_lo, keep_hi
+    )
 
     xb = swap(to_b, "gx", "b")
     xa = swap(to_a, "gx", "a")

time: 74.7 us -> 72.4 us (0.969)
  waiting for transfers between devices: 7.19 us -> 11.4 us
  Pallas kernels: 42.2 us -> 38.7 us
  starting transfers between devices: 23.6 us -> 20.2 us
    ppermute x12 -> x14, waiting for transfers between devices: 7.19 us -> 11.4 us  [swap(): return lax.ppermute(x, axis, route)]
    ppermute x12 -> x14, starting transfers between devices: 23.6 us -> 20.2 us  [swap(): return lax.ppermute(x, axis, route)]
    pallas_call x1, Pallas kernels: 6.4 us -> 5.38 us  [own_splat(): pl.pallas_call(own_splat_kernel, in_specs=[pl.BlockSpec(memory_space=SMEM...]
    pallas_call x1, Pallas kernels: 6.38 us -> 5.38 us  [edge_convs(): pl.pallas_call(edge_kernel, in_specs=[vm] * 7 + [pl.BlockSpec(memory_spac...]
    pallas_call x1, Pallas kernels: 5.87 us -> 4.97 us  [far_splat(): pl.pallas_call(far_splat_kernel, in_specs=[anywhere] * 5, out_specs=[vm,...]
    pallas_call x1 -> x2, Pallas kernels: 2.45 us -> 2.32 us  [the longest x1 2.27 us: sum_tiles(): pl.pallas_call(sum_kernel, in_specs=[vm] * 9, out_specs=[vm] * 4 + [pl.Bl...]
  transfers between devices with their start and end apart: 12 -> 14, of which waited for: 3 -> 5; matrix products, arithmetic and copies ran while one was open for 0% -> 0% of each run, Pallas kernels for 30% -> 32%
where the time goes in v5:
time: 72.4 us; the launch traced here: 72.3 us
  Pallas kernels  38.7 us (53%)
  starting transfers between devices  20.2 us (28%)
  waiting for transfers between devices  11.4 us (16%)
  between operations  1.77 us (2%)
    ppermute x14, starting transfers between devices, swap(): return lax.ppermute(x, axis, route)  20.2 us
    ppermute x14, waiting for transfers between devices, swap(): return lax.ppermute(x, axis, route)  11.4 us
    pallas_call x1, Pallas kernels, inner_convs(): pl.pallas_call(inner_kernel, in_specs=[vm] * 7, out_specs=[vm, vm], out_s...  8.18 us
    pallas_call x1, Pallas kernels, own_splat(): pl.pallas_call(own_splat_kernel, in_specs=[pl.BlockSpec(memory_space=SMEM...  5.38 us
    pallas_call x1, Pallas kernels, edge_convs(): pl.pallas_call(edge_kernel, in_specs=[vm] * 7 + [pl.BlockSpec(memory_spac...  5.38 us
    pallas_call x1, Pallas kernels, far_splat(): pl.pallas_call(far_splat_kernel, in_specs=[anywhere] * 5, out_specs=[vm,...  4.97 us
    pallas_call x1, Pallas kernels, own_read(): pl.pallas_call(own_read_kernel, in_specs=[pl.BlockSpec(memory_space=SMEM)...  4.27 us
    pallas_call x1, Pallas kernels, far_read(): pl.pallas_call(far_read_kernel, in_specs=[smem, smem] + [vm] * 6, out_spe...  2.65 us
  transfers between devices with their start and end apart: 14, of which 5 were waited for; matrix products, arithmetic and copies ran while one was open for 0% of the time, Pallas kernels for 32%

profile of v5, /device:TPU:0, one launch (start us, length us, event | category | flops | bytes accessed | tf_op | source)
XLA Modules:
  0.0 72.3 jit_solution(14399213493561894816)
XLA Ops:
  1.3 5.0 %far_splat.1 = (bf16[1584,128]{1,0:T(8,128)(2,1)}, bf16[1584,128]{1,0:T(8,128)(2,1)}, bf16[1584,128]{1,0:T(8,128)(2,1)}, s32[128]{0:T(128)}) custom-call(s32[256]{0:T(256)} %owners_h.1, s32[256]{0:T(256)} %ids.3, s32[1]{0:T(128)S(6)} %copy.17.counts_h.counts, bf16[32,32768]{1,0:T(8,128)(2,1)} %f_hbm.3, bf16[32768,128]{1,0:T(8,128)(2,1)} %w_hbm.5), custom_call_target="tpu_custom_call" | custom-call | flops 134217728 | bytes 6291456 | tf_op jit(solution)/shard_map/far_splat/pallas_call | solution.py:146
  6.3 1.7 %collective-permute-start = (bf16[1584,128]{1,0:T(8,128)(2,1)}, bf16[1584,128]{1,0:T(8,128)(2,1)S(1)}, u32[]{:S(2)}, u32[]{:S(2)}) collective-permute-start(bf16[1584,128]{1,0:T(8,128)(2,1)} %get-tuple-element.61), channel_id=1, source_target_pairs={{0,8},{8,0},{16,24},{24,16},{32,40},{40,32},{48,56},{56,48},{64,72... | collective-permute-start | bytes 1216520 | tf_op jit(solution)/shard_map/ppermute | solution.py:869
  8.0 0.0 copy-start.6
  8.0 0.0 copy-start.8
  8.1 4.4 %collective-permute-start.1 = (bf16[1584,128]{1,0:T(8,128)(2,1)}, bf16[1584,128]{1,0:T(8,128)(2,1)S(1)}, u32[]{:S(2)}, u32[]{:S(2)}) collective-permute-start(bf16[1584,128]{1,0:T(8,128)(2,1)} %get-tuple-element.62), channel_id=1, source_target_pairs={{0,120},{8,16},{16,8},{24,32},{32,24},{40,48},{48,40},{56,64},{64,... | collective-permute-start | bytes 1216520 | tf_op jit(solution)/shard_map/ppermute | solution.py:869
  12.5 5.4 %own_splat.1.own = bf16[2,16,128,128]{3,2,1,0:T(8,128)(2,1)} custom-call(s32[256]{0:T(256)} %ids.3, bf16[32,32768]{1,0:T(8,128)(2,1)} %f_hbm.3, bf16[32768,128]{1,0:T(8,128)(2,1)} %w_hbm.5), custom_call_target="tpu_custom_call" | custom-call | flops 134217728 | bytes 6291456 | tf_op jit(solution)/shard_map/own_splat/pallas_call | solution.py:192
  18.0 1.7 %prepare.1 = (bf16[2304,256]{1,0:T(8,128)(2,1)S(1)}, bf16[3072,256]{1,0:T(8,128)(2,1)S(1)}, bf16[1536,256]{1,0:T(8,128)(2,1)S(1)}, bf16[2560,256]{1,0:T(8,128)(2...) custom-call(bf16[27,32,32]{2,1,0:T(8,128)(2,1)S(1)} %copy-done.6, ...), custom_call_target="tpu_custom_call" | custom-call | flops 471859200 | bytes 5242880 | tf_op jit(solution)/shard_map/prepare/pallas_call | solution.py:829
  19.7 2.8 %collective-permute-done.1.xb = bf16[1584,128]{1,0:T(8,128)(2,1)S(1)} collective-permute-done((bf16[1584,128]{1,0:T(8,128)(2,1)}, bf16[1584,128]{1,0:T(8,128)(2,1)S(1)}, u32[]{:S(2)}, u32[]{:S(2)}) %collective-permute-start.1) | collective-permute-done | bytes 405536 | tf_op jit(solution)/shard_map/ppermute | solution.py:869
  22.5 0.1 bundle.1
  22.5 0.1 collective-permute-start.2
  22.6 4.2 %collective-permute-start.3 = (bf16[1584,128]{1,0:T(8,128)(2,1)S(1)}, bf16[1584,128]{1,0:T(8,128)(2,1)S(1)}, u32[]{:S(2)}, u32[]{:S(2)}) collective-permute-start(bf16[1584,128]{1,0:T(8,128)(2,1)S(1)} %get-tuple-element.68), channel_id=1, source_target_pairs={{0,7},{1,2},{2,1},{3,4},{4,3},{5,6},{6,5},{7,0},{8,15},{9,10},{10,... | collective-permute-start | bytes 1216520 | tf_op jit(solution)/shard_map/ppermute | solution.py:869
  26.8 2.1 %column.1 = (f32[2,16,128,128]{3,2,1,0:T(8,128)S(1)}, s32[8,128]{1,0:T(8,128)S(1)}, bf16[4,16,128]{2,1,0:T(8,128)(2,1)S(1)}, bf16[4,16,128]{2,1,0:T(8,128)(2,1)S...) custom-call(bf16[2,16,128,128]{3,2,1,0:T(8,128)(2,1)S(1)} %copy-done, ...), custom_call_target="tpu_custom_call" | custom-call | flops 1000 | bytes 4194304 | tf_op jit(solution)/shard_map/column/pallas_call | solution.py:294
  28.9 0.1 collective-permute-start.4
  29.0 0.5 collective-permute-start.5
  29.5 1.7 %collective-permute-start.6 = (bf16[4,16,128]{2,1,0:T(8,128)(2,1)S(1)}, bf16[4,16,128]{2,1,0:T(8,128)(2,1)S(1)}, u32[]{:S(2)}, u32[]{:S(2)}) collective-permute-start(bf16[4,16,128]{2,1,0:T(8,128)(2,1)S(1)} %get-tuple-element.73), channel_id=1, source_target_pairs={{0,2},{1,3},{2,0},{3,1},{4,6},{5,7},{6,4},{7,5},{8,10},{9,11},{10,... | collective-permute-start | bytes 49160 | tf_op jit(solution)/shard_map/ppermute | solution.py:869
  31.1 0.0 collective-permute-start.7
  31.2 2.3 %collective-permute-done.5.next_b = bf16[4,16,128]{2,1,0:T(8,128)(2,1)S(1)} collective-permute-done((bf16[4,16,128]{2,1,0:T(8,128)(2,1)S(1)}, bf16[4,16,128]{2,1,0:T(8,128)(2,1)S(1)}, u32[]{:S(2)}, u32[]{:S(2)}) %collective-permute-start.5) | collective-permute-done | bytes 16416 | tf_op jit(solution)/shard_map/ppermute | solution.py:869
  33.5 2.6 %collective-permute-done.7.far_b = bf16[4,16,128]{2,1,0:T(8,128)(2,1)S(1)} collective-permute-done((bf16[4,16,128]{2,1,0:T(8,128)(2,1)S(1)}, bf16[4,16,128]{2,1,0:T(8,128)(2,1)S(1)}, u32[]{:S(2)}, u32[]{:S(2)}) %collective-permute-start.7) | collective-permute-done | bytes 16416 | tf_op jit(solution)/shard_map/ppermute | solution.py:869
  36.1 2.3 %sum_tiles.1 = (bf16[2,16,128,128]{3,2,1,0:T(8,128)(2,1)S(1)}, bf16[2,16,144,128]{3,2,1,0:T(8,128)(2,1)S(1)}, bf16[8,144,128]{2,1,0:T(8,128)(2,1)S(1)}, bf16[8,144,128]{2,1,0:T(8,128)(2,1)S(1)}, s32[8,128]{1,0:T(8,128)S(1)}) custom-call(f32[2,16,128,128]{3,2,1,0:T(8,128)S(1)} %get-tuple-element.70.part, bf16[1584,128]{1,0:T(8,128)(2,1)S(1)} %collective-permute-done.2.ya, ...), custom_call_target="tpu_custom_call" | custom-call | flops 1000 | bytes 4194304 | tf_op jit(solution)/shard_map/sum_tiles/pallas_call | solution.py:379
  38.4 0.1 collective-permute-start.8
  38.5 4.6 %collective-permute-start.9 = (bf16[8,144,128]{2,1,0:T(8,128)(2,1)S(1)}, bf16[8,144,128]{2,1,0:T(8,128)(2,1)S(1)}, u32[]{:S(2)}, u32[]{:S(2)}) collective-permute-start(bf16[8,144,128]{2,1,0:T(8,128)(2,1)S(1)} %get-tuple-element.78), channel_id=1, source_target_pairs={{0,120},{8,16},{16,8},{24,32},{32,24},{40,48},{48,40},{56,64},{64,... | collective-permute-start | bytes 884744 | tf_op jit(solution)/shard_map/ppermute | solution.py:869
  43.1 8.2 %inner_convs.1 = (f32[8,2,128,256]{3,2,1,0:T(8,128)S(1)}, f32[2,576,256]{2,1,0:T(8,128)S(1)}) custom-call(bf16[2,16,144,128]{3,2,1,0:T(8,128)(2,1)S(1)} %get-tuple-element.79.x, bf16[2,8,2,128,128]{4,3,2,1,0:T(8,128)(2,1)S(1)} %bitcast.5, bf16[2304,256]{1,0:T(8,128)(2,1)S(1)} %get-tuple-element.81.t1, bf16[3072,256]{1,0:T(8,128)(2,1)S(1)} %get-tuple-element.82.t1o, ...), custom_call_target="tpu_custom_call" | custom-call | flops 6039797760 | bytes 6291456 | tf_op jit(solution)/shard_map/inner_convs/pallas_call | solution.py:464
  51.3 5.4 %edge_convs.1 = (bf16[8,2,128,256]{3,2,1,0:T(8,128)(2,1)S(1)}, f32[128,8,128]{2,1,0:T(8,128)S(1)}, bf16[3,64,128]{2,1,0:T(8,128)(2,1)S(1)}, bf16[3,64,128]{2,1,0:T(8,128)(2,1)S(1)}, bf16[2,64,128]{2,1,0:T(8,128)(2,1)S(1)}) custom-call(bf16[8,144,128]{2,1,0:T(8,128)(2,1)S(1)} %collective-permute-done.8.ra, ...), custom_call_target="tpu_custom_call" | custom-call | flops 2717908992 | bytes 6291456 | tf_op jit(solution)/shard_map/edge_convs/pallas_call | solution.py:582
  56.7 0.1 collective-permute-start.10
  56.8 0.3 collective-permute-start.11
  57.1 1.8 %turn.1 = bf16[32,16,8,128]{3,2,1,0:T(8,128)(2,1)} custom-call(bf16[8,2,128,256]{3,2,1,0:T(8,128)(2,1)S(1)} %get-tuple-element.93.total), custom_call_target="tpu_custom_call" | custom-call | flops 1000 | bytes 8388608 | tf_op jit(solution)/shard_map/turn/pallas_call | solution.py:610
  58.9 2.7 %collective-permute-done.11.yb = bf16[3,64,128]{2,1,0:T(8,128)(2,1)S(1)} collective-permute-done((bf16[3,64,128]{2,1,0:T(8,128)(2,1)S(1)}, bf16[3,64,128]{2,1,0:T(8,128)(2,1)S(1)}, u32[]{:S(2)}, u32[]{:S(2)}) %collective-permute-start.11) | collective-permute-done | bytes 49184 | tf_op jit(solution)/shard_map/ppermute | solution.py:869
  61.6 0.1 collective-permute-start.12
  61.7 2.4 %collective-permute-start.13 = (bf16[3,64,128]{2,1,0:T(8,128)(2,1)S(1)}, bf16[3,64,128]{2,1,0:T(8,128)(2,1)S(1)}, u32[]{:S(2)}, u32[]{:S(2)}) collective-permute-start(bf16[3,64,128]{2,1,0:T(8,128)(2,1)S(1)} %pad_maximum_fusion.1), channel_id=1, source_target_pairs={{0,120},{8,16},{16,8},{24,32},{32,24},{40,48},{48,40},{56,64},{64,... | collective-permute-start | bytes 147464 | tf_op jit(solution)/shard_map/ppermute | solution.py:869
  64.1 4.3 %own_read.1 = (f32[3,16384]{1,0:T(4,128)S(1)}, bf16[16384,128]{1,0:T(8,128)(2,1)S(1)}) custom-call(s32[256]{0:T(256)S(1)} %copy-done.9, f32[128,8,128]{2,1,0:T(8,128)S(1)} %get-tuple-element.101.table, bf16[32768,128]{1,0:T(8,128)(2,1)} %w_hbm.5), custom_call_target="tpu_custom_call" | custom-call | flops 134217728 | bytes 9437184 | tf_op jit(solution)/shard_map/own_read/pallas_call | solution.py:678
  68.4 1.0 %collective-permute-done.13.xb = bf16[3,64,128]{2,1,0:T(8,128)(2,1)S(1)} collective-permute-done((bf16[3,64,128]{2,1,0:T(8,128)(2,1)S(1)}, bf16[3,64,128]{2,1,0:T(8,128)(2,1)S(1)}, u32[]{:S(2)}, u32[]{:S(2)}) %collective-permute-start.13) | collective-permute-done | bytes 49184 | tf_op jit(solution)/shard_map/ppermute | solution.py:869
  69.4 2.6 %far_read.1 = f32[3,32768]{1,0:T(4,128)} custom-call(s32[128]{0:T(128)S(1)} %copy-done.13, s32[1]{0:T(128)S(6)} %copy.17.counts_h.counts, bf16[3,64,128]{2,1,0:T(8,128)(2,1)S(1)} %collective-permute-done.12.xa, bf16[3,64,128]{2,1,0:T(8,128)(2,1)S(1)} %collective-permute-done.13.xb, bf16[3,64,128]{2,1,0:T(8,128)(2,1)S(1)} %collective-permute-done.10.ya, ...), custom_call_target="tpu_custom_call" | custom-call | flops 134217728 | bytes 5242880 | tf_op jit(solution)/shard_map/far_read/pallas_call | solution.py:733
  (39 shorter events, 0.1 us)
Async XLA Ops:
  6.3 13.5 %collective-permute-start = (bf16[1584,128]{1,0:T(8,128)(2,1)}, bf16[1584,128]{1,0:T(8,128)(2,1)S(1)}, u32[]{:S(2)}, u32[]{:S(2)}) collective-permute-start(bf16[1584,128]{1,0:T(8,128)(2,1)} %get-tuple-element.61), channel_id=1, source_target_pairs={{0,8},{8,0},{16,24},{24,16},{32,40},{40,32},{48,56},{56,48},{64,72... | collective-permute-start | bytes 1216520 | tf_op jit(solution)/shard_map/ppermute | solution.py:869
  8.0 9.9 %copy-start.2 = (bf16[128,2048]{1,0:T(8,128)(2,1)S(1)}, bf16[128,2048]{1,0:T(8,128)(2,1)}, u32[]{:S(2)}) copy-start(bf16[128,2048]{1,0:T(8,128)(2,1)} %constant.13.clone.e2a) | copy-start | bytes 1572868
  8.0 10.0 %copy-start.3 = (bf16[128,2048]{1,0:T(8,128)(2,1)S(1)}, bf16[128,2048]{1,0:T(8,128)(2,1)}, u32[]{:S(2)}) copy-start(bf16[128,2048]{1,0:T(8,128)(2,1)} %constant.10.clone.e1a) | copy-start | bytes 1572868
  8.0 10.0 %copy-start.4 = (bf16[128,1024]{1,0:T(8,128)(2,1)S(1)}, bf16[128,1024]{1,0:T(8,128)(2,1)}, u32[]{:S(2)}) copy-start(bf16[128,1024]{1,0:T(8,128)(2,1)} %constant.14.clone.e2b) | copy-start | bytes 786436
  8.0 10.0 %copy-start.5 = (bf16[128,1024]{1,0:T(8,128)(2,1)S(1)}, bf16[128,1024]{1,0:T(8,128)(2,1)}, u32[]{:S(2)}) copy-start(bf16[128,1024]{1,0:T(8,128)(2,1)} %constant.11.clone.e1o) | copy-start | bytes 786436
  8.0 10.0 %copy-start.6 = (bf16[27,32,32]{2,1,0:T(8,128)(2,1)S(1)}, bf16[27,32,32]{2,1,0:T(8,128)(2,1)}, u32[]{:S(2)}) copy-start(bf16[27,32,32]{2,1,0:T(8,128)(2,1)} %c1.1) | copy-start | bytes 165892
  8.0 10.0 %copy-start.7 = (bf16[27,32,32]{2,1,0:T(8,128)(2,1)S(1)}, bf16[27,32,32]{2,1,0:T(8,128)(2,1)}, u32[]{:S(2)}) copy-start(bf16[27,32,32]{2,1,0:T(8,128)(2,1)} %c2.1) | copy-start | bytes 165892
  8.0 10.0 %copy-start.8 = (bf16[128,512]{1,0:T(8,128)(2,1)S(1)}, bf16[128,512]{1,0:T(8,128)(2,1)}, u32[]{:S(2)}) copy-start(bf16[128,512]{1,0:T(8,128)(2,1)} %constant.12.clone.e1r) | copy-start | bytes 393220
  8.0 10.0 %copy-start.10 = (bf16[3,32]{1,0:T(4,128)(2,1)S(1)}, bf16[3,32]{1,0:T(4,128)(2,1)}, u32[]{:S(2)}) copy-start(bf16[3,32]{1,0:T(4,128)(2,1)} %head.1) | copy-start | bytes 580
  8.0 10.0 %copy-start.11 = (f32[32]{0:T(128)S(1)}, f32[32]{0:T(128)}, u32[]{:S(2)}) copy-start(f32[32]{0:T(128)} %param.21) | copy-start | bytes 388
  8.1 10.0 %copy-start.12 = (f32[32]{0:T(128)S(1)}, f32[32]{0:T(128)}, u32[]{:S(2)}) copy-start(f32[32]{0:T(128)} %param.23) | copy-start | bytes 388
  8.1 14.4 %collective-permute-start.1 = (bf16[1584,128]{1,0:T(8,128)(2,1)}, bf16[1584,128]{1,0:T(8,128)(2,1)S(1)}, u32[]{:S(2)}, u32[]{:S(2)}) collective-permute-start(bf16[1584,128]{1,0:T(8,128)(2,1)} %get-tuple-element.62), channel_id=1, source_target_pairs={{0,120},{8,16},{16,8},{24,32},{32,24},{40,48},{48,40},{56,64},{64,... | collective-permute-start | bytes 1216520 | tf_op jit(solution)/shard_map/ppermute | solution.py:869
  17.9 4.6 %copy-start.1 = (bf16[1584,128]{1,0:T(8,128)(2,1)S(1)}, bf16[1584,128]{1,0:T(8,128)(2,1)}, u32[]{:S(2)}) copy-start(bf16[1584,128]{1,0:T(8,128)(2,1)} %get-tuple-element.66.mid) | copy-start | bytes 1216516
  17.9 8.9 %copy-start = (bf16[2,16,128,128]{3,2,1,0:T(8,128)(2,1)S(1)}, bf16[2,16,128,128]{3,2,1,0:T(8,128)(2,1)}, u32[]{:S(2)}) copy-start(bf16[2,16,128,128]{3,2,1,0:T(8,128)(2,1)} %own_splat.1.own) | copy-start | bytes 3145732
  22.5 13.5 %collective-permute-start.2 = (bf16[1584,128]{1,0:T(8,128)(2,1)S(1)}, bf16[1584,128]{1,0:T(8,128)(2,1)S(1)}, u32[]{:S(2)}, u32[]{:S(2)}) collective-permute-start(bf16[1584,128]{1,0:T(8,128)(2,1)S(1)} %get-tuple-element.67), channel_id=1, source_target_pairs={{0,1},{1,0},{2,3},{3,2},{4,5},{5,4},{6,7},{7,6},{8,9},{9,8},{10,11... | collective-permute-start | bytes 1216520 | tf_op jit(solution)/shard_map/ppermute | solution.py:869
  22.6 13.5 %collective-permute-start.3 = (bf16[1584,128]{1,0:T(8,128)(2,1)S(1)}, bf16[1584,128]{1,0:T(8,128)(2,1)S(1)}, u32[]{:S(2)}, u32[]{:S(2)}) collective-permute-start(bf16[1584,128]{1,0:T(8,128)(2,1)S(1)} %get-tuple-element.68), channel_id=1, source_target_pairs={{0,7},{1,2},{2,1},{3,4},{4,3},{5,6},{6,5},{7,0},{8,15},{9,10},{10,... | collective-permute-start | bytes 1216520 | tf_op jit(solution)/shard_map/ppermute | solution.py:869
  28.9 2.2 %collective-permute-start.4 = (bf16[4,16,128]{2,1,0:T(8,128)(2,1)S(1)}, bf16[4,16,128]{2,1,0:T(8,128)(2,1)S(1)}, u32[]{:S(2)}, u32[]{:S(2)}) collective-permute-start(bf16[4,16,128]{2,1,0:T(8,128)(2,1)S(1)} %get-tuple-element.71), channel_id=1, source_target_pairs={{0,1},{1,0},{2,3},{3,2},{4,5},{5,4},{6,7},{7,6},{8,9},{9,8},{10,11... | collective-permute-start | bytes 49160 | tf_op jit(solution)/shard_map/ppermute | solution.py:869
  29.0 4.5 %collective-permute-start.5 = (bf16[4,16,128]{2,1,0:T(8,128)(2,1)S(1)}, bf16[4,16,128]{2,1,0:T(8,128)(2,1)S(1)}, u32[]{:S(2)}, u32[]{:S(2)}) collective-permute-start(bf16[4,16,128]{2,1,0:T(8,128)(2,1)S(1)} %get-tuple-element.72), channel_id=1, source_target_pairs={{0,7},{1,2},{2,1},{3,4},{4,3},{5,6},{6,5},{7,0},{8,15},{9,10},{10,... | collective-permute-start | bytes 49160 | tf_op jit(solution)/shard_map/ppermute | solution.py:869
  29.5 4.0 %collective-permute-start.6 = (bf16[4,16,128]{2,1,0:T(8,128)(2,1)S(1)}, bf16[4,16,128]{2,1,0:T(8,128)(2,1)S(1)}, u32[]{:S(2)}, u32[]{:S(2)}) collective-permute-start(bf16[4,16,128]{2,1,0:T(8,128)(2,1)S(1)} %get-tuple-element.73), channel_id=1, source_target_pairs={{0,2},{1,3},{2,0},{3,1},{4,6},{5,7},{6,4},{7,5},{8,10},{9,11},{10,... | collective-permute-start | bytes 49160 | tf_op jit(solution)/shard_map/ppermute | solution.py:869
  31.1 5.0 %collective-permute-start.7 = (bf16[4,16,128]{2,1,0:T(8,128)(2,1)S(1)}, bf16[4,16,128]{2,1,0:T(8,128)(2,1)S(1)}, u32[]{:S(2)}, u32[]{:S(2)}) collective-permute-start(bf16[4,16,128]{2,1,0:T(8,128)(2,1)S(1)} %get-tuple-element.74), channel_id=1, source_target_pairs={{0,6},{1,7},{2,4},{3,5},{4,2},{5,3},{6,0},{7,1},{8,14},{9,15},{10,... | collective-permute-start | bytes 49160 | tf_op jit(solution)/shard_map/ppermute | solution.py:869
  38.4 12.9 %collective-permute-start.8 = (bf16[8,144,128]{2,1,0:T(8,128)(2,1)S(1)}, bf16[8,144,128]{2,1,0:T(8,128)(2,1)S(1)}, u32[]{:S(2)}, u32[]{:S(2)}) collective-permute-start(bf16[8,144,128]{2,1,0:T(8,128)(2,1)S(1)} %get-tuple-element.77), channel_id=1, source_target_pairs={{0,8},{8,0},{16,24},{24,16},{32,40},{40,32},{48,56},{56,48},{64,72... | collective-permute-start | bytes 884744 | tf_op jit(solution)/shard_map/ppermute | solution.py:869
  38.5 12.8 %collective-permute-start.9 = (bf16[8,144,128]{2,1,0:T(8,128)(2,1)S(1)}, bf16[8,144,128]{2,1,0:T(8,128)(2,1)S(1)}, u32[]{:S(2)}, u32[]{:S(2)}) collective-permute-start(bf16[8,144,128]{2,1,0:T(8,128)(2,1)S(1)} %get-tuple-element.78), channel_id=1, source_target_pairs={{0,120},{8,16},{16,8},{24,32},{32,24},{40,48},{48,40},{56,64},{64,... | collective-permute-start | bytes 884744 | tf_op jit(solution)/shard_map/ppermute | solution.py:869
  56.7 7.4 %copy-start.9 = (s32[256]{0:T(256)S(1)}, s32[256]{0:T(256)}, u32[]{:S(2)}) copy-start(s32[256]{0:T(256)} %ids.3) | copy-start | bytes 3076
  56.7 2.2 %collective-permute-start.10 = (bf16[3,64,128]{2,1,0:T(8,128)(2,1)S(1)}, bf16[3,64,128]{2,1,0:T(8,128)(2,1)S(1)}, u32[]{:S(2)}, u32[]{:S(2)}) collective-permute-start(bf16[3,64,128]{2,1,0:T(8,128)(2,1)S(1)} %get-tuple-element.94), channel_id=1, source_target_pairs={{0,1},{1,0},{2,3},{3,2},{4,5},{5,4},{6,7},{7,6},{8,9},{9,8},{10,11... | collective-permute-start | bytes 147464 | tf_op jit(solution)/shard_map/ppermute | solution.py:869
  56.8 4.8 %collective-permute-start.11 = (bf16[3,64,128]{2,1,0:T(8,128)(2,1)S(1)}, bf16[3,64,128]{2,1,0:T(8,128)(2,1)S(1)}, u32[]{:S(2)}, u32[]{:S(2)}) collective-permute-start(bf16[3,64,128]{2,1,0:T(8,128)(2,1)S(1)} %get-tuple-element.95), channel_id=1, source_target_pairs={{0,7},{1,2},{2,1},{3,4},{4,3},{5,6},{6,5},{7,0},{8,15},{9,10},{10,... | collective-permute-start | bytes 147464 | tf_op jit(solution)/shard_map/ppermute | solution.py:869
  61.6 6.8 %collective-permute-start.12 = (bf16[3,64,128]{2,1,0:T(8,128)(2,1)S(1)}, bf16[3,64,128]{2,1,0:T(8,128)(2,1)S(1)}, u32[]{:S(2)}, u32[]{:S(2)}) collective-permute-start(bf16[3,64,128]{2,1,0:T(8,128)(2,1)S(1)} %pad_maximum_fusion), channel_id=1, source_target_pairs={{0,8},{8,0},{16,24},{24,16},{32,40},{40,32},{48,56},{56,48},{64,72... | collective-permute-start | bytes 147464 | tf_op jit(solution)/shard_map/ppermute | solution.py:869
  61.7 7.7 %collective-permute-start.13 = (bf16[3,64,128]{2,1,0:T(8,128)(2,1)S(1)}, bf16[3,64,128]{2,1,0:T(8,128)(2,1)S(1)}, u32[]{:S(2)}, u32[]{:S(2)}) collective-permute-start(bf16[3,64,128]{2,1,0:T(8,128)(2,1)S(1)} %pad_maximum_fusion.1), channel_id=1, source_target_pairs={{0,120},{8,16},{16,8},{24,32},{32,24},{40,48},{48,40},{56,64},{64,... | collective-permute-start | bytes 147464 | tf_op jit(solution)/shard_map/ppermute | solution.py:869
  64.1 5.3 %copy-start.13 = (s32[128]{0:T(128)S(1)}, s32[128]{0:T(128)}, u32[]{:S(2)}) copy-start(s32[128]{0:T(128)} %get-tuple-element.97.slots) | copy-start | bytes 1540

commit v6 on v5

--- a/solution.py
+++ b/solution.py
@@ -410,6 +410,7 @@
 
 
 PAIRS = SLAB // 2
+FETCHES = 8
 
 
 def window(ref, n, k):
@@ -421,20 +422,34 @@
     return out
 
 
-def inner_kernel(x, g, t1, t1o, b1, t2, b2, part, pre, xs, hs):
+def inner_kernel(x, g, t1, t1o, b1, t2, b2, w_hbm, part, pre, w, xs, xe, hs, sems):
+    lane = lanes_of((1, ROWS, 128))
+    rows = w.shape[0] // FETCHES
+    fetches = [
+        pltpu.make_async_copy(
+            w_hbm.at[pl.ds(k * rows, rows)], w.at[pl.ds(k * rows, rows)], sems.at[k]
+        )
+        for k in range(FETCHES)
+    ]
+    for fetch in fetches:
+        fetch.start()
     iy = lax.axis_index("gy")
     for dy in range(3):
         xs[dy, 0, 0] = jnp.zeros((ROWS, 256), BF16)
         xs[dy, PAIRS, 1] = jnp.zeros((ROWS, 256), BF16)
+        xe[dy, 0, 0] = jnp.zeros((ROWS, 128), BF16)
+        xe[dy, PAIRS, 1] = jnp.zeros((ROWS, 128), BF16)
         hs[dy, 0, 0] = jnp.zeros((BY, 256), BF16)
         hs[dy, PAIRS, 1] = jnp.zeros((BY, 256), BF16)
 
     def shift(n, carry):
         for k in range(2):
-            for tx in range(2):
-                v = x[tx, pl.ds(2 * n + k, 1)].astype(F32)
-                for dy, s in enumerate(shifted(v)):
-                    xs[dy, pl.ds(n + k, 1), 1 - k, :, tx * 128 : tx * 128 + 128] = s.astype(BF16)
+            both = [shifted(x[tx, pl.ds(2 * n + k, 1)].astype(F32)) for tx in range(2)]
+            for dy in range(3):
+                s0, s1 = both[0][dy], both[1][dy]
+                xs[dy, pl.ds(n + k, 1), 1 - k, :, 0:128] = s0.astype(BF16)
+                xs[dy, pl.ds(n + k, 1), 1 - k, :, 128:256] = s1.astype(BF16)
+                xe[dy, pl.ds(n + k, 1), 1 - k] = jnp.where(lane < 64, s0, s1).astype(BF16)
         return carry
 
     lax.fori_loop(0, PAIRS, shift, 0)
@@ -448,7 +463,7 @@
                 m = n * 4 + zo
                 hs[dy, m : m + 4, 1 - zo] = s[:, 8 : 8 + BY].astype(BF16)
     for n in range(2):
-        taps = sum([window(xs, n, zi) for zi in range(4)], [])
+        taps = sum([window(xe, n, zi) for zi in range(4)], [])
         acc = jnp.dot(jnp.concatenate(taps, 1), t1o[...], preferred_element_type=F32) + b1[...]
         pre[n] = acc
     for n in range(2):
@@ -457,26 +472,31 @@
             taps += [g[tx, n * 4 : n * 4 + 4, zo].reshape(4 * BY, 128) for tx in range(2)]
             acc = jnp.dot(jnp.concatenate(taps, 1), t2[...], preferred_element_type=F32) + b2[...]
             part[n * 4 : n * 4 + 4, zo] = acc.reshape(4, BY, 256)
-
-
-def inner_convs(x, g, t1, t1o, b1, t2, b2):
+    for fetch in fetches:
+        fetch.wait()
+
+
+def inner_convs(x, g, t1, t1o, b1, t2, b2, weights):
     vm = pl.BlockSpec(memory_space=VMEM)
     return pl.pallas_call(
         inner_kernel,
-        in_specs=[vm] * 7,
-        out_specs=[vm, vm],
+        in_specs=[vm] * 7 + [pl.BlockSpec(memory_space=pl.ANY)],
+        out_specs=[vm, vm, vm],
         out_shape=[
             jax.ShapeDtypeStruct((PAIRS, 2, BY, 256), F32),
             jax.ShapeDtypeStruct((2, 4 * ROWS, 256), F32),
+            jax.ShapeDtypeStruct(weights.shape, BF16),
         ],
         scratch_shapes=[
             VMEM((3, PAIRS + 1, 2, ROWS, 256), BF16),
+            VMEM((3, PAIRS + 1, 2, ROWS, 128), BF16),
             VMEM((3, PAIRS + 1, 2, BY, 256), BF16),
+            pltpu.SemaphoreType.DMA((FETCHES,)),
         ],
         compiler_params=params(32),
         cost_estimate=cost(2 * 20 * 256 * 256 * 2304, 6 * MIB),
         name="inner_convs",
-    )(x, g.reshape(2, PAIRS, 2, BY, 128), t1, t1o, b1, t2, b2)
+    )(x, g.reshape(2, PAIRS, 2, BY, 128), t1, t1o, b1, t2, b2, weights)
 
 
 def tile_row(tile):
@@ -635,7 +655,7 @@
     for b in range(BATCH):
         v = r[4 * b : 4 * b + 3]
         if count is not None:
-            v = jnp.where(128 + first + b < count, v, 0.0)
+            v = jnp.where(first + b < count, v, 0.0)
         out[:, at + b * 128 : at + (b + 1) * 128] = v
 
 
@@ -644,54 +664,28 @@
     return jnp.where(row < 4, r0, pltpu.roll(r1, 4, 0))
 
 
-def weight_copies(w_hbm, wv, sems, first):
-    n = 128 // BATCH
-    rows = BATCH * 128
-    return [
-        pltpu.make_async_copy(
-            w_hbm.at[pl.ds(first * 128 + k * rows, rows)], wv.at[pl.ds(k * rows, rows)], sems.at[k]
-        )
-        for k in range(n)
-    ]
-
-
-def own_read_kernel(ids, table, w_hbm, out, far_w, wv, sems, fsems):
-    copies = weight_copies(w_hbm, wv, sems, 0)
-    later = weight_copies(w_hbm, far_w, fsems, 128)
-    for copy in copies + later:
-        copy.start()
-    for k, copy in enumerate(copies):
+def own_read_kernel(ids, table, w, out):
+    for k in range(128 // BATCH):
         rows = [
             two_blocks(
                 table[tile_row(ids[k * BATCH + 2 * j])], table[tile_row(ids[k * BATCH + 2 * j + 1])]
             )
             for j in range(BATCH // 2)
         ]
-        copy.wait()
-        read_batch(jnp.concatenate(rows, 0), wv, k * BATCH, out, k * BATCH * 128, None)
-    for copy in later:
-        copy.wait()
-
-
-def own_read(ids, table, weights, particles):
+        read_batch(jnp.concatenate(rows, 0), w, k * BATCH, out, k * BATCH * 128, None)
+
+
+def own_read(ids, table, w):
     vm = pl.BlockSpec(memory_space=VMEM)
     return pl.pallas_call(
         own_read_kernel,
-        in_specs=[pl.BlockSpec(memory_space=SMEM), vm, pl.BlockSpec(memory_space=pl.ANY)],
-        out_specs=[vm, vm],
-        out_shape=[
-            jax.ShapeDtypeStruct((3, particles // 2), F32),
-            jax.ShapeDtypeStruct((particles // 2, 128), BF16),
-        ],
-        scratch_shapes=[
-            VMEM((particles // 2, 128), BF16),
-            pltpu.SemaphoreType.DMA((128 // BATCH,)),
-            pltpu.SemaphoreType.DMA((128 // BATCH,)),
-        ],
-        compiler_params=params(48),
+        in_specs=[pl.BlockSpec(memory_space=SMEM), vm, vm],
+        out_specs=vm,
+        out_shape=jax.ShapeDtypeStruct((3, w.shape[0] // 2), F32),
+        compiler_params=params(24),
         cost_estimate=cost(2 * 128 * 32 * 128 * 128, 9 * MIB),
         name="own_read",
-    )(ids, table, weights)
+    )(ids, table, w)
 
 
 def far_read_kernel(slots, counts, xa, xb, ya, yb, w, near, out, table, made, sems):
@@ -716,7 +710,7 @@
             two_blocks(table[slots[k * BATCH + 2 * j]], table[slots[k * BATCH + 2 * j + 1]])
             for j in range(BATCH // 2)
         ]
-        read_batch(jnp.concatenate(rows, 0), w, k * BATCH, made.at[k], 0, counts[0])
+        read_batch(jnp.concatenate(rows, 0), w, 128 + k * BATCH, made.at[k], 0, counts[0])
         copies.append(
             pltpu.make_async_copy(
                 made.at[k], out.at[:, pl.ds(half + k * size, size)], sems.at[k]
@@ -821,7 +815,7 @@
     inner = [none, 1, 2, 3, 4, 5, 6, none]
     every = list(range(8))
     e1a = band(every, inner, False)
-    e1o = band(every, [-1, 0, 7, 8], False)
+    e1o = band([0, 1, 6, 7], [-1, 0, 7, 8], False)
     e1r = band([-2, -1, 8, 9], [-1, 0, 7, 8], False)
     e2a = band(inner, every, True)
     e2b = band([-1, 0, 7, 8], every, True)
@@ -832,7 +826,7 @@
         out_specs=[vm] * 8,
         out_shape=[
             jax.ShapeDtypeStruct((2304, 256), BF16),
-            jax.ShapeDtypeStruct((3072, 256), BF16),
+            jax.ShapeDtypeStruct((1536, 256), BF16),
             jax.ShapeDtypeStruct((1536, 256), BF16),
             jax.ShapeDtypeStruct((2560, 256), BF16),
             jax.ShapeDtypeStruct((1152, 256), BF16),
@@ -858,7 +852,6 @@
     bias_second,
     head,
 ):
-    particles = features.shape[1]
 
     def swap(x, axis, partner, reach=1):
         size = lax.axis_size(axis)
@@ -891,19 +884,19 @@
 
     xb = swap(to_b, "gx", "b")
     xa = swap(to_a, "gx", "a")
-    part, pre = inner_convs(x, g, t1a, t1o, b1, t2a, b2)
+    part, pre, w = inner_convs(x, g, t1a, t1o, b1, t2a, b2, weights)
     total, table, ans_ya, ans_yb, ans_x = edge_convs(xa, xb, part, pre, t1r, t2b, headx, ids, idx)
 
     back_ya = swap(ans_ya, "gy", "a")
     back_yb = swap(ans_yb, "gy", "b")
     grid_out = turn(total)
     grid_out, back_ya, back_yb = lax.optimization_barrier((grid_out, back_ya, back_yb))
-    near, far_w = own_read(tile_ids, table, weights, particles)
+    near = own_read(tile_ids, table, w)
     to_a = jnp.stack([back_ya[0], ans_x[0], back_yb[0]])
     to_b = jnp.stack([back_ya[2], ans_x[1], back_yb[2]])
     back_xb = swap(to_b, "gx", "b")
     back_xa = swap(to_a, "gx", "a")
-    velocity = far_read(slots, counts, back_xa, back_xb, back_ya, back_yb, far_w, near)
+    velocity = far_read(slots, counts, back_xa, back_xb, back_ya, back_yb, w, near)
     return grid_out, velocity
 
 

time: 72.4 us -> 72.3 us (level)
  Pallas kernels: 38.7 us -> 36.4 us
  waiting for transfers between devices: 11.4 us -> 13.6 us
    pallas_call x1, Pallas kernels: 4.27 us -> 2.12 us  [own_read(): pl.pallas_call(own_read_kernel, in_specs=[pl.BlockSpec(memory_space=SMEM)...]
    ppermute x14, waiting for transfers between devices: 11.4 us -> 13.6 us  [swap(): return lax.ppermute(x, axis, route)]
  transfers between devices with their start and end apart: 14 -> 14, of which waited for: 5 -> 5; matrix products, arithmetic and copies ran while one was open for 0% -> 0% of each run, Pallas kernels for 32% -> 29%
where the time goes in v6:
time: 72.3 us; the launch traced here: 72.2 us
  Pallas kernels  36.4 us (50%)
  starting transfers between devices  20.3 us (28%)
  waiting for transfers between devices  13.6 us (19%)
  between operations  1.77 us (2%)
    ppermute x14, starting transfers between devices, swap(): return lax.ppermute(x, axis, route)  20.3 us
    ppermute x14, waiting for transfers between devices, swap(): return lax.ppermute(x, axis, route)  13.6 us
    pallas_call x1, Pallas kernels, inner_convs(): pl.pallas_call(inner_kernel, in_specs=[vm] * 7 + [pl.BlockSpec(memory_spa...  8.1 us
    pallas_call x1, Pallas kernels, edge_convs(): pl.pallas_call(edge_kernel, in_specs=[vm] * 7 + [pl.BlockSpec(memory_spac...  5.39 us
    pallas_call x1, Pallas kernels, own_splat(): pl.pallas_call(own_splat_kernel, in_specs=[pl.BlockSpec(memory_space=SMEM...  5.38 us
    pallas_call x1, Pallas kernels, far_splat(): pl.pallas_call(far_splat_kernel, in_specs=[anywhere] * 5, out_specs=[vm,...  4.98 us
    pallas_call x1, Pallas kernels, far_read(): pl.pallas_call(far_read_kernel, in_specs=[smem, smem] + [vm] * 6, out_spe...  2.65 us
    pallas_call x1, Pallas kernels, sum_tiles(): pl.pallas_call(sum_kernel, in_specs=[vm] * 9, out_specs=[vm] * 4 + [pl.Bl...  2.27 us
  transfers between devices with their start and end apart: 14, of which 5 were waited for; matrix products, arithmetic and copies ran while one was open for 0% of the time, Pallas kernels for 29%

profile of v6, /device:TPU:0, one launch (start us, length us, event | category | flops | bytes accessed | tf_op | source)
XLA Modules:
  0.0 72.2 jit_solution(15709528822141773135)
XLA Ops:
  1.3 5.0 %far_splat.1 = (bf16[1584,128]{1,0:T(8,128)(2,1)}, bf16[1584,128]{1,0:T(8,128)(2,1)}, bf16[1584,128]{1,0:T(8,128)(2,1)}, s32[128]{0:T(128)}) custom-call(s32[256]{0:T(256)} %owners_h.1, s32[256]{0:T(256)} %ids.3, s32[1]{0:T(128)S(6)} %copy.17.counts_h.counts, bf16[32,32768]{1,0:T(8,128)(2,1)} %f_hbm.3, bf16[32768,128]{1,0:T(8,128)(2,1)} %w_hbm.5), custom_call_target="tpu_custom_call" | custom-call | flops 134217728 | bytes 6291456 | tf_op jit(solution)/shard_map/far_splat/pallas_call | solution.py:146
  6.3 1.7 %collective-permute-start = (bf16[1584,128]{1,0:T(8,128)(2,1)}, bf16[1584,128]{1,0:T(8,128)(2,1)S(1)}, u32[]{:S(2)}, u32[]{:S(2)}) collective-permute-start(bf16[1584,128]{1,0:T(8,128)(2,1)} %get-tuple-element.60), channel_id=1, source_target_pairs={{0,8},{8,0},{16,24},{24,16},{32,40},{40,32},{48,56},{56,48},{64,72... | collective-permute-start | bytes 1216520 | tf_op jit(solution)/shard_map/ppermute | solution.py:862
  8.0 0.0 copy-start.7
  8.0 0.0 copy-start.8
  8.1 4.5 %collective-permute-start.1 = (bf16[1584,128]{1,0:T(8,128)(2,1)}, bf16[1584,128]{1,0:T(8,128)(2,1)S(1)}, u32[]{:S(2)}, u32[]{:S(2)}) collective-permute-start(bf16[1584,128]{1,0:T(8,128)(2,1)} %get-tuple-element.61), channel_id=1, source_target_pairs={{0,120},{8,16},{16,8},{24,32},{32,24},{40,48},{48,40},{56,64},{64,... | collective-permute-start | bytes 1216520 | tf_op jit(solution)/shard_map/ppermute | solution.py:862
  12.5 5.4 %own_splat.1.own = bf16[2,16,128,128]{3,2,1,0:T(8,128)(2,1)} custom-call(s32[256]{0:T(256)} %ids.3, bf16[32,32768]{1,0:T(8,128)(2,1)} %f_hbm.3, bf16[32768,128]{1,0:T(8,128)(2,1)} %w_hbm.5), custom_call_target="tpu_custom_call" | custom-call | flops 134217728 | bytes 6291456 | tf_op jit(solution)/shard_map/own_splat/pallas_call | solution.py:192
  18.0 1.6 %prepare.1 = (bf16[2304,256]{1,0:T(8,128)(2,1)S(1)}, bf16[1536,256]{1,0:T(8,128)(2,1)S(1)}, bf16[1536,256]{1,0:T(8,128)(2,1)S(1)}, bf16[2560,256]{1,0:T(8,128)(2...) custom-call(bf16[27,32,32]{2,1,0:T(8,128)(2,1)S(1)} %copy-done.5, ...), custom_call_target="tpu_custom_call" | custom-call | flops 471859200 | bytes 5242880 | tf_op jit(solution)/shard_map/prepare/pallas_call | solution.py:823
  19.6 2.8 %collective-permute-done.1.xb = bf16[1584,128]{1,0:T(8,128)(2,1)S(1)} collective-permute-done((bf16[1584,128]{1,0:T(8,128)(2,1)}, bf16[1584,128]{1,0:T(8,128)(2,1)S(1)}, u32[]{:S(2)}, u32[]{:S(2)}) %collective-permute-start.1) | collective-permute-done | bytes 405536 | tf_op jit(solution)/shard_map/ppermute | solution.py:862
  22.5 0.1 bundle.1
  22.5 0.1 collective-permute-start.2
  22.6 4.2 %collective-permute-start.3 = (bf16[1584,128]{1,0:T(8,128)(2,1)S(1)}, bf16[1584,128]{1,0:T(8,128)(2,1)S(1)}, u32[]{:S(2)}, u32[]{:S(2)}) collective-permute-start(bf16[1584,128]{1,0:T(8,128)(2,1)S(1)} %get-tuple-element.67), channel_id=1, source_target_pairs={{0,7},{1,2},{2,1},{3,4},{4,3},{5,6},{6,5},{7,0},{8,15},{9,10},{10,... | collective-permute-start | bytes 1216520 | tf_op jit(solution)/shard_map/ppermute | solution.py:862
  26.8 2.1 %column.1 = (f32[2,16,128,128]{3,2,1,0:T(8,128)S(1)}, s32[8,128]{1,0:T(8,128)S(1)}, bf16[4,16,128]{2,1,0:T(8,128)(2,1)S(1)}, bf16[4,16,128]{2,1,0:T(8,128)(2,1)S...) custom-call(bf16[2,16,128,128]{3,2,1,0:T(8,128)(2,1)S(1)} %copy-done, ...), custom_call_target="tpu_custom_call" | custom-call | flops 1000 | bytes 4194304 | tf_op jit(solution)/shard_map/column/pallas_call | solution.py:294
  28.9 0.1 collective-permute-start.4
  29.0 0.5 collective-permute-start.5
  29.5 1.7 %collective-permute-start.6 = (bf16[4,16,128]{2,1,0:T(8,128)(2,1)S(1)}, bf16[4,16,128]{2,1,0:T(8,128)(2,1)S(1)}, u32[]{:S(2)}, u32[]{:S(2)}) collective-permute-start(bf16[4,16,128]{2,1,0:T(8,128)(2,1)S(1)} %get-tuple-element.72), channel_id=1, source_target_pairs={{0,2},{1,3},{2,0},{3,1},{4,6},{5,7},{6,4},{7,5},{8,10},{9,11},{10,... | collective-permute-start | bytes 49160 | tf_op jit(solution)/shard_map/ppermute | solution.py:862
  31.1 0.1 collective-permute-start.7
  31.2 2.3 %collective-permute-done.5.next_b = bf16[4,16,128]{2,1,0:T(8,128)(2,1)S(1)} collective-permute-done((bf16[4,16,128]{2,1,0:T(8,128)(2,1)S(1)}, bf16[4,16,128]{2,1,0:T(8,128)(2,1)S(1)}, u32[]{:S(2)}, u32[]{:S(2)}) %collective-permute-start.5) | collective-permute-done | bytes 16416 | tf_op jit(solution)/shard_map/ppermute | solution.py:862
  33.4 2.6 %collective-permute-done.7.far_b = bf16[4,16,128]{2,1,0:T(8,128)(2,1)S(1)} collective-permute-done((bf16[4,16,128]{2,1,0:T(8,128)(2,1)S(1)}, bf16[4,16,128]{2,1,0:T(8,128)(2,1)S(1)}, u32[]{:S(2)}, u32[]{:S(2)}) %collective-permute-start.7) | collective-permute-done | bytes 16416 | tf_op jit(solution)/shard_map/ppermute | solution.py:862
  36.1 2.3 %sum_tiles.1 = (bf16[2,16,128,128]{3,2,1,0:T(8,128)(2,1)S(1)}, bf16[2,16,144,128]{3,2,1,0:T(8,128)(2,1)S(1)}, bf16[8,144,128]{2,1,0:T(8,128)(2,1)S(1)}, bf16[8,144,128]{2,1,0:T(8,128)(2,1)S(1)}, s32[8,128]{1,0:T(8,128)S(1)}) custom-call(f32[2,16,128,128]{3,2,1,0:T(8,128)S(1)} %get-tuple-element.69.part, bf16[1584,128]{1,0:T(8,128)(2,1)S(1)} %collective-permute-done.2.ya, ...), custom_call_target="tpu_custom_call" | custom-call | flops 1000 | bytes 4194304 | tf_op jit(solution)/shard_map/sum_tiles/pallas_call | solution.py:379
  38.4 0.1 collective-permute-start.8
  38.4 4.6 %collective-permute-start.9 = (bf16[8,144,128]{2,1,0:T(8,128)(2,1)S(1)}, bf16[8,144,128]{2,1,0:T(8,128)(2,1)S(1)}, u32[]{:S(2)}, u32[]{:S(2)}) collective-permute-start(bf16[8,144,128]{2,1,0:T(8,128)(2,1)S(1)} %get-tuple-element.77), channel_id=1, source_target_pairs={{0,120},{8,16},{16,8},{24,32},{32,24},{40,48},{48,40},{56,64},{64,... | collective-permute-start | bytes 884744 | tf_op jit(solution)/shard_map/ppermute | solution.py:862
  43.1 8.1 %inner_convs.1 = (f32[8,2,128,256]{3,2,1,0:T(8,128)S(1)}, f32[2,576,256]{2,1,0:T(8,128)S(1)}, bf16[32768,128]{1,0:T(8,128)(2,1)S(1)}) custom-call(bf16[2,16,144,128]{3,2,1,0:T(8,128)(2,1)S(1)} %get-tuple-element.78.x, bf16[2,8,2,128,128]{4,3,2,1,0:T(8,128)(2,1)S(1)} %bitcast.5, bf16[2304,256]{1,0:T(8,128)(2,1)S(1)} %get-tuple-element.80.t1, ...), custom_call_target="tpu_custom_call" | custom-call | flops 6039797760 | bytes 6291456 | tf_op jit(solution)/shard_map/inner_convs/pallas_call | solution.py:481
  51.2 5.4 %edge_convs.1 = (bf16[8,2,128,256]{3,2,1,0:T(8,128)(2,1)S(1)}, f32[128,8,128]{2,1,0:T(8,128)S(1)}, bf16[3,64,128]{2,1,0:T(8,128)(2,1)S(1)}, bf16[3,64,128]{2,1,0:T(8,128)(2,1)S(1)}, bf16[2,64,128]{2,1,0:T(8,128)(2,1)S(1)}) custom-call(bf16[8,144,128]{2,1,0:T(8,128)(2,1)S(1)} %collective-permute-done.8.ra, ...), custom_call_target="tpu_custom_call" | custom-call | flops 2717908992 | bytes 6291456 | tf_op jit(solution)/shard_map/edge_convs/pallas_call | solution.py:602
  56.6 0.1 collective-permute-start.10
  56.7 0.3 collective-permute-start.11
  57.0 1.8 %turn.1 = bf16[32,16,8,128]{3,2,1,0:T(8,128)(2,1)} custom-call(bf16[8,2,128,256]{3,2,1,0:T(8,128)(2,1)S(1)} %get-tuple-element.92.total), custom_call_target="tpu_custom_call" | custom-call | flops 1000 | bytes 8388608 | tf_op jit(solution)/shard_map/turn/pallas_call | solution.py:630
  58.8 2.7 %collective-permute-done.11.yb = bf16[3,64,128]{2,1,0:T(8,128)(2,1)S(1)} collective-permute-done((bf16[3,64,128]{2,1,0:T(8,128)(2,1)S(1)}, bf16[3,64,128]{2,1,0:T(8,128)(2,1)S(1)}, u32[]{:S(2)}, u32[]{:S(2)}) %collective-permute-start.11) | collective-permute-done | bytes 49184 | tf_op jit(solution)/shard_map/ppermute | solution.py:862
  61.5 0.1 collective-permute-start.12
  61.6 2.5 %collective-permute-start.13 = (bf16[3,64,128]{2,1,0:T(8,128)(2,1)S(1)}, bf16[3,64,128]{2,1,0:T(8,128)(2,1)S(1)}, u32[]{:S(2)}, u32[]{:S(2)}) collective-permute-start(bf16[3,64,128]{2,1,0:T(8,128)(2,1)S(1)} %pad_maximum_fusion.1), channel_id=1, source_target_pairs={{0,120},{8,16},{16,8},{24,32},{32,24},{40,48},{48,40},{56,64},{64,... | collective-permute-start | bytes 147464 | tf_op jit(solution)/shard_map/ppermute | solution.py:862
  64.1 2.1 %own_read.1.near = f32[3,16384]{1,0:T(4,128)S(1)} custom-call(s32[256]{0:T(256)S(1)} %copy-done.9, f32[128,8,128]{2,1,0:T(8,128)S(1)} %get-tuple-element.101.table, bf16[32768,128]{1,0:T(8,128)(2,1)S(1)} %get-tuple-element.100.w), custom_call_target="tpu_custom_call" | custom-call | flops 134217728 | bytes 9437184 | tf_op jit(solution)/shard_map/own_read/pallas_call | solution.py:680
  66.2 3.1 %collective-permute-done.13.xb = bf16[3,64,128]{2,1,0:T(8,128)(2,1)S(1)} collective-permute-done((bf16[3,64,128]{2,1,0:T(8,128)(2,1)S(1)}, bf16[3,64,128]{2,1,0:T(8,128)(2,1)S(1)}, u32[]{:S(2)}, u32[]{:S(2)}) %collective-permute-start.13) | collective-permute-done | bytes 49184 | tf_op jit(solution)/shard_map/ppermute | solution.py:862
  69.3 2.6 %far_read.1 = f32[3,32768]{1,0:T(4,128)} custom-call(s32[128]{0:T(128)S(1)} %copy-done.13, s32[1]{0:T(128)S(6)} %copy.17.counts_h.counts, bf16[3,64,128]{2,1,0:T(8,128)(2,1)S(1)} %collective-permute-done.12.xa, bf16[3,64,128]{2,1,0:T(8,128)(2,1)S(1)} %collective-permute-done.13.xb, bf16[3,64,128]{2,1,0:T(8,128)(2,1)S(1)} %collective-permute-done.10.ya, ...), custom_call_target="tpu_custom_call" | custom-call | flops 134217728 | bytes 5242880 | tf_op jit(solution)/shard_map/far_read/pallas_call | solution.py:727
  (39 shorter events, 0.1 us)
Async XLA Ops:
  6.3 13.4 %collective-permute-start = (bf16[1584,128]{1,0:T(8,128)(2,1)}, bf16[1584,128]{1,0:T(8,128)(2,1)S(1)}, u32[]{:S(2)}, u32[]{:S(2)}) collective-permute-start(bf16[1584,128]{1,0:T(8,128)(2,1)} %get-tuple-element.60), channel_id=1, source_target_pairs={{0,8},{8,0},{16,24},{24,16},{32,40},{40,32},{48,56},{56,48},{64,72... | collective-permute-start | bytes 1216520 | tf_op jit(solution)/shard_map/ppermute | solution.py:862
  8.0 10.0 %copy-start.2 = (bf16[128,2048]{1,0:T(8,128)(2,1)S(1)}, bf16[128,2048]{1,0:T(8,128)(2,1)}, u32[]{:S(2)}) copy-start(bf16[128,2048]{1,0:T(8,128)(2,1)} %constant.13.clone.e2a) | copy-start | bytes 1572868
  8.0 10.0 %copy-start.3 = (bf16[128,2048]{1,0:T(8,128)(2,1)S(1)}, bf16[128,2048]{1,0:T(8,128)(2,1)}, u32[]{:S(2)}) copy-start(bf16[128,2048]{1,0:T(8,128)(2,1)} %constant.10.clone.e1a) | copy-start | bytes 1572868
  8.0 10.0 %copy-start.4 = (bf16[128,1024]{1,0:T(8,128)(2,1)S(1)}, bf16[128,1024]{1,0:T(8,128)(2,1)}, u32[]{:S(2)}) copy-start(bf16[128,1024]{1,0:T(8,128)(2,1)} %constant.14.clone.e2b) | copy-start | bytes 786436
  8.0 10.0 %copy-start.5 = (bf16[27,32,32]{2,1,0:T(8,128)(2,1)S(1)}, bf16[27,32,32]{2,1,0:T(8,128)(2,1)}, u32[]{:S(2)}) copy-start(bf16[27,32,32]{2,1,0:T(8,128)(2,1)} %c1.1) | copy-start | bytes 165892
  8.0 10.0 %copy-start.6 = (bf16[27,32,32]{2,1,0:T(8,128)(2,1)S(1)}, bf16[27,32,32]{2,1,0:T(8,128)(2,1)}, u32[]{:S(2)}) copy-start(bf16[27,32,32]{2,1,0:T(8,128)(2,1)} %c2.1) | copy-start | bytes 165892
  8.0 10.0 %copy-start.7 = (bf16[128,512]{1,0:T(8,128)(2,1)S(1)}, bf16[128,512]{1,0:T(8,128)(2,1)}, u32[]{:S(2)}) copy-start(bf16[128,512]{1,0:T(8,128)(2,1)} %constant.12.clone.e1r) | copy-start | bytes 393220
  8.0 10.0 %copy-start.8 = (bf16[128,512]{1,0:T(8,128)(2,1)S(1)}, bf16[128,512]{1,0:T(8,128)(2,1)}, u32[]{:S(2)}) copy-start(bf16[128,512]{1,0:T(8,128)(2,1)} %constant.11.clone.e1o) | copy-start | bytes 393220
  8.0 10.0 %copy-start.10 = (bf16[3,32]{1,0:T(4,128)(2,1)S(1)}, bf16[3,32]{1,0:T(4,128)(2,1)}, u32[]{:S(2)}) copy-start(bf16[3,32]{1,0:T(4,128)(2,1)} %head.1) | copy-start | bytes 580
  8.0 10.0 %copy-start.11 = (f32[32]{0:T(128)S(1)}, f32[32]{0:T(128)}, u32[]{:S(2)}) copy-start(f32[32]{0:T(128)} %param.21) | copy-start | bytes 388
  8.0 10.0 %copy-start.12 = (f32[32]{0:T(128)S(1)}, f32[32]{0:T(128)}, u32[]{:S(2)}) copy-start(f32[32]{0:T(128)} %param.23) | copy-start | bytes 388
  8.1 14.4 %collective-permute-start.1 = (bf16[1584,128]{1,0:T(8,128)(2,1)}, bf16[1584,128]{1,0:T(8,128)(2,1)S(1)}, u32[]{:S(2)}, u32[]{:S(2)}) collective-permute-start(bf16[1584,128]{1,0:T(8,128)(2,1)} %get-tuple-element.61), channel_id=1, source_target_pairs={{0,120},{8,16},{16,8},{24,32},{32,24},{40,48},{48,40},{56,64},{64,... | collective-permute-start | bytes 1216520 | tf_op jit(solution)/shard_map/ppermute | solution.py:862
  17.9 4.6 %copy-start.1 = (bf16[1584,128]{1,0:T(8,128)(2,1)S(1)}, bf16[1584,128]{1,0:T(8,128)(2,1)}, u32[]{:S(2)}) copy-start(bf16[1584,128]{1,0:T(8,128)(2,1)} %get-tuple-element.65.mid) | copy-start | bytes 1216516
  17.9 8.9 %copy-start = (bf16[2,16,128,128]{3,2,1,0:T(8,128)(2,1)S(1)}, bf16[2,16,128,128]{3,2,1,0:T(8,128)(2,1)}, u32[]{:S(2)}) copy-start(bf16[2,16,128,128]{3,2,1,0:T(8,128)(2,1)} %own_splat.1.own) | copy-start | bytes 3145732
  22.5 13.5 %collective-permute-start.2 = (bf16[1584,128]{1,0:T(8,128)(2,1)S(1)}, bf16[1584,128]{1,0:T(8,128)(2,1)S(1)}, u32[]{:S(2)}, u32[]{:S(2)}) collective-permute-start(bf16[1584,128]{1,0:T(8,128)(2,1)S(1)} %get-tuple-element.66), channel_id=1, source_target_pairs={{0,1},{1,0},{2,3},{3,2},{4,5},{5,4},{6,7},{7,6},{8,9},{9,8},{10,11... | collective-permute-start | bytes 1216520 | tf_op jit(solution)/shard_map/ppermute | solution.py:862
  22.6 13.4 %collective-permute-start.3 = (bf16[1584,128]{1,0:T(8,128)(2,1)S(1)}, bf16[1584,128]{1,0:T(8,128)(2,1)S(1)}, u32[]{:S(2)}, u32[]{:S(2)}) collective-permute-start(bf16[1584,128]{1,0:T(8,128)(2,1)S(1)} %get-tuple-element.67), channel_id=1, source_target_pairs={{0,7},{1,2},{2,1},{3,4},{4,3},{5,6},{6,5},{7,0},{8,15},{9,10},{10,... | collective-permute-start | bytes 1216520 | tf_op jit(solution)/shard_map/ppermute | solution.py:862
  28.9 2.2 %collective-permute-start.4 = (bf16[4,16,128]{2,1,0:T(8,128)(2,1)S(1)}, bf16[4,16,128]{2,1,0:T(8,128)(2,1)S(1)}, u32[]{:S(2)}, u32[]{:S(2)}) collective-permute-start(bf16[4,16,128]{2,1,0:T(8,128)(2,1)S(1)} %get-tuple-element.70), channel_id=1, source_target_pairs={{0,1},{1,0},{2,3},{3,2},{4,5},{5,4},{6,7},{7,6},{8,9},{9,8},{10,11... | collective-permute-start | bytes 49160 | tf_op jit(solution)/shard_map/ppermute | solution.py:862
  29.0 4.5 %collective-permute-start.5 = (bf16[4,16,128]{2,1,0:T(8,128)(2,1)S(1)}, bf16[4,16,128]{2,1,0:T(8,128)(2,1)S(1)}, u32[]{:S(2)}, u32[]{:S(2)}) collective-permute-start(bf16[4,16,128]{2,1,0:T(8,128)(2,1)S(1)} %get-tuple-element.71), channel_id=1, source_target_pairs={{0,7},{1,2},{2,1},{3,4},{4,3},{5,6},{6,5},{7,0},{8,15},{9,10},{10,... | collective-permute-start | bytes 49160 | tf_op jit(solution)/shard_map/ppermute | solution.py:862
  29.5 4.0 %collective-permute-start.6 = (bf16[4,16,128]{2,1,0:T(8,128)(2,1)S(1)}, bf16[4,16,128]{2,1,0:T(8,128)(2,1)S(1)}, u32[]{:S(2)}, u32[]{:S(2)}) collective-permute-start(bf16[4,16,128]{2,1,0:T(8,128)(2,1)S(1)} %get-tuple-element.72), channel_id=1, source_target_pairs={{0,2},{1,3},{2,0},{3,1},{4,6},{5,7},{6,4},{7,5},{8,10},{9,11},{10,... | collective-permute-start | bytes 49160 | tf_op jit(solution)/shard_map/ppermute | solution.py:862
  31.1 5.0 %collective-permute-start.7 = (bf16[4,16,128]{2,1,0:T(8,128)(2,1)S(1)}, bf16[4,16,128]{2,1,0:T(8,128)(2,1)S(1)}, u32[]{:S(2)}, u32[]{:S(2)}) collective-permute-start(bf16[4,16,128]{2,1,0:T(8,128)(2,1)S(1)} %get-tuple-element.73), channel_id=1, source_target_pairs={{0,6},{1,7},{2,4},{3,5},{4,2},{5,3},{6,0},{7,1},{8,14},{9,15},{10,... | collective-permute-start | bytes 49160 | tf_op jit(solution)/shard_map/ppermute | solution.py:862
  38.4 12.8 %collective-permute-start.8 = (bf16[8,144,128]{2,1,0:T(8,128)(2,1)S(1)}, bf16[8,144,128]{2,1,0:T(8,128)(2,1)S(1)}, u32[]{:S(2)}, u32[]{:S(2)}) collective-permute-start(bf16[8,144,128]{2,1,0:T(8,128)(2,1)S(1)} %get-tuple-element.76), channel_id=1, source_target_pairs={{0,8},{8,0},{16,24},{24,16},{32,40},{40,32},{48,56},{56,48},{64,72... | collective-permute-start | bytes 884744 | tf_op jit(solution)/shard_map/ppermute | solution.py:862
  38.4 12.7 %collective-permute-start.9 = (bf16[8,144,128]{2,1,0:T(8,128)(2,1)S(1)}, bf16[8,144,128]{2,1,0:T(8,128)(2,1)S(1)}, u32[]{:S(2)}, u32[]{:S(2)}) collective-permute-start(bf16[8,144,128]{2,1,0:T(8,128)(2,1)S(1)} %get-tuple-element.77), channel_id=1, source_target_pairs={{0,120},{8,16},{16,8},{24,32},{32,24},{40,48},{48,40},{56,64},{64,... | collective-permute-start | bytes 884744 | tf_op jit(solution)/shard_map/ppermute | solution.py:862
  56.6 7.5 %copy-start.9 = (s32[256]{0:T(256)S(1)}, s32[256]{0:T(256)}, u32[]{:S(2)}) copy-start(s32[256]{0:T(256)} %ids.3) | copy-start | bytes 3076
  56.6 2.2 %collective-permute-start.10 = (bf16[3,64,128]{2,1,0:T(8,128)(2,1)S(1)}, bf16[3,64,128]{2,1,0:T(8,128)(2,1)S(1)}, u32[]{:S(2)}, u32[]{:S(2)}) collective-permute-start(bf16[3,64,128]{2,1,0:T(8,128)(2,1)S(1)} %get-tuple-element.93), channel_id=1, source_target_pairs={{0,1},{1,0},{2,3},{3,2},{4,5},{5,4},{6,7},{7,6},{8,9},{9,8},{10,11... | collective-permute-start | bytes 147464 | tf_op jit(solution)/shard_map/ppermute | solution.py:862
  56.7 4.8 %collective-permute-start.11 = (bf16[3,64,128]{2,1,0:T(8,128)(2,1)S(1)}, bf16[3,64,128]{2,1,0:T(8,128)(2,1)S(1)}, u32[]{:S(2)}, u32[]{:S(2)}) collective-permute-start(bf16[3,64,128]{2,1,0:T(8,128)(2,1)S(1)} %get-tuple-element.94), channel_id=1, source_target_pairs={{0,7},{1,2},{2,1},{3,4},{4,3},{5,6},{6,5},{7,0},{8,15},{9,10},{10,... | collective-permute-start | bytes 147464 | tf_op jit(solution)/shard_map/ppermute | solution.py:862
  61.5 4.7 %collective-permute-start.12 = (bf16[3,64,128]{2,1,0:T(8,128)(2,1)S(1)}, bf16[3,64,128]{2,1,0:T(8,128)(2,1)S(1)}, u32[]{:S(2)}, u32[]{:S(2)}) collective-permute-start(bf16[3,64,128]{2,1,0:T(8,128)(2,1)S(1)} %pad_maximum_fusion), channel_id=1, source_target_pairs={{0,8},{8,0},{16,24},{24,16},{32,40},{40,32},{48,56},{56,48},{64,72... | collective-permute-start | bytes 147464 | tf_op jit(solution)/shard_map/ppermute | solution.py:862
  61.6 7.7 %collective-permute-start.13 = (bf16[3,64,128]{2,1,0:T(8,128)(2,1)S(1)}, bf16[3,64,128]{2,1,0:T(8,128)(2,1)S(1)}, u32[]{:S(2)}, u32[]{:S(2)}) collective-permute-start(bf16[3,64,128]{2,1,0:T(8,128)(2,1)S(1)} %pad_maximum_fusion.1), channel_id=1, source_target_pairs={{0,120},{8,16},{16,8},{24,32},{32,24},{40,48},{48,40},{56,64},{64,... | collective-permute-start | bytes 147464 | tf_op jit(solution)/shard_map/ppermute | solution.py:862
  64.1 5.2 %copy-start.13 = (s32[128]{0:T(128)S(1)}, s32[128]{0:T(128)}, u32[]{:S(2)}) copy-start(s32[128]{0:T(128)} %get-tuple-element.96.slots) | copy-start | bytes 1540

commit v7 on v5

--- a/solution.py
+++ b/solution.py
@@ -421,20 +421,25 @@
     return out
 
 
-def inner_kernel(x, g, t1, t1o, b1, t2, b2, part, pre, xs, hs):
+def inner_kernel(x, g, t1, t1o, b1, t2, b2, part, pre, xs, xe, hs):
     iy = lax.axis_index("gy")
+    lane = lanes_of((1, ROWS, 128))
     for dy in range(3):
         xs[dy, 0, 0] = jnp.zeros((ROWS, 256), BF16)
         xs[dy, PAIRS, 1] = jnp.zeros((ROWS, 256), BF16)
+        xe[dy, 0, 0] = jnp.zeros((ROWS, 128), BF16)
+        xe[dy, PAIRS, 1] = jnp.zeros((ROWS, 128), BF16)
         hs[dy, 0, 0] = jnp.zeros((BY, 256), BF16)
         hs[dy, PAIRS, 1] = jnp.zeros((BY, 256), BF16)
 
     def shift(n, carry):
         for k in range(2):
-            for tx in range(2):
-                v = x[tx, pl.ds(2 * n + k, 1)].astype(F32)
-                for dy, s in enumerate(shifted(v)):
-                    xs[dy, pl.ds(n + k, 1), 1 - k, :, tx * 128 : tx * 128 + 128] = s.astype(BF16)
+            both = [shifted(x[tx, pl.ds(2 * n + k, 1)].astype(F32)) for tx in range(2)]
+            for dy in range(3):
+                s0, s1 = both[0][dy], both[1][dy]
+                xs[dy, pl.ds(n + k, 1), 1 - k, :, 0:128] = s0.astype(BF16)
+                xs[dy, pl.ds(n + k, 1), 1 - k, :, 128:256] = s1.astype(BF16)
+                xe[dy, pl.ds(n + k, 1), 1 - k] = jnp.where(lane < 64, s0, s1).astype(BF16)
         return carry
 
     lax.fori_loop(0, PAIRS, shift, 0)
@@ -448,7 +453,7 @@
                 m = n * 4 + zo
                 hs[dy, m : m + 4, 1 - zo] = s[:, 8 : 8 + BY].astype(BF16)
     for n in range(2):
-        taps = sum([window(xs, n, zi) for zi in range(4)], [])
+        taps = sum([window(xe, n, zi) for zi in range(4)], [])
         acc = jnp.dot(jnp.concatenate(taps, 1), t1o[...], preferred_element_type=F32) + b1[...]
         pre[n] = acc
     for n in range(2):
@@ -471,6 +476,7 @@
         ],
         scratch_shapes=[
             VMEM((3, PAIRS + 1, 2, ROWS, 256), BF16),
+            VMEM((3, PAIRS + 1, 2, ROWS, 128), BF16),
             VMEM((3, PAIRS + 1, 2, BY, 256), BF16),
         ],
         compiler_params=params(32),
@@ -821,7 +827,7 @@
     inner = [none, 1, 2, 3, 4, 5, 6, none]
     every = list(range(8))
     e1a = band(every, inner, False)
-    e1o = band(every, [-1, 0, 7, 8], False)
+    e1o = band([0, 1, 6, 7], [-1, 0, 7, 8], False)
     e1r = band([-2, -1, 8, 9], [-1, 0, 7, 8], False)
     e2a = band(inner, every, True)
     e2b = band([-1, 0, 7, 8], every, True)
@@ -832,7 +838,7 @@
         out_specs=[vm] * 8,
         out_shape=[
             jax.ShapeDtypeStruct((2304, 256), BF16),
-            jax.ShapeDtypeStruct((3072, 256), BF16),
+            jax.ShapeDtypeStruct((1536, 256), BF16),
             jax.ShapeDtypeStruct((1536, 256), BF16),
             jax.ShapeDtypeStruct((2560, 256), BF16),
             jax.ShapeDtypeStruct((1152, 256), BF16),

time: 72.4 us -> 72.2 us (level)
  no operation moved by 1% of the time
where the time goes in v7:
time: 72.2 us; the launch traced here: 72.1 us
  Pallas kernels  38.5 us (53%)
  starting transfers between devices  20.4 us (28%)
  waiting for transfers between devices  11.3 us (16%)
  between operations  1.77 us (2%)
    ppermute x14, starting transfers between devices, swap(): return lax.ppermute(x, axis, route)  20.4 us
    ppermute x14, waiting for transfers between devices, swap(): return lax.ppermute(x, axis, route)  11.3 us
    pallas_call x1, Pallas kernels, inner_convs(): pl.pallas_call(inner_kernel, in_specs=[vm] * 7, out_specs=[vm, vm], out_s...  8.01 us
    pallas_call x1, Pallas kernels, own_splat(): pl.pallas_call(own_splat_kernel, in_specs=[pl.BlockSpec(memory_space=SMEM...  5.38 us
    pallas_call x1, Pallas kernels, edge_convs(): pl.pallas_call(edge_kernel, in_specs=[vm] * 7 + [pl.BlockSpec(memory_spac...  5.38 us
    pallas_call x1, Pallas kernels, far_splat(): pl.pallas_call(far_splat_kernel, in_specs=[anywhere] * 5, out_specs=[vm,...  4.97 us
    pallas_call x1, Pallas kernels, own_read(): pl.pallas_call(own_read_kernel, in_specs=[pl.BlockSpec(memory_space=SMEM)...  4.27 us
    pallas_call x1, Pallas kernels, far_read(): pl.pallas_call(far_read_kernel, in_specs=[smem, smem] + [vm] * 6, out_spe...  2.64 us
  transfers between devices with their start and end apart: 14, of which 5 were waited for; matrix products, arithmetic and copies ran while one was open for 0% of the time, Pallas kernels for 32%

profile of v7, /device:TPU:0, one launch (start us, length us, event | category | flops | bytes accessed | tf_op | source)
XLA Modules:
  0.0 72.1 jit_solution(1723993978406236610)
XLA Ops:
  1.3 5.0 %far_splat.1 = (bf16[1584,128]{1,0:T(8,128)(2,1)}, bf16[1584,128]{1,0:T(8,128)(2,1)}, bf16[1584,128]{1,0:T(8,128)(2,1)}, s32[128]{0:T(128)}) custom-call(s32[256]{0:T(256)} %owners_h.1, s32[256]{0:T(256)} %ids.3, s32[1]{0:T(128)S(6)} %copy.17.counts_h.counts, bf16[32,32768]{1,0:T(8,128)(2,1)} %f_hbm.3, bf16[32768,128]{1,0:T(8,128)(2,1)} %w_hbm.5), custom_call_target="tpu_custom_call" | custom-call | flops 134217728 | bytes 6291456 | tf_op jit(solution)/shard_map/far_splat/pallas_call | solution.py:146
  6.3 1.7 %collective-permute-start = (bf16[1584,128]{1,0:T(8,128)(2,1)}, bf16[1584,128]{1,0:T(8,128)(2,1)S(1)}, u32[]{:S(2)}, u32[]{:S(2)}) collective-permute-start(bf16[1584,128]{1,0:T(8,128)(2,1)} %get-tuple-element.61), channel_id=1, source_target_pairs={{0,8},{8,0},{16,24},{24,16},{32,40},{40,32},{48,56},{56,48},{64,72... | collective-permute-start | bytes 1216520 | tf_op jit(solution)/shard_map/ppermute | solution.py:875
  8.0 0.0 copy-start.7
  8.0 0.0 copy-start.8
  8.1 4.4 %collective-permute-start.1 = (bf16[1584,128]{1,0:T(8,128)(2,1)}, bf16[1584,128]{1,0:T(8,128)(2,1)S(1)}, u32[]{:S(2)}, u32[]{:S(2)}) collective-permute-start(bf16[1584,128]{1,0:T(8,128)(2,1)} %get-tuple-element.62), channel_id=1, source_target_pairs={{0,120},{8,16},{16,8},{24,32},{32,24},{40,48},{48,40},{56,64},{64,... | collective-permute-start | bytes 1216520 | tf_op jit(solution)/shard_map/ppermute | solution.py:875
  12.5 5.4 %own_splat.1.own = bf16[2,16,128,128]{3,2,1,0:T(8,128)(2,1)} custom-call(s32[256]{0:T(256)} %ids.3, bf16[32,32768]{1,0:T(8,128)(2,1)} %f_hbm.3, bf16[32768,128]{1,0:T(8,128)(2,1)} %w_hbm.5), custom_call_target="tpu_custom_call" | custom-call | flops 134217728 | bytes 6291456 | tf_op jit(solution)/shard_map/own_splat/pallas_call | solution.py:192
  18.0 1.6 %prepare.1 = (bf16[2304,256]{1,0:T(8,128)(2,1)S(1)}, bf16[1536,256]{1,0:T(8,128)(2,1)S(1)}, bf16[1536,256]{1,0:T(8,128)(2,1)S(1)}, bf16[2560,256]{1,0:T(8,128)(2...) custom-call(bf16[27,32,32]{2,1,0:T(8,128)(2,1)S(1)} %copy-done.5, ...), custom_call_target="tpu_custom_call" | custom-call | flops 471859200 | bytes 5242880 | tf_op jit(solution)/shard_map/prepare/pallas_call | solution.py:835
  19.6 2.8 %collective-permute-done.1.xb = bf16[1584,128]{1,0:T(8,128)(2,1)S(1)} collective-permute-done((bf16[1584,128]{1,0:T(8,128)(2,1)}, bf16[1584,128]{1,0:T(8,128)(2,1)S(1)}, u32[]{:S(2)}, u32[]{:S(2)}) %collective-permute-start.1) | collective-permute-done | bytes 405536 | tf_op jit(solution)/shard_map/ppermute | solution.py:875
  22.5 0.1 bundle.1
  22.5 0.1 collective-permute-start.2
  22.6 4.2 %collective-permute-start.3 = (bf16[1584,128]{1,0:T(8,128)(2,1)S(1)}, bf16[1584,128]{1,0:T(8,128)(2,1)S(1)}, u32[]{:S(2)}, u32[]{:S(2)}) collective-permute-start(bf16[1584,128]{1,0:T(8,128)(2,1)S(1)} %get-tuple-element.68), channel_id=1, source_target_pairs={{0,7},{1,2},{2,1},{3,4},{4,3},{5,6},{6,5},{7,0},{8,15},{9,10},{10,... | collective-permute-start | bytes 1216520 | tf_op jit(solution)/shard_map/ppermute | solution.py:875
  26.8 2.1 %column.1 = (f32[2,16,128,128]{3,2,1,0:T(8,128)S(1)}, s32[8,128]{1,0:T(8,128)S(1)}, bf16[4,16,128]{2,1,0:T(8,128)(2,1)S(1)}, bf16[4,16,128]{2,1,0:T(8,128)(2,1)S...) custom-call(bf16[2,16,128,128]{3,2,1,0:T(8,128)(2,1)S(1)} %copy-done, ...), custom_call_target="tpu_custom_call" | custom-call | flops 1000 | bytes 4194304 | tf_op jit(solution)/shard_map/column/pallas_call | solution.py:294
  28.9 0.1 collective-permute-start.4
  29.0 0.5 collective-permute-start.5
  29.5 1.6 %collective-permute-start.6 = (bf16[4,16,128]{2,1,0:T(8,128)(2,1)S(1)}, bf16[4,16,128]{2,1,0:T(8,128)(2,1)S(1)}, u32[]{:S(2)}, u32[]{:S(2)}) collective-permute-start(bf16[4,16,128]{2,1,0:T(8,128)(2,1)S(1)} %get-tuple-element.73), channel_id=1, source_target_pairs={{0,2},{1,3},{2,0},{3,1},{4,6},{5,7},{6,4},{7,5},{8,10},{9,11},{10,... | collective-permute-start | bytes 49160 | tf_op jit(solution)/shard_map/ppermute | solution.py:875
  31.1 0.1 collective-permute-start.7
  31.2 2.3 %collective-permute-done.5.next_b = bf16[4,16,128]{2,1,0:T(8,128)(2,1)S(1)} collective-permute-done((bf16[4,16,128]{2,1,0:T(8,128)(2,1)S(1)}, bf16[4,16,128]{2,1,0:T(8,128)(2,1)S(1)}, u32[]{:S(2)}, u32[]{:S(2)}) %collective-permute-start.5) | collective-permute-done | bytes 16416 | tf_op jit(solution)/shard_map/ppermute | solution.py:875
  33.4 2.6 %collective-permute-done.7.far_b = bf16[4,16,128]{2,1,0:T(8,128)(2,1)S(1)} collective-permute-done((bf16[4,16,128]{2,1,0:T(8,128)(2,1)S(1)}, bf16[4,16,128]{2,1,0:T(8,128)(2,1)S(1)}, u32[]{:S(2)}, u32[]{:S(2)}) %collective-permute-start.7) | collective-permute-done | bytes 16416 | tf_op jit(solution)/shard_map/ppermute | solution.py:875
  36.1 2.3 %sum_tiles.1 = (bf16[2,16,128,128]{3,2,1,0:T(8,128)(2,1)S(1)}, bf16[2,16,144,128]{3,2,1,0:T(8,128)(2,1)S(1)}, bf16[8,144,128]{2,1,0:T(8,128)(2,1)S(1)}, bf16[8,144,128]{2,1,0:T(8,128)(2,1)S(1)}, s32[8,128]{1,0:T(8,128)S(1)}) custom-call(f32[2,16,128,128]{3,2,1,0:T(8,128)S(1)} %get-tuple-element.70.part, bf16[1584,128]{1,0:T(8,128)(2,1)S(1)} %collective-permute-done.2.ya, ...), custom_call_target="tpu_custom_call" | custom-call | flops 1000 | bytes 4194304 | tf_op jit(solution)/shard_map/sum_tiles/pallas_call | solution.py:379
  38.3 0.1 collective-permute-start.8
  38.4 4.7 %collective-permute-start.9 = (bf16[8,144,128]{2,1,0:T(8,128)(2,1)S(1)}, bf16[8,144,128]{2,1,0:T(8,128)(2,1)S(1)}, u32[]{:S(2)}, u32[]{:S(2)}) collective-permute-start(bf16[8,144,128]{2,1,0:T(8,128)(2,1)S(1)} %get-tuple-element.78), channel_id=1, source_target_pairs={{0,120},{8,16},{16,8},{24,32},{32,24},{40,48},{48,40},{56,64},{64,... | collective-permute-start | bytes 884744 | tf_op jit(solution)/shard_map/ppermute | solution.py:875
  43.1 8.0 %inner_convs.1 = (f32[8,2,128,256]{3,2,1,0:T(8,128)S(1)}, f32[2,576,256]{2,1,0:T(8,128)S(1)}) custom-call(bf16[2,16,144,128]{3,2,1,0:T(8,128)(2,1)S(1)} %get-tuple-element.79.x, bf16[2,8,2,128,128]{4,3,2,1,0:T(8,128)(2,1)S(1)} %bitcast.5, bf16[2304,256]{1,0:T(8,128)(2,1)S(1)} %get-tuple-element.81.t1, bf16[1536,256]{1,0:T(8,128)(2,1)S(1)} %get-tuple-element.82.t1o, ...), custom_call_target="tpu_custom_call" | custom-call | flops 6039797760 | bytes 6291456 | tf_op jit(solution)/shard_map/inner_convs/pallas_call | solution.py:469
  51.1 5.4 %edge_convs.1 = (bf16[8,2,128,256]{3,2,1,0:T(8,128)(2,1)S(1)}, f32[128,8,128]{2,1,0:T(8,128)S(1)}, bf16[3,64,128]{2,1,0:T(8,128)(2,1)S(1)}, bf16[3,64,128]{2,1,0:T(8,128)(2,1)S(1)}, bf16[2,64,128]{2,1,0:T(8,128)(2,1)S(1)}) custom-call(bf16[8,144,128]{2,1,0:T(8,128)(2,1)S(1)} %collective-permute-done.8.ra, ...), custom_call_target="tpu_custom_call" | custom-call | flops 2717908992 | bytes 6291456 | tf_op jit(solution)/shard_map/edge_convs/pallas_call | solution.py:588
  56.5 0.1 collective-permute-start.10
  56.6 0.3 collective-permute-start.11
  56.9 1.8 %turn.1 = bf16[32,16,8,128]{3,2,1,0:T(8,128)(2,1)} custom-call(bf16[8,2,128,256]{3,2,1,0:T(8,128)(2,1)S(1)} %get-tuple-element.93.total), custom_call_target="tpu_custom_call" | custom-call | flops 1000 | bytes 8388608 | tf_op jit(solution)/shard_map/turn/pallas_call | solution.py:616
  58.7 2.7 %collective-permute-done.11.yb = bf16[3,64,128]{2,1,0:T(8,128)(2,1)S(1)} collective-permute-done((bf16[3,64,128]{2,1,0:T(8,128)(2,1)S(1)}, bf16[3,64,128]{2,1,0:T(8,128)(2,1)S(1)}, u32[]{:S(2)}, u32[]{:S(2)}) %collective-permute-start.11) | collective-permute-done | bytes 49184 | tf_op jit(solution)/shard_map/ppermute | solution.py:875
  61.5 0.1 collective-permute-start.12
  61.6 2.5 %collective-permute-start.13 = (bf16[3,64,128]{2,1,0:T(8,128)(2,1)S(1)}, bf16[3,64,128]{2,1,0:T(8,128)(2,1)S(1)}, u32[]{:S(2)}, u32[]{:S(2)}) collective-permute-start(bf16[3,64,128]{2,1,0:T(8,128)(2,1)S(1)} %pad_maximum_fusion.1), channel_id=1, source_target_pairs={{0,120},{8,16},{16,8},{24,32},{32,24},{40,48},{48,40},{56,64},{64,... | collective-permute-start | bytes 147464 | tf_op jit(solution)/shard_map/ppermute | solution.py:875
  64.1 4.3 %own_read.1 = (f32[3,16384]{1,0:T(4,128)S(1)}, bf16[16384,128]{1,0:T(8,128)(2,1)S(1)}) custom-call(s32[256]{0:T(256)S(1)} %copy-done.9, f32[128,8,128]{2,1,0:T(8,128)S(1)} %get-tuple-element.101.table, bf16[32768,128]{1,0:T(8,128)(2,1)} %w_hbm.5), custom_call_target="tpu_custom_call" | custom-call | flops 134217728 | bytes 9437184 | tf_op jit(solution)/shard_map/own_read/pallas_call | solution.py:684
  68.4 0.9 %collective-permute-done.13.xb = bf16[3,64,128]{2,1,0:T(8,128)(2,1)S(1)} collective-permute-done((bf16[3,64,128]{2,1,0:T(8,128)(2,1)S(1)}, bf16[3,64,128]{2,1,0:T(8,128)(2,1)S(1)}, u32[]{:S(2)}, u32[]{:S(2)}) %collective-permute-start.13) | collective-permute-done | bytes 49184 | tf_op jit(solution)/shard_map/ppermute | solution.py:875
  69.3 2.6 %far_read.1 = f32[3,32768]{1,0:T(4,128)} custom-call(s32[128]{0:T(128)S(1)} %copy-done.13, s32[1]{0:T(128)S(6)} %copy.17.counts_h.counts, bf16[3,64,128]{2,1,0:T(8,128)(2,1)S(1)} %collective-permute-done.12.xa, bf16[3,64,128]{2,1,0:T(8,128)(2,1)S(1)} %collective-permute-done.13.xb, bf16[3,64,128]{2,1,0:T(8,128)(2,1)S(1)} %collective-permute-done.10.ya, ...), custom_call_target="tpu_custom_call" | custom-call | flops 134217728 | bytes 5242880 | tf_op jit(solution)/shard_map/far_read/pallas_call | solution.py:739
  (39 shorter events, 0.1 us)
Async XLA Ops:
  6.3 13.4 %collective-permute-start = (bf16[1584,128]{1,0:T(8,128)(2,1)}, bf16[1584,128]{1,0:T(8,128)(2,1)S(1)}, u32[]{:S(2)}, u32[]{:S(2)}) collective-permute-start(bf16[1584,128]{1,0:T(8,128)(2,1)} %get-tuple-element.61), channel_id=1, source_target_pairs={{0,8},{8,0},{16,24},{24,16},{32,40},{40,32},{48,56},{56,48},{64,72... | collective-permute-start | bytes 1216520 | tf_op jit(solution)/shard_map/ppermute | solution.py:875
  8.0 9.9 %copy-start.2 = (bf16[128,2048]{1,0:T(8,128)(2,1)S(1)}, bf16[128,2048]{1,0:T(8,128)(2,1)}, u32[]{:S(2)}) copy-start(bf16[128,2048]{1,0:T(8,128)(2,1)} %constant.13.clone.e2a) | copy-start | bytes 1572868
  8.0 9.9 %copy-start.3 = (bf16[128,2048]{1,0:T(8,128)(2,1)S(1)}, bf16[128,2048]{1,0:T(8,128)(2,1)}, u32[]{:S(2)}) copy-start(bf16[128,2048]{1,0:T(8,128)(2,1)} %constant.10.clone.e1a) | copy-start | bytes 1572868
  8.0 9.9 %copy-start.4 = (bf16[128,1024]{1,0:T(8,128)(2,1)S(1)}, bf16[128,1024]{1,0:T(8,128)(2,1)}, u32[]{:S(2)}) copy-start(bf16[128,1024]{1,0:T(8,128)(2,1)} %constant.14.clone.e2b) | copy-start | bytes 786436
  8.0 10.0 %copy-start.5 = (bf16[27,32,32]{2,1,0:T(8,128)(2,1)S(1)}, bf16[27,32,32]{2,1,0:T(8,128)(2,1)}, u32[]{:S(2)}) copy-start(bf16[27,32,32]{2,1,0:T(8,128)(2,1)} %c1.1) | copy-start | bytes 165892
  8.0 10.0 %copy-start.6 = (bf16[27,32,32]{2,1,0:T(8,128)(2,1)S(1)}, bf16[27,32,32]{2,1,0:T(8,128)(2,1)}, u32[]{:S(2)}) copy-start(bf16[27,32,32]{2,1,0:T(8,128)(2,1)} %c2.1) | copy-start | bytes 165892
  8.0 10.0 %copy-start.7 = (bf16[128,512]{1,0:T(8,128)(2,1)S(1)}, bf16[128,512]{1,0:T(8,128)(2,1)}, u32[]{:S(2)}) copy-start(bf16[128,512]{1,0:T(8,128)(2,1)} %constant.12.clone.e1r) | copy-start | bytes 393220
  8.0 10.0 %copy-start.8 = (bf16[128,512]{1,0:T(8,128)(2,1)S(1)}, bf16[128,512]{1,0:T(8,128)(2,1)}, u32[]{:S(2)}) copy-start(bf16[128,512]{1,0:T(8,128)(2,1)} %constant.11.clone.e1o) | copy-start | bytes 393220
  8.0 10.0 %copy-start.10 = (bf16[3,32]{1,0:T(4,128)(2,1)S(1)}, bf16[3,32]{1,0:T(4,128)(2,1)}, u32[]{:S(2)}) copy-start(bf16[3,32]{1,0:T(4,128)(2,1)} %head.1) | copy-start | bytes 580
  8.0 10.0 %copy-start.11 = (f32[32]{0:T(128)S(1)}, f32[32]{0:T(128)}, u32[]{:S(2)}) copy-start(f32[32]{0:T(128)} %param.21) | copy-start | bytes 388
  8.0 9.9 %copy-start.12 = (f32[32]{0:T(128)S(1)}, f32[32]{0:T(128)}, u32[]{:S(2)}) copy-start(f32[32]{0:T(128)} %param.23) | copy-start | bytes 388
  8.1 14.4 %collective-permute-start.1 = (bf16[1584,128]{1,0:T(8,128)(2,1)}, bf16[1584,128]{1,0:T(8,128)(2,1)S(1)}, u32[]{:S(2)}, u32[]{:S(2)}) collective-permute-start(bf16[1584,128]{1,0:T(8,128)(2,1)} %get-tuple-element.62), channel_id=1, source_target_pairs={{0,120},{8,16},{16,8},{24,32},{32,24},{40,48},{48,40},{56,64},{64,... | collective-permute-start | bytes 1216520 | tf_op jit(solution)/shard_map/ppermute | solution.py:875
  17.9 4.6 %copy-start.1 = (bf16[1584,128]{1,0:T(8,128)(2,1)S(1)}, bf16[1584,128]{1,0:T(8,128)(2,1)}, u32[]{:S(2)}) copy-start(bf16[1584,128]{1,0:T(8,128)(2,1)} %get-tuple-element.66.mid) | copy-start | bytes 1216516
  17.9 8.9 %copy-start = (bf16[2,16,128,128]{3,2,1,0:T(8,128)(2,1)S(1)}, bf16[2,16,128,128]{3,2,1,0:T(8,128)(2,1)}, u32[]{:S(2)}) copy-start(bf16[2,16,128,128]{3,2,1,0:T(8,128)(2,1)} %own_splat.1.own) | copy-start | bytes 3145732
  22.5 13.5 %collective-permute-start.2 = (bf16[1584,128]{1,0:T(8,128)(2,1)S(1)}, bf16[1584,128]{1,0:T(8,128)(2,1)S(1)}, u32[]{:S(2)}, u32[]{:S(2)}) collective-permute-start(bf16[1584,128]{1,0:T(8,128)(2,1)S(1)} %get-tuple-element.67), channel_id=1, source_target_pairs={{0,1},{1,0},{2,3},{3,2},{4,5},{5,4},{6,7},{7,6},{8,9},{9,8},{10,11... | collective-permute-start | bytes 1216520 | tf_op jit(solution)/shard_map/ppermute | solution.py:875
  22.6 13.5 %collective-permute-start.3 = (bf16[1584,128]{1,0:T(8,128)(2,1)S(1)}, bf16[1584,128]{1,0:T(8,128)(2,1)S(1)}, u32[]{:S(2)}, u32[]{:S(2)}) collective-permute-start(bf16[1584,128]{1,0:T(8,128)(2,1)S(1)} %get-tuple-element.68), channel_id=1, source_target_pairs={{0,7},{1,2},{2,1},{3,4},{4,3},{5,6},{6,5},{7,0},{8,15},{9,10},{10,... | collective-permute-start | bytes 1216520 | tf_op jit(solution)/shard_map/ppermute | solution.py:875
  28.9 2.2 %collective-permute-start.4 = (bf16[4,16,128]{2,1,0:T(8,128)(2,1)S(1)}, bf16[4,16,128]{2,1,0:T(8,128)(2,1)S(1)}, u32[]{:S(2)}, u32[]{:S(2)}) collective-permute-start(bf16[4,16,128]{2,1,0:T(8,128)(2,1)S(1)} %get-tuple-element.71), channel_id=1, source_target_pairs={{0,1},{1,0},{2,3},{3,2},{4,5},{5,4},{6,7},{7,6},{8,9},{9,8},{10,11... | collective-permute-start | bytes 49160 | tf_op jit(solution)/shard_map/ppermute | solution.py:875
  29.0 4.5 %collective-permute-start.5 = (bf16[4,16,128]{2,1,0:T(8,128)(2,1)S(1)}, bf16[4,16,128]{2,1,0:T(8,128)(2,1)S(1)}, u32[]{:S(2)}, u32[]{:S(2)}) collective-permute-start(bf16[4,16,128]{2,1,0:T(8,128)(2,1)S(1)} %get-tuple-element.72), channel_id=1, source_target_pairs={{0,7},{1,2},{2,1},{3,4},{4,3},{5,6},{6,5},{7,0},{8,15},{9,10},{10,... | collective-permute-start | bytes 49160 | tf_op jit(solution)/shard_map/ppermute | solution.py:875
  29.5 4.0 %collective-permute-start.6 = (bf16[4,16,128]{2,1,0:T(8,128)(2,1)S(1)}, bf16[4,16,128]{2,1,0:T(8,128)(2,1)S(1)}, u32[]{:S(2)}, u32[]{:S(2)}) collective-permute-start(bf16[4,16,128]{2,1,0:T(8,128)(2,1)S(1)} %get-tuple-element.73), channel_id=1, source_target_pairs={{0,2},{1,3},{2,0},{3,1},{4,6},{5,7},{6,4},{7,5},{8,10},{9,11},{10,... | collective-permute-start | bytes 49160 | tf_op jit(solution)/shard_map/ppermute | solution.py:875
  31.1 5.0 %collective-permute-start.7 = (bf16[4,16,128]{2,1,0:T(8,128)(2,1)S(1)}, bf16[4,16,128]{2,1,0:T(8,128)(2,1)S(1)}, u32[]{:S(2)}, u32[]{:S(2)}) collective-permute-start(bf16[4,16,128]{2,1,0:T(8,128)(2,1)S(1)} %get-tuple-element.74), channel_id=1, source_target_pairs={{0,6},{1,7},{2,4},{3,5},{4,2},{5,3},{6,0},{7,1},{8,14},{9,15},{10,... | collective-permute-start | bytes 49160 | tf_op jit(solution)/shard_map/ppermute | solution.py:875
  38.3 12.8 %collective-permute-start.8 = (bf16[8,144,128]{2,1,0:T(8,128)(2,1)S(1)}, bf16[8,144,128]{2,1,0:T(8,128)(2,1)S(1)}, u32[]{:S(2)}, u32[]{:S(2)}) collective-permute-start(bf16[8,144,128]{2,1,0:T(8,128)(2,1)S(1)} %get-tuple-element.77), channel_id=1, source_target_pairs={{0,8},{8,0},{16,24},{24,16},{32,40},{40,32},{48,56},{56,48},{64,72... | collective-permute-start | bytes 884744 | tf_op jit(solution)/shard_map/ppermute | solution.py:875
  38.4 12.7 %collective-permute-start.9 = (bf16[8,144,128]{2,1,0:T(8,128)(2,1)S(1)}, bf16[8,144,128]{2,1,0:T(8,128)(2,1)S(1)}, u32[]{:S(2)}, u32[]{:S(2)}) collective-permute-start(bf16[8,144,128]{2,1,0:T(8,128)(2,1)S(1)} %get-tuple-element.78), channel_id=1, source_target_pairs={{0,120},{8,16},{16,8},{24,32},{32,24},{40,48},{48,40},{56,64},{64,... | collective-permute-start | bytes 884744 | tf_op jit(solution)/shard_map/ppermute | solution.py:875
  56.5 7.6 %copy-start.9 = (s32[256]{0:T(256)S(1)}, s32[256]{0:T(256)}, u32[]{:S(2)}) copy-start(s32[256]{0:T(256)} %ids.3) | copy-start | bytes 3076
  56.5 2.2 %collective-permute-start.10 = (bf16[3,64,128]{2,1,0:T(8,128)(2,1)S(1)}, bf16[3,64,128]{2,1,0:T(8,128)(2,1)S(1)}, u32[]{:S(2)}, u32[]{:S(2)}) collective-permute-start(bf16[3,64,128]{2,1,0:T(8,128)(2,1)S(1)} %get-tuple-element.94), channel_id=1, source_target_pairs={{0,1},{1,0},{2,3},{3,2},{4,5},{5,4},{6,7},{7,6},{8,9},{9,8},{10,11... | collective-permute-start | bytes 147464 | tf_op jit(solution)/shard_map/ppermute | solution.py:875
  56.6 4.8 %collective-permute-start.11 = (bf16[3,64,128]{2,1,0:T(8,128)(2,1)S(1)}, bf16[3,64,128]{2,1,0:T(8,128)(2,1)S(1)}, u32[]{:S(2)}, u32[]{:S(2)}) collective-permute-start(bf16[3,64,128]{2,1,0:T(8,128)(2,1)S(1)} %get-tuple-element.95), channel_id=1, source_target_pairs={{0,7},{1,2},{2,1},{3,4},{4,3},{5,6},{6,5},{7,0},{8,15},{9,10},{10,... | collective-permute-start | bytes 147464 | tf_op jit(solution)/shard_map/ppermute | solution.py:875
  61.5 6.9 %collective-permute-start.12 = (bf16[3,64,128]{2,1,0:T(8,128)(2,1)S(1)}, bf16[3,64,128]{2,1,0:T(8,128)(2,1)S(1)}, u32[]{:S(2)}, u32[]{:S(2)}) collective-permute-start(bf16[3,64,128]{2,1,0:T(8,128)(2,1)S(1)} %pad_maximum_fusion), channel_id=1, source_target_pairs={{0,8},{8,0},{16,24},{24,16},{32,40},{40,32},{48,56},{56,48},{64,72... | collective-permute-start | bytes 147464 | tf_op jit(solution)/shard_map/ppermute | solution.py:875
  61.6 7.7 %collective-permute-start.13 = (bf16[3,64,128]{2,1,0:T(8,128)(2,1)S(1)}, bf16[3,64,128]{2,1,0:T(8,128)(2,1)S(1)}, u32[]{:S(2)}, u32[]{:S(2)}) collective-permute-start(bf16[3,64,128]{2,1,0:T(8,128)(2,1)S(1)} %pad_maximum_fusion.1), channel_id=1, source_target_pairs={{0,120},{8,16},{16,8},{24,32},{32,24},{40,48},{48,40},{56,64},{64,... | collective-permute-start | bytes 147464 | tf_op jit(solution)/shard_map/ppermute | solution.py:875
  64.1 5.2 %copy-start.13 = (s32[128]{0:T(128)S(1)}, s32[128]{0:T(128)}, u32[]{:S(2)}) copy-start(s32[128]{0:T(128)} %get-tuple-element.97.slots) | copy-start | bytes 1540
